TPU v7x, 512 devices: a whole 4x8x8 slice. The times are simulated.
512 devices in a mesh: group: 16 (over x, z_lo, core), loop: 32 (over y, z_hi).
Axes of the slice: x: 4, y: 8, z: 8 (z_hi: 4, z_lo: 2; z = z_hi * 2 + z_lo), core: 2. Of those that a mesh axis runs over, the one named last changes fastest.
Arguments:
- tile_vals: bfloat16 [16, 32, 32, 128, 128], P('group', 'loop'), may hold values from 0 to 1
- tile_rows: int32 [16, 32, 32], P('group', 'loop'), may hold values from 0 to 15, as said below
- tile_cols: int32 [16, 32, 32], P('group', 'loop'), may hold values from 0 to 15, as said below
- tile_count: int32 [16, 32], P('group', 'loop'), may hold values from 8 to 32, as said below
- start_panel: float32 [32, 2048, 64], P('loop', 'group'), may hold values from -6 to 6
Outputs:
- session_panel: float32 [32, 2048, 64], P('loop', 'group')
- attendee_panel: float32 [16, 2048, 64], P('group', 'loop')
Inputs may be any that keep to these rules, and one draw needn't show every extreme that they name: `tile_count`: 32 is reached in every draw, at a block drawn from the seed. Within one block, the 32 slots name distinct pairs of tile_rows and tile_cols. Within one block, the 32 slots name distinct pairs of tile_rows and tile_cols.
All inputs are finite; a program needn't handle non-finite values.
Results may differ from a plain program's by a relative error of at most 0.0054.
Values may be sent and summed in bfloat16 or wider, within the bound.
No kernel may reach another device: no remote copies, remote signals or barrier semaphores. Data moves between devices by JAX's collectives and lax.ppermute only.
A program may use at most 64 MiB of HBM per device.

v0:
```python
import jax
import jax.numpy as jnp
from jax import lax
from jax.sharding import PartitionSpec as P

ROWS_DEV = 2048
COLS_DEV = 2048
ITERS = 3


def orthonormal(stacked, gram_sum):
    factor = jnp.linalg.cholesky(gram_sum)
    return jax.scipy.linalg.solve_triangular(factor, stacked.T, lower=True).T


def per_device(tile_vals, tile_rows, tile_cols, tile_count, start_panel):
    highest = lax.Precision.HIGHEST
    values = tile_vals[0, 0]
    row_pick = tile_rows[0, 0]
    col_pick = tile_cols[0, 0]
    tile_total = tile_count[0, 0]
    slot_count = values.shape[0]
    tile_side = values.shape[1]
    panel_width = start_panel.shape[2]
    n_loop = lax.axis_size("loop")
    rows_dev = ROWS_DEV
    cols_dev = COLS_DEV
    row_blocks = rows_dev // tile_side
    col_blocks = cols_dev // tile_side
    alive_mask = (jnp.arange(slot_count) < tile_total).astype(jnp.float32)
    row_onehot = (row_pick[None, :] == jnp.arange(row_blocks)[:, None]).astype(jnp.float32)
    col_onehot = (col_pick[None, :] == jnp.arange(col_blocks)[:, None]).astype(jnp.float32)
    live_tiles = values.astype(jnp.float32) * alive_mask[:, None, None]
    row_local = jnp.dot(row_onehot, jnp.sum(live_tiles, axis=2), precision=highest).reshape(
        rows_dev
    )
    col_local = jnp.dot(col_onehot, jnp.sum(live_tiles, axis=1), precision=highest).reshape(
        cols_dev
    )
    col_scale = lax.rsqrt(
        lax.psum_scatter(col_local, "group", scatter_dimension=0, tiled=True) + 1.0
    )

    def tile_term(blocks, picked, target_onehot, forward):
        chosen = jnp.take(blocks, picked, axis=0)
        if forward:
            product = jnp.einsum("tij,tjk->tik", values, chosen, preferred_element_type=jnp.float32)
        else:
            product = jnp.einsum("tij,tik->tjk", values, chosen, preferred_element_type=jnp.float32)
        product = product * alive_mask[:, None, None]
        return jnp.einsum("rt,tik->rik", target_onehot, product, precision=highest)

    def apply_backward(whole_rows):
        blocks = whole_rows.reshape(row_blocks, tile_side, panel_width)
        return tile_term(blocks, row_pick, col_onehot, False).reshape(cols_dev, panel_width)

    panel = start_panel[0]
    attendee = jnp.zeros((rows_dev // n_loop, panel_width), jnp.float32)
    row_scale = lax.rsqrt(
        lax.psum_scatter(row_local, "loop", scatter_dimension=0, tiled=True) + 1.0
    )
    for iteration in range(ITERS):
        scaled = (panel * col_scale[:, None]).astype(jnp.bfloat16)
        gathered = lax.all_gather(scaled, "group", axis=0, tiled=True)
        apply_blocks = gathered.reshape(col_blocks, tile_side, panel_width)
        partial_rows = tile_term(apply_blocks, col_pick, row_onehot, True).reshape(
            rows_dev, panel_width
        )
        summed = (
            lax.psum_scatter(partial_rows, "loop", scatter_dimension=0, tiled=True)
            * row_scale[:, None]
        )
        gram_sum = lax.psum(jnp.dot(summed.T, summed, precision=highest), ("group", "loop"))
        attendee = orthonormal(summed, gram_sum)
        whole_rows = lax.all_gather(
            (attendee * row_scale[:, None]).astype(jnp.bfloat16), "loop", axis=0, tiled=True
        )
        partial_cols = apply_backward(whole_rows)
        summed_cols = (
            lax.psum_scatter(partial_cols, "group", scatter_dimension=0, tiled=True)
            * col_scale[:, None]
        )
        gram_cols = lax.psum(
            jnp.dot(summed_cols.T, summed_cols, precision=highest), ("group", "loop")
        )
        panel = orthonormal(summed_cols, gram_cols)
    return (panel[None], attendee[None])


def solution(mesh):
    in_specs = (
        P("group", "loop", None, None, None),
        P("group", "loop", None),
        P("group", "loop", None),
        P("group", "loop"),
        P("loop", "group", None),
    )
    out_specs = (P("loop", "group", None), P("group", "loop", None))
    return jax.shard_map(
        per_device, mesh=mesh, in_specs=in_specs, out_specs=out_specs, check_vma=False
    )
```

profile of v0, /device:TPU:1, one launch (start us, length us, event | category | flops | bytes accessed | tf_op | source)
XLA Modules:
  0.0 1882.3 jit_solution(13323279002396904671)
XLA Ops:
  11.3 33.8 %all-reduce = f32[2048]{0:T(1024)S(1)} all-reduce(f32[2048]{0:T(1024)S(1)} %convolution_bitcast_fusion.2), channel_id=2, replica_groups=mesh['group'=16,'loop'=32] {'group'}, use_global_device_ids=true, to_apply=%region_1.0.clone | all-reduce | flops 2048 | bytes 16384
  47.2 17.8 all_gather.18
  71.7 73.5 %all-reduce.1 = f32[2048]{0:T(1024)S(1)} all-reduce(f32[2048]{0:T(1024)S(1)} %convolution_bitcast_fusion.1), channel_id=4, replica_groups=mesh['group'=16,'loop'=32] {'loop'}, use_global_device_ids=true, to_apply=%region_4.0.clone | all-reduce | flops 2048 | bytes 16384
  145.3 145.7 %reduce-scatter.19.cloned.1.call-done = f32[64,64]{1,0:T(8,128)} async-done(((f32[2048,64]{1,0:T(8,128)}), f32[64,64]{1,0:T(8,128)}) %reduce-scatter.19.cloned.1.call-update) | async-done | bytes 16400
  292.0 100.1 %psum.42 = f32[64,64]{0,1:T(8,128)S(1)} all-reduce(f32[64,64]{0,1:T(8,128)S(1)} %fusion.105), channel_id=1, replica_groups=mesh['group'=16,'loop'=32] {'group','loop'}, use_global_device_ids=true, to_apply=%region_5.7 | all-reduce | flops 4096 | bytes 32768 | tf_op jit(solution)/shard_map/psum | solution.py:73
  392.2 5.8 cholesky.104
  399.4 4.9 custom-call.12
  404.6 67.6 %all_gather.19 = bf16[2048,64]{1,0:T(8,128)(2,1)S(1)} all-gather(bf16[64,64]{1,0:T(8,128)(2,1)S(1)} %copy.92), channel_id=1, replica_groups=mesh['group'=16,'loop'=32] {'loop'}, dimensions={0}, use_global_device_ids=true | all-gather | bytes 270336 | tf_op jit(solution)/shard_map/all_gather | solution.py:75
  475.7 70.1 %reduce-scatter.13.cloned.1.call-done = f32[128,64]{0,1:T(8,128)} async-done(((f32[2048,64]{0,1:T(8,128)}), f32[128,64]{0,1:T(8,128)}) %reduce-scatter.13.cloned.1.call-update) | async-done | bytes 32784 | tf_op jit(solution)/shard_map/reduce_scatter | solution.py:80
  546.8 100.2 %psum.43 = f32[64,64]{0,1:T(8,128)S(1)} all-reduce(f32[64,64]{0,1:T(8,128)S(1)} %fusion.102), channel_id=1, replica_groups=mesh['group'=16,'loop'=32] {'group','loop'}, use_global_device_ids=true, to_apply=%region_9.13 | all-reduce | flops 4096 | bytes 32768 | tf_op jit(solution)/shard_map/psum | solution.py:83
  647.1 5.8 cholesky.115
  654.3 4.9 custom-call.13
  660.2 18.2 all_gather.20
  682.5 216.3 %reduce-scatter.21.cloned.1.call-done = f32[64,64]{1,0:T(8,128)} async-done(((f32[2048,64]{1,0:T(8,128)}), f32[64,64]{1,0:T(8,128)}) %reduce-scatter.21.cloned.1.call-update) | async-done | bytes 16400
  899.8 99.8 %psum.44 = f32[64,64]{0,1:T(8,128)S(1)} all-reduce(f32[64,64]{0,1:T(8,128)S(1)} %fusion.99), channel_id=1, replica_groups=mesh['group'=16,'loop'=32] {'group','loop'}, use_global_device_ids=true, to_apply=%region_11.16 | all-reduce | flops 4096 | bytes 32768 | tf_op jit(solution)/shard_map/psum | solution.py:73
  999.7 5.8 cholesky.126
  1006.9 4.9 custom-call.14
  1012.1 66.5 %all_gather.21 = bf16[2048,64]{1,0:T(8,128)(2,1)S(1)} all-gather(bf16[64,64]{1,0:T(8,128)(2,1)S(1)} %copy.102), channel_id=1, replica_groups=mesh['group'=16,'loop'=32] {'loop'}, dimensions={0}, use_global_device_ids=true | all-gather | bytes 270336 | tf_op jit(solution)/shard_map/all_gather | solution.py:75
  1082.1 70.7 %reduce-scatter.15.cloned.1.call-done = f32[128,64]{0,1:T(8,128)} async-done(((f32[2048,64]{0,1:T(8,128)}), f32[128,64]{0,1:T(8,128)}) %reduce-scatter.15.cloned.1.call-update) | async-done | bytes 32784 | tf_op jit(solution)/shard_map/reduce_scatter | solution.py:80
  1153.8 100.1 %psum.45 = f32[64,64]{0,1:T(8,128)S(1)} all-reduce(f32[64,64]{0,1:T(8,128)S(1)} %fusion.96), channel_id=1, replica_groups=mesh['group'=16,'loop'=32] {'group','loop'}, use_global_device_ids=true, to_apply=%region_13.18 | all-reduce | flops 4096 | bytes 32768 | tf_op jit(solution)/shard_map/psum | solution.py:83
  1254.0 5.8 cholesky.137
  1261.2 4.9 custom-call.15
  1267.1 18.3 all_gather.22
  1289.5 216.4 %reduce-scatter.23.cloned.1.call-done = f32[64,64]{1,0:T(8,128)} async-done(((f32[2048,64]{1,0:T(8,128)}), f32[64,64]{1,0:T(8,128)}) %reduce-scatter.23.cloned.1.call-update) | async-done | bytes 16400
  1507.0 99.8 %psum.46 = f32[64,64]{0,1:T(8,128)S(1)} all-reduce(f32[64,64]{0,1:T(8,128)S(1)} %fusion.93), channel_id=1, replica_groups=mesh['group'=16,'loop'=32] {'group','loop'}, use_global_device_ids=true, to_apply=%region_15.20 | all-reduce | flops 4096 | bytes 32768 | tf_op jit(solution)/shard_map/psum | solution.py:73
  1606.8 5.8 cholesky.148
  1614.0 4.9 custom-call.16
  1619.3 66.5 %all_gather.23 = bf16[2048,64]{1,0:T(8,128)(2,1)S(1)} all-gather(bf16[64,64]{1,0:T(8,128)(2,1)S(1)} %copy.112), channel_id=1, replica_groups=mesh['group'=16,'loop'=32] {'loop'}, dimensions={0}, use_global_device_ids=true | all-gather | bytes 270336 | tf_op jit(solution)/shard_map/all_gather | solution.py:75
  1689.9 70.7 %reduce-scatter.17.cloned.1.call-done = f32[128,64]{0,1:T(8,128)} async-done(((f32[2048,64]{0,1:T(8,128)}), f32[128,64]{0,1:T(8,128)}) %reduce-scatter.17.cloned.1.call-update) | async-done | bytes 32784 | tf_op jit(solution)/shard_map/reduce_scatter | solution.py:80
  1761.6 100.1 %psum.47 = f32[64,64]{0,1:T(8,128)S(1)} all-reduce(f32[64,64]{0,1:T(8,128)S(1)} %fusion.90), channel_id=1, replica_groups=mesh['group'=16,'loop'=32] {'group','loop'}, use_global_device_ids=true, to_apply=%region_17.22 | all-reduce | flops 4096 | bytes 32768 | tf_op jit(solution)/shard_map/psum | solution.py:83
  1861.8 5.8 cholesky.159
  1869.0 4.9 custom-call.17
  (114 shorter events, 49.1 us)
Async XLA Ops:
  7.2 4.0 copy-start.3
  7.2 40.0 %copy-start.1 = (f32[1,128,64]{1,2,0:T(8,128)S(1)}, f32[1,128,64]{1,2,0:T(8,128)}, u32[]{:S(2)}) copy-start(f32[1,128,64]{1,2,0:T(8,128)} %param.16) | copy-start | bytes 98308
  7.2 283.8 %reduce-scatter.19.cloned.1.call-start = ((), (), s32[]{:S(2)}) async-start(), calls=%async_computation.9 | async-start | bytes 1081344
  65.0 1.2 copy-start
  66.2 0.9 copy-start.2
  69.6 476.2 %reduce-scatter.13.cloned.1.call-start = ((), (), s32[]{:S(2)}) async-start(), calls=%async_computation.6 | async-start | bytes 557056 | tf_op jit(solution)/shard_map/reduce_scatter | solution.py:80
  475.6 423.2 %reduce-scatter.21.cloned.1.call-start = ((), (), s32[]{:S(2)}) async-start(), calls=%async_computation.10 | async-start | bytes 1081344
  682.4 470.4 %reduce-scatter.15.cloned.1.call-start = ((), (), s32[]{:S(2)}) async-start(), calls=%async_computation.7 | async-start | bytes 557056 | tf_op jit(solution)/shard_map/reduce_scatter | solution.py:80
  1082.1 423.9 %reduce-scatter.23.cloned.1.call-start = ((), (), s32[]{:S(2)}) async-start(), calls=%async_computation.11 | async-start | bytes 1081344
  1289.5 471.1 %reduce-scatter.17.cloned.1.call-start = ((), (), s32[]{:S(2)}) async-start(), calls=%async_computation.8 | async-start | bytes 557056 | tf_op jit(solution)/shard_map/reduce_scatter | solution.py:80
Sparse Core Ops, SparseCore 0:
  69.7 221.2 reduce-scatter.18
  475.8 70.0 reduce-scatter.12
  682.5 216.2 reduce-scatter.20
  1082.2 70.5 reduce-scatter.14
  1289.6 216.3 reduce-scatter.22
  1689.3 71.2 reduce-scatter.16
where the time goes:
time: 1880 us
  blocking collectives  962 us (51%)
  waiting for transfers between devices  790 us (42%)
  other arithmetic  75.9 us (4%)
    unnamed x9, waiting for transfers between devices  579 us
    psum x3, blocking collectives, per_device(): lax.psum(jnp.dot(summed_cols.T, summed_cols, precision=highest), ('group'...  300 us
    psum x3, blocking collectives, per_device(): lax.psum(jnp.dot(summed.T, summed, precision=highest), ('group', 'loop'))  300 us
    reduce_scatter x3, waiting for transfers between devices, per_device(): lax.psum_scatter(partial_cols, 'group', scatter_dimension=0, tiled=True)  211 us
    all_gather x3, blocking collectives, per_device(): lax.all_gather((attendee * row_scale[:, None]).astype(jnp.bfloat16), 'loo...  201 us
    unnamed x2, blocking collectives  107 us
    all_gather x3, blocking collectives, per_device(): gathered = lax.all_gather(scaled, 'group', axis=0, tiled=True)  54.3 us
    another operation x18, other arithmetic, orthonormal(): factor = jnp.linalg.cholesky(gram_sum)  39.1 us
  transfers between devices with their start and end apart: 6, of which 6 were waited for; matrix products, arithmetic and copies ran while one was open for 0% of the time, Pallas kernels for 0%

commit v1 on v0

v1 whole, which is shorter than its diff:
```python
import functools

import jax
import jax.numpy as jnp
from jax import lax
from jax.experimental import pallas as pl
from jax.experimental.pallas import tpu as pltpu
from jax.sharding import PartitionSpec as P

ITERS = 3
SIDE = 128
WIDTH = 64
LANES = 128
GRAM_ROWS = 48
DEGREE_ROWS = 16
F32 = jnp.float32
BF16 = jnp.bfloat16
HIGHEST = lax.Precision.HIGHEST


def iota(shape, dim):
    return lax.broadcasted_iota(jnp.int32, shape, dim)


def halves_to_rows(packed):
    return jnp.concatenate([packed[:, :WIDTH], packed[:, WIDTH:]], axis=0)


def rows_to_halves(rows):
    half = rows.shape[0] // 2
    return jnp.concatenate([rows[:half], rows[half:]], axis=1)


def lanes_to_packed(row, half):
    shape = (half, LANES)
    spread = jnp.broadcast_to(row, shape)
    delta = iota(shape, 1) - iota(shape, 0)
    first = jnp.sum(jnp.where(delta == 0, spread, 0.0), axis=1, keepdims=True)
    last = jnp.sum(jnp.where(delta == half, spread, 0.0), axis=1, keepdims=True)
    return jnp.where(iota(shape, 1) < WIDTH, first, last)


def split_two(value):
    high = value.astype(BF16).astype(F32)
    return high, value - high


def diagonal_blocks(square):
    return square[:WIDTH, :WIDTH] + square[WIDTH:, WIDTH:]


def inverse_factor(gram):
    eye = (iota((WIDTH, WIDTH), 0) == iota((WIDTH, WIDTH), 1)).astype(F32)
    whole = jnp.concatenate([gram, eye], axis=1)
    blocks = [whole[8 * b : 8 * b + 8] for b in range(WIDTH // 8)]
    below = iota((8, 1), 0)
    for k in range(WIDTH):
        at, inner = k // 8, k % 8
        row = blocks[at][inner : inner + 1]
        row = row * (1.0 / row[:, k : k + 1])
        for b in range(at, WIDTH // 8):
            if b == at and inner == 7:
                continue
            column = blocks[b][:, k : k + 1]
            if b == at:
                column = jnp.where(below > inner, column, 0.0)
            blocks[b] = blocks[b] - column * row
    whole = jnp.concatenate(blocks, axis=0)
    pivots = jnp.sum(whole[:, :WIDTH] * eye, axis=1, keepdims=True)
    return whole[:, WIDTH:] * lax.rsqrt(pivots)


def apply_factor(packed, inverse):
    zero = jnp.zeros((WIDTH, WIDTH), F32)
    both = jnp.concatenate(
        [
            jnp.concatenate([inverse, zero], axis=1),
            jnp.concatenate([zero, inverse], axis=1),
        ],
        axis=0,
    )
    return lax.dot_general(
        packed, both, (((1,), (1,)), ((), ())), precision=HIGHEST, preferred_element_type=F32
    )


def gram_to_message(gram):
    shape = (WIDTH, WIDTH)
    high, low = split_two(gram)
    mixed = jnp.where(iota(shape, 0) >= iota(shape, 1), high, low.T)
    diagonal = jnp.sum(jnp.where(iota(shape, 0) == iota(shape, 1), low, 0.0), axis=0, keepdims=True)
    diagonal = jnp.concatenate([diagonal, diagonal], axis=1)
    return rows_to_halves(mixed), jnp.broadcast_to(diagonal, (16, LANES))


def message_to_gram(mixed, diagonal):
    shape = (WIDTH, WIDTH)
    square = halves_to_rows(mixed)
    on_diagonal = iota(shape, 0) == iota(shape, 1)
    return jnp.where(on_diagonal, square + diagonal[:1, :WIDTH], square + square.T)


def degree_kernel(row_at, col_at, values, col_degree, row_degree, col_sum, row_sum):
    col_sum[...] = jnp.zeros_like(col_sum)
    row_sum[...] = jnp.zeros_like(row_sum)
    ones = jnp.ones((8, SIDE), BF16)
    for t in range(values.shape[0]):
        tile = values[t]
        col_sum[col_at[t]] += jnp.dot(ones, tile, preferred_element_type=F32)
        row_sum[row_at[t]] += lax.dot_general(
            ones, tile, (((1,), (1,)), ((), ())), preferred_element_type=F32
        )
    for b in range(col_degree.shape[0]):
        col_degree[b : b + 1] = col_sum[b, :1]
        row_degree[b : b + 1] = row_sum[b, :1]


def product_kernel(kind, n_from, rows_from, n_to, rows_to, *refs):
    if kind == "start":
        source, target, gathered, tiles, extra, out, weight, spread, total = refs
    elif kind == "degree":
        source, target, gathered, tiles, out, weight, spread, total = refs
    else:
        source, target, gathered, tiles, weight, out, spread, total = refs
    lane_low = iota((SIDE // 2, LANES), 1) < WIDTH
    n_blocks = total.shape[0] - 1
    per_block = SIDE // 2 // rows_from

    if kind == "start":
        degree = 1.0 + jnp.sum(gathered[:, rows_from:, :], axis=0)

    grams = jnp.zeros((2 * LANES, LANES), F32)
    for b in range(n_blocks):
        rows = slice(b * SIDE // 2, (b + 1) * SIDE // 2)
        if kind == "start":
            packed_degree = lanes_to_packed(degree[b : b + 1], SIDE // 2)
            weight[rows] = packed_degree
            panel = (gathered[b, :rows_from] * lax.rsqrt(packed_degree)).astype(BF16).astype(F32)
        else:
            parts = [
                gathered[b * per_block + j, :rows_from].astype(F32) for j in range(per_block)
            ]
            panel = parts[0] if per_block == 1 else jnp.concatenate(parts, axis=0)
        if kind == "degree":
            packs = []
            for j in range(per_block):
                pieces = gathered[b * per_block + j, rows_from:].astype(F32)
                packs.append(lanes_to_packed(jnp.sum(pieces[:3], axis=0, keepdims=True), rows_from))
            packed_degree = packs[0] if per_block == 1 else jnp.concatenate(packs, axis=0)
            weight[rows] = packed_degree
        turned = pltpu.roll(panel, WIDTH, 1)
        half = SIDE // 2
        spread[b, :half] = jnp.where(lane_low, panel, 0.0).astype(BF16)
        spread[b, half : 2 * half] = jnp.where(lane_low, turned, 0.0).astype(BF16)
        spread[b, 2 * half : 3 * half] = jnp.where(lane_low, 0.0, turned).astype(BF16)
        spread[b, 3 * half :] = jnp.where(lane_low, 0.0, panel).astype(BF16)
        if kind != "start":
            high, low = split_two(panel * weight[rows])
            both = jnp.concatenate([high, low], axis=1).astype(BF16)
            grams = grams + lax.dot_general(
                both, panel.astype(BF16), (((0,), (0,)), ((), ())), preferred_element_type=F32
            )
        total[b] = jnp.zeros((half, LANES), F32)
    total[n_blocks] = jnp.zeros((half, LANES), F32)

    for t in range(tiles.shape[0]):
        total[target[t]] += jnp.dot(tiles[t], spread[source[t]], preferred_element_type=F32)

    if kind == "start":
        message = extra[...]
    else:
        gram = diagonal_blocks(grams[:LANES]) + diagonal_blocks(grams[LANES:])
        mixed, diagonal = gram_to_message(gram)
        mixed, diagonal = mixed.astype(BF16), diagonal.astype(BF16)
    to_block = SIDE // 2 // rows_to
    for d in range(n_to):
        first = d % to_block * rows_to
        out[d, :rows_to] = total[d // to_block, first : first + rows_to].astype(BF16)
        if kind == "start":
            out[d, rows_to:] = message[d]
        else:
            out[d, rows_to : rows_to + 32] = mixed
            out[d, rows_to + 32 :] = diagonal


def sum_kernel(kind, n_from, rows, n_copies, *refs):
    if kind == "degree":
        received, copies, summed_out, scale_out = refs
    elif kind == "plain":
        received, scale_ref, copies, summed_out = refs
    else:
        received, scale_ref, other, copies, summed_out, other_out = refs
    summed = received[0].astype(F32)
    for s in range(1, n_from):
        summed = summed + received[s].astype(F32)
    panel = summed[:rows]
    if kind == "degree":
        pieces = summed[rows:]
        degree = 1.0 + jnp.sum(pieces[:3], axis=0, keepdims=True)
        scale = lax.rsqrt(lanes_to_packed(degree, rows))
        scale_out[...] = scale
        panel = panel * scale
    else:
        scale = scale_ref[...]
        gram = message_to_gram(summed[rows : rows + 32], summed[rows + 32 :])
        inverse = inverse_factor(gram)
        panel = apply_factor(panel * scale, inverse)
    summed_out[...] = panel
    if kind == "last":
        other_out[...] = halves_to_rows(apply_factor(other[...], inverse))
        square = lax.dot_general(
            panel, panel, (((0,), (0,)), ((), ())), precision=HIGHEST, preferred_element_type=F32
        )
        message = rows_to_halves(diagonal_blocks(square))
    else:
        message = (panel * scale).astype(BF16)
    for d in range(n_copies):
        copies[d, : message.shape[0]] = message
    if kind == "degree":
        high, rest = split_two(degree)
        middle, low = split_two(rest)
        at = iota((DEGREE_ROWS, LANES), 0)
        tail = jnp.where(at == 0, high, jnp.where(at == 1, middle, jnp.where(at == 2, low, 0.0)))
        tail = tail.astype(BF16)
        for d in range(n_copies):
            copies[d, rows:] = tail


def last_kernel(n_from, received, panel, out):
    summed = received[0]
    for s in range(1, n_from):
        summed = summed + received[s]
    inverse = inverse_factor(halves_to_rows(summed))
    out[...] = halves_to_rows(apply_factor(panel[...], inverse))


VMEM = pl.BlockSpec(memory_space=pltpu.VMEM)
SMEM = pl.BlockSpec(memory_space=pltpu.SMEM)


def call(kernel, name, in_specs, out_shapes, scratch=()):
    return pl.pallas_call(
        kernel,
        name=name,
        in_specs=in_specs,
        out_specs=[VMEM] * len(out_shapes),
        out_shape=[jax.ShapeDtypeStruct(s, d) for s, d in out_shapes],
        scratch_shapes=list(scratch),
        compiler_params=pltpu.CompilerParams(vmem_limit_bytes=32 * 1024 * 1024),
    )


def exchange(array, axis):
    n, rows, lanes = array.shape
    return lax.all_to_all(
        array.reshape(n * rows, lanes), axis, split_axis=0, concat_axis=0, tiled=True
    ).reshape(n, rows, lanes)


def per_device(tile_vals, tile_rows, tile_cols, tile_count, start_panel):
    values = tile_vals[0, 0]
    slots = values.shape[0]
    n_group, n_loop = lax.axis_size("group"), lax.axis_size("loop")
    rows_dev, cols_dev = 2048, 2048
    row_blocks, col_blocks = rows_dev // SIDE, cols_dev // SIDE
    row_half, col_half = rows_dev // n_loop // 2, cols_dev // n_group // 2
    half = SIDE // 2

    alive = jnp.arange(slots) < tile_count[0, 0]
    row_from, col_from = tile_rows[0, 0], tile_cols[0, 0]
    row_to = jnp.where(alive, row_from, row_blocks)
    col_to = jnp.where(alive, col_from, col_blocks)

    col_part, row_part = call(
        degree_kernel,
        "degrees",
        [SMEM, SMEM, VMEM],
        [((col_blocks, SIDE), F32), ((row_blocks, SIDE), F32)],
        [pltpu.VMEM((col_blocks + 1, 8, SIDE), F32), pltpu.VMEM((row_blocks + 1, 8, SIDE), F32)],
    )(row_to, col_to, values)

    start = start_panel[0]
    start = jnp.concatenate([start[:col_half], start[col_half:]], axis=1)
    first = jnp.concatenate([start, col_part], axis=0)
    gathered = exchange(jnp.broadcast_to(first[None], (n_group,) + first.shape), "group")

    forward = values.reshape(slots, half // row_half, 2, row_half, SIDE)
    forward = forward.transpose(0, 1, 3, 2, 4).reshape(slots, half, 2 * SIDE)
    turned = values.transpose(0, 2, 1).reshape(slots, SIDE, half // row_half, 2, row_half)
    turned = turned.transpose(0, 1, 3, 2, 4).reshape(slots, half // col_half, 2, col_half, SIDE)
    backward = turned.transpose(0, 1, 3, 2, 4).reshape(slots, half, 2 * SIDE)

    pieces = row_part.reshape(n_loop, 2 * row_half)
    high = pieces.astype(BF16)
    middle = (pieces - high.astype(F32)).astype(BF16)
    low = (pieces - high.astype(F32) - middle.astype(F32)).astype(BF16)
    degrees = jnp.stack([high, middle, low], axis=1)
    degrees = jnp.pad(degrees, ((0, 0), (0, DEGREE_ROWS - 3), (0, LANES - 2 * row_half)))

    spread = lambda blocks: [
        pltpu.VMEM((blocks, 2 * SIDE, LANES), BF16),
    ]
    total = lambda blocks: [pltpu.VMEM((blocks + 1, half, LANES), F32)]

    col_scale = row_scale = col_weight = row_weight = None
    for iteration in range(ITERS):
        if iteration == 0:
            outgoing, col_weight = call(
                functools.partial(product_kernel, "start", n_group, col_half, n_loop, row_half),
                "forward_start",
                [SMEM, SMEM, VMEM, VMEM, VMEM],
                [((n_loop, row_half + DEGREE_ROWS, LANES), BF16), ((cols_dev // 2, LANES), F32)],
                spread(col_blocks) + total(row_blocks),
            )(col_from, row_to, gathered, forward, degrees)
            own = lax.axis_index("group") * col_half
            col_scale = lax.rsqrt(lax.dynamic_slice_in_dim(col_weight, own, col_half, 0))
        else:
            (outgoing,) = call(
                functools.partial(product_kernel, "plain", n_group, col_half, n_loop, row_half),
                "forward",
                [SMEM, SMEM, VMEM, VMEM, VMEM],
                [((n_loop, row_half + GRAM_ROWS, LANES), BF16)],
                spread(col_blocks) + total(row_blocks),
            )(col_from, row_to, gathered, forward, col_weight)
        received = exchange(outgoing, "loop")
        if iteration == 0:
            copies, attendee_sum, row_scale = call(
                functools.partial(sum_kernel, "degree", n_loop, row_half, n_loop),
                "attendee_start",
                [VMEM],
                [
                    ((n_loop, row_half + DEGREE_ROWS, LANES), BF16),
                    ((row_half, LANES), F32),
                    ((row_half, LANES), F32),
                ],
            )(received)
        else:
            copies, attendee_sum = call(
                functools.partial(sum_kernel, "plain", n_loop, row_half, n_loop),
                "attendee",
                [VMEM, VMEM],
                [((n_loop, row_half, LANES), BF16), ((row_half, LANES), F32)],
            )(received, row_scale)
        gathered = exchange(copies, "loop")
        if iteration == 0:
            outgoing, row_weight = call(
                functools.partial(product_kernel, "degree", n_loop, row_half, n_group, col_half),
                "backward_start",
                [SMEM, SMEM, VMEM, VMEM],
                [((n_group, col_half + GRAM_ROWS, LANES), BF16), ((rows_dev // 2, LANES), F32)],
                spread(row_blocks) + total(col_blocks),
            )(row_from, col_to, gathered, backward)
        else:
            (outgoing,) = call(
                functools.partial(product_kernel, "plain", n_loop, row_half, n_group, col_half),
                "backward",
                [SMEM, SMEM, VMEM, VMEM, VMEM],
                [((n_group, col_half + GRAM_ROWS, LANES), BF16)],
                spread(row_blocks) + total(col_blocks),
            )(row_from, col_to, gathered, backward, row_weight)
        received = exchange(outgoing, "group")
        if iteration < ITERS - 1:
            copies, session_sum = call(
                functools.partial(sum_kernel, "plain", n_group, col_half, n_group),
                "session",
                [VMEM, VMEM],
                [((n_group, col_half, LANES), BF16), ((col_half, LANES), F32)],
            )(received, col_scale)
            gathered = exchange(copies, "group")
        else:
            copies, session_sum, attendee = call(
                functools.partial(sum_kernel, "last", n_group, col_half, n_group),
                "session_last",
                [VMEM, VMEM, VMEM],
                [
                    ((n_group, WIDTH // 2, LANES), F32),
                    ((col_half, LANES), F32),
                    ((2 * row_half, WIDTH), F32),
                ],
            )(received, col_scale, attendee_sum)
    gram = jnp.sum(exchange(copies, "group"), axis=0)
    grams = exchange(jnp.broadcast_to(gram[None], (n_loop,) + gram.shape), "loop")
    (session,) = call(
        functools.partial(last_kernel, n_loop),
        "session_out",
        [VMEM, VMEM],
        [((2 * col_half, WIDTH), F32)],
    )(grams, session_sum)
    return (session[None], attendee[None])


def solution(mesh):
    in_specs = (
        P("group", "loop", None, None, None),
        P("group", "loop", None),
        P("group", "loop", None),
        P("group", "loop"),
        P("loop", "group", None),
    )
    out_specs = (P("loop", "group", None), P("group", "loop", None))
    return jax.shard_map(
        per_device, mesh=mesh, in_specs=in_specs, out_specs=out_specs, check_vma=False
    )
```

time: 1880 us -> 324 us (0.17)
  waiting for transfers between devices: 790 us -> 16.5 us
  blocking collectives: 962 us -> 201 us
  other arithmetic: 75.9 us -> 0.92 us
  Pallas kernels: 0 us -> 50.9 us
  starting transfers between devices: 0.25 us -> 24 us
    psum x6 -> x0, blocking collectives: 600 us -> none  [the longest x3 300 us: per_device(): lax.psum(jnp.dot(summed_cols.T, summed_cols, precision=highest), ('group'...]
    unnamed x9 -> x0, waiting for transfers between devices: 579 us -> none
    all_gather x6 -> x0, blocking collectives: 255 us -> none  [the longest x3 201 us: per_device(): lax.all_gather((attendee * row_scale[:, None]).astype(jnp.bfloat16), 'loo...]
    reduce_scatter x3 -> x0, waiting for transfers between devices: 211 us -> none  [per_device(): lax.psum_scatter(partial_cols, 'group', scatter_dimension=0, tiled=True)]
    all_to_all x0 -> x11, blocking collectives: none -> 201 us  [exchange(): lax.all_to_all(array.reshape(n * rows, lanes), axis, split_axis=0, concat...]
    unnamed x2 -> x0, blocking collectives: 107 us -> none
    another operation x30 -> x1, other arithmetic: 72.4 us -> 0.1 us  [per_device(): degrees = jnp.stack([high, middle, low], axis=1)]
    pallas_call x0 -> x14, Pallas kernels: none -> 50.9 us  [the longest x2 13.7 us: per_device(): call(functools.partial(sum_kernel, 'plain', n_group, col_half, n_group),...]
  transfers between devices with their start and end apart: 6 -> 3, of which waited for: 6 -> 2; matrix products, arithmetic and copies ran while one was open for 0% -> 6% of each run, Pallas kernels for 0% -> 0%
where the time goes in v1:
time: 324 us; the launch traced here: 320 us
  blocking collectives  201 us (62%)
  Pallas kernels  50.9 us (16%)
  local copies, waits for them, and re-layouts  24.5 us (8%)
  starting transfers between devices  24 us (7%)
  waiting for transfers between devices  16.5 us (5%)
    all_to_all x11, blocking collectives, exchange(): lax.all_to_all(array.reshape(n * rows, lanes), axis, split_axis=0, concat...  201 us
    all_to_all x3, starting transfers between devices, exchange(): lax.all_to_all(array.reshape(n * rows, lanes), axis, split_axis=0, concat...  24 us
    all_to_all x3, waiting for transfers between devices, exchange(): lax.all_to_all(array.reshape(n * rows, lanes), axis, split_axis=0, concat...  16.5 us
    pallas_call x2, Pallas kernels, per_device(): call(functools.partial(sum_kernel, 'plain', n_group, col_half, n_group),...  13.7 us
    pallas_call x2, Pallas kernels, per_device(): call(functools.partial(sum_kernel, 'plain', n_loop, row_half, n_loop), 'a...  12.1 us
    pallas_call x1, Pallas kernels, per_device(): call(functools.partial(sum_kernel, 'last', n_group, col_half, n_group), '...  6.77 us
  transfers between devices with their start and end apart: 3, of which 2 were waited for; matrix products, arithmetic and copies ran while one was open for 6% of the time, Pallas kernels for 0%

profile of v1, /device:TPU:1, one launch (start us, length us, event | category | flops | bytes accessed | tf_op | source)
XLA Modules:
  0.0 319.6 jit_solution(4483410110061367381)
XLA Ops:
  6.8 10.3 %all-to-all-start = ((f32[16,80,128]{2,1,0:T(8,128)}), f32[16,80,128]{2,1,0:T(8,128)S(1)}, u32[]{:S(2)}, u32[]{:S(2)}) async-start(f32[16,80,128]{2,1,0:T(8,128)} %broadcast_in_dim.24), calls=%async_computation | async-start | bytes 1310720 | tf_op jit(solution)/shard_map/all_to_all | solution.py:255
  17.2 2.1 copy.20
  19.3 1.7 reshape.152.refs_3_
  21.2 7.2 %all-to-all-done.refs_2_ = f32[16,80,128]{2,1,0:T(8,128)S(1)} async-done(((f32[16,80,128]{2,1,0:T(8,128)}), f32[16,80,128]{2,1,0:T(8,128)S(1)}, u32[]{:S(2)}, u32[]{:S(2)}) %all-to-all-start) | async-done | bytes 655392 | tf_op jit(solution)/shard_map/all_to_all | solution.py:255
  28.4 1.6 forward_start.1
  30.0 26.3 %all_to_all.84.refs_0_ = bf16[32,48,128]{2,1,0:T(8,128)(2,1)S(1)} all-to-all(bf16[32,48,128]{2,1,0:T(8,128)(2,1)S(1)} %get-tuple-element.20), channel_id=1, replica_groups=mesh['group'=16,'loop'=32] {'loop'}, dimensions={0} | all-to-all | bytes 786432 | tf_op jit(solution)/shard_map/all_to_all | solution.py:255
  57.3 6.6 %all-to-all-start.2 = ((bf16[32,48,128]{2,1,0:T(8,128)(2,1)}), bf16[32,48,128]{2,1,0:T(8,128)(2,1)S(1)}, u32[]{:S(2)}, u32[]{:S(2)}) async-start(bf16[32,48,128]{2,1,0:T(8,128)(2,1)} %get-tuple-element.21), calls=%async_computation.2 | async-start | bytes 786432 | tf_op jit(solution)/shard_map/all_to_all | solution.py:255
  65.0 5.0 %reshape.155 = bf16[32,1,2,64,128]{3,2,4,0,1:T(2,128)(2,1)} reshape(bf16[32,128,2,2,32]{1,4,3,2,0:T(8,128)(2,1)} %bitcast.42) | data formatting | bytes 2097152 | tf_op jit(solution)/shard_map/reshape | solution.py:290
  69.9 6.2 %copy.15 = bf16[32,1,64,2,128]{4,3,2,0,1:T(2,128)(2,1)} copy(bf16[32,1,64,2,128]{2,3,4,0,1:T(2,128)(2,1)} %bitcast.41) | data formatting | bytes 2097152 | tf_op jit(solution)/shard_map/transpose | solution.py:291
  76.1 1.7 reshape.156.refs_3_
  79.6 2.3 backward_start.1
  82.7 7.1 %all-to-all-start.3 = ((bf16[16,112,128]{2,1,0:T(8,128)(2,1)}), bf16[16,112,128]{2,1,0:T(8,128)(2,1)}, u32[]{:S(2)}, u32[]{:S(2)}) async-start(bf16[16,112,128]{2,1,0:T(8,128)(2,1)} %copy-done.4), calls=%async_computation.3 | async-start | bytes 917504 | tf_op jit(solution)/shard_map/all_to_all | solution.py:255
  89.8 9.3 %all-to-all-done.3.refs_0_ = bf16[16,112,128]{2,1,0:T(8,128)(2,1)} async-done(((bf16[16,112,128]{2,1,0:T(8,128)(2,1)}), bf16[16,112,128]{2,1,0:T(8,128)(2,1)}, u32[]{:S(2)}, u32[]{:S(2)}) %all-to-all-start.3) | async-done | bytes 458784 | tf_op jit(solution)/shard_map/all_to_all | solution.py:255
  99.1 7.4 %session.2 = (bf16[16,64,128]{2,1,0:T(8,128)(2,1)S(1)}, f32[64,128]{1,0:T(8,128)}) custom-call(bf16[16,112,128]{2,1,0:T(8,128)(2,1)} %all-to-all-done.3.refs_0_, f32[64,128]{1,0:T(8,128)S(1)} %dynamic-slice_rsqrt_fusion.refs_1_), custom_call_target="tpu_custom_call" | custom-call | tf_op jit(solution)/shard_map/session/pallas_call | solution.py:363
  106.4 10.8 %all_to_all.85.refs_2_ = bf16[16,64,128]{2,1,0:T(8,128)(2,1)S(1)} all-to-all(bf16[16,64,128]{2,1,0:T(8,128)(2,1)S(1)} %get-tuple-element.24), channel_id=1, replica_groups=mesh['group'=16,'loop'=32] {'group'}, dimensions={0} | all-to-all | bytes 524288 | tf_op jit(solution)/shard_map/all_to_all | solution.py:255
  117.2 1.6 forward.2
  118.8 29.8 %all_to_all.86.refs_0_ = bf16[32,80,128]{2,1,0:T(8,128)(2,1)S(1)} all-to-all(bf16[32,80,128]{2,1,0:T(8,128)(2,1)S(1)} %forward.2), channel_id=1, replica_groups=mesh['group'=16,'loop'=32] {'loop'}, dimensions={0} | all-to-all | bytes 1310720 | tf_op jit(solution)/shard_map/all_to_all | solution.py:255
  148.7 6.4 %attendee.2 = (bf16[32,32,128]{2,1,0:T(8,128)(2,1)S(1)}, f32[32,128]{1,0:T(8,128)}) custom-call(bf16[32,80,128]{2,1,0:T(8,128)(2,1)S(1)} %all_to_all.86.refs_0_, f32[32,128]{1,0:T(8,128)S(1)} %get-tuple-element.25.refs_1_), custom_call_target="tpu_custom_call" | custom-call | tf_op jit(solution)/shard_map/attendee/pallas_call | solution.py:338
  155.0 18.5 %all_to_all.87.refs_2_ = bf16[32,32,128]{2,1,0:T(8,128)(2,1)S(1)} all-to-all(bf16[32,32,128]{2,1,0:T(8,128)(2,1)S(1)} %get-tuple-element.26), channel_id=1, replica_groups=mesh['group'=16,'loop'=32] {'loop'}, dimensions={0} | all-to-all | bytes 524288 | tf_op jit(solution)/shard_map/all_to_all | solution.py:255
  173.5 1.6 backward.2
  175.1 15.2 %all_to_all.88.refs_0_ = bf16[16,112,128]{2,1,0:T(8,128)(2,1)S(1)} all-to-all(bf16[16,112,128]{2,1,0:T(8,128)(2,1)S(1)} %backward.2), channel_id=1, replica_groups=mesh['group'=16,'loop'=32] {'group'}, dimensions={0} | all-to-all | bytes 917504 | tf_op jit(solution)/shard_map/all_to_all | solution.py:255
  190.3 6.4 %session.3 = (bf16[16,64,128]{2,1,0:T(8,128)(2,1)S(1)}, f32[64,128]{1,0:T(8,128)}) custom-call(bf16[16,112,128]{2,1,0:T(8,128)(2,1)S(1)} %all_to_all.88.refs_0_, f32[64,128]{1,0:T(8,128)S(1)} %dynamic-slice_rsqrt_fusion.refs_1_), custom_call_target="tpu_custom_call" | custom-call | tf_op jit(solution)/shard_map/session/pallas_call | solution.py:363
  196.6 10.8 %all_to_all.89.refs_2_ = bf16[16,64,128]{2,1,0:T(8,128)(2,1)S(1)} all-to-all(bf16[16,64,128]{2,1,0:T(8,128)(2,1)S(1)} %get-tuple-element.28), channel_id=1, replica_groups=mesh['group'=16,'loop'=32] {'group'}, dimensions={0} | all-to-all | bytes 524288 | tf_op jit(solution)/shard_map/all_to_all | solution.py:255
  209.0 24.3 %all_to_all.90.refs_0_ = bf16[32,80,128]{2,1,0:T(8,128)(2,1)S(1)} all-to-all(bf16[32,80,128]{2,1,0:T(8,128)(2,1)S(1)} %forward.3), channel_id=1, replica_groups=mesh['group'=16,'loop'=32] {'loop'}, dimensions={0} | all-to-all | bytes 1310720 | tf_op jit(solution)/shard_map/all_to_all | solution.py:255
  233.3 5.8 %attendee.3 = (bf16[32,32,128]{2,1,0:T(8,128)(2,1)S(1)}, f32[32,128]{1,0:T(8,128)S(1)}) custom-call(bf16[32,80,128]{2,1,0:T(8,128)(2,1)S(1)} %all_to_all.90.refs_0_, f32[32,128]{1,0:T(8,128)S(1)} %get-tuple-element.25.refs_1_), custom_call_target="tpu_custom_call" | custom-call | tf_op jit(solution)/shard_map/attendee/pallas_call | solution.py:338
  239.1 18.5 %all_to_all.91.refs_2_ = bf16[32,32,128]{2,1,0:T(8,128)(2,1)S(1)} all-to-all(bf16[32,32,128]{2,1,0:T(8,128)(2,1)S(1)} %get-tuple-element.29), channel_id=1, replica_groups=mesh['group'=16,'loop'=32] {'loop'}, dimensions={0} | all-to-all | bytes 524288 | tf_op jit(solution)/shard_map/all_to_all | solution.py:255
  257.6 1.6 backward.3
  259.2 15.3 %all_to_all.92.refs_0_ = bf16[16,112,128]{2,1,0:T(8,128)(2,1)S(1)} all-to-all(bf16[16,112,128]{2,1,0:T(8,128)(2,1)S(1)} %backward.3), channel_id=1, replica_groups=mesh['group'=16,'loop'=32] {'group'}, dimensions={0} | all-to-all | bytes 917504 | tf_op jit(solution)/shard_map/all_to_all | solution.py:255
  274.4 6.8 %session_last.1 = (f32[16,32,128]{2,1,0:T(8,128)S(1)}, f32[64,128]{1,0:T(8,128)S(1)}, f32[64,64]{1,0:T(8,128)}) custom-call(bf16[16,112,128]{2,1,0:T(8,128)(2,1)S(1)} %all_to_all.92.refs_0_, f32[64,128]{1,0:T(8,128)S(1)} %dynamic-slice_rsqrt_fusion.refs_1_, f32[32,128]{1,0:T(8,128)S(1)} %get-tuple-element.30.refs_2_), custom_call_target="tpu_custom_call" | custom-call | tf_op jit(solution)/shard_map/session_last/pallas_call | solution.py:371
  281.2 10.8 %all_to_all.93 = f32[16,32,128]{2,1,0:T(8,128)S(1)} all-to-all(f32[16,32,128]{2,1,0:T(8,128)S(1)} %get-tuple-element.31), channel_id=1, replica_groups=mesh['group'=16,'loop'=32] {'group'}, dimensions={0} | all-to-all | bytes 524288 | tf_op jit(solution)/shard_map/all_to_all | solution.py:255
  292.1 21.1 %all_to_all.94.received = f32[32,32,128]{2,1,0:T(8,128)S(1)} all-to-all(f32[32,32,128]{2,1,0:T(8,128)S(1)} %broadcast_in_dim.25), channel_id=1, replica_groups=mesh['group'=16,'loop'=32] {'loop'}, dimensions={0} | all-to-all | bytes 1048576 | tf_op jit(solution)/shard_map/all_to_all | solution.py:255
  313.2 5.7 %session_out.1 = f32[128,64]{1,0:T(8,128)S(1)} custom-call(f32[32,32,128]{2,1,0:T(8,128)S(1)} %all_to_all.94.received, f32[64,128]{1,0:T(8,128)S(1)} %get-tuple-element.32.panel), custom_call_target="tpu_custom_call" | custom-call | tf_op jit(solution)/shard_map/session_out/pallas_call | solution.py:383
  (32 shorter events, 12.7 us)
Async XLA Ops:
  2.0 1.2 copy-start
  3.2 14.0 %copy-start.1 = (bf16[1,1,32,128,128]{4,3,2,1,0:T(8,128)(2,1)S(1)}, bf16[1,1,32,128,128]{4,3,2,1,0:T(8,128)(2,1)}, u32[]{:S(2)}) copy-start(bf16[1,1,32,128,128]{4,3,2,1,0:T(8,128)(2,1)} %param.5) | copy-start | bytes 3145732
  6.8 21.6 %all-to-all-start = ((f32[16,80,128]{2,1,0:T(8,128)}), f32[16,80,128]{2,1,0:T(8,128)S(1)}, u32[]{:S(2)}, u32[]{:S(2)}) async-start(f32[16,80,128]{2,1,0:T(8,128)} %broadcast_in_dim.24), calls=%async_computation | async-start | bytes 1310720 | tf_op jit(solution)/shard_map/all_to_all | solution.py:255
  17.2 11.2 %copy-start.5 = (s32[1,1,32]{2,1,0:T(1,128)S(1)}, s32[1,1,32]{2,1,0:T(1,128)}, u32[]{:S(2)}) copy-start(s32[1,1,32]{2,1,0:T(1,128)} %param.7) | copy-start | bytes 388
  57.3 20.6 %all-to-all-start.2 = ((bf16[32,48,128]{2,1,0:T(8,128)(2,1)}), bf16[32,48,128]{2,1,0:T(8,128)(2,1)S(1)}, u32[]{:S(2)}, u32[]{:S(2)}) async-start(bf16[32,48,128]{2,1,0:T(8,128)(2,1)} %get-tuple-element.21), calls=%async_computation.2 | async-start | bytes 786432 | tf_op jit(solution)/shard_map/all_to_all | solution.py:255
  69.9 8.7 %copy-start.6 = (s32[1,1,32]{2,1,0:T(1,128)S(1)}, s32[1,1,32]{2,1,0:T(1,128)}, u32[]{:S(2)}) copy-start(s32[1,1,32]{2,1,0:T(1,128)} %param.6) | copy-start | bytes 388
  77.9 0.8 copy-start.2
  78.6 1.0 copy-start.3
  81.9 0.8 copy-start.4
  82.7 16.4 %all-to-all-start.3 = ((bf16[16,112,128]{2,1,0:T(8,128)(2,1)}), bf16[16,112,128]{2,1,0:T(8,128)(2,1)}, u32[]{:S(2)}, u32[]{:S(2)}) async-start(bf16[16,112,128]{2,1,0:T(8,128)(2,1)} %copy-done.4), calls=%async_computation.3 | async-start | bytes 917504 | tf_op jit(solution)/shard_map/all_to_all | solution.py:255

commit v2 on v1

v2 whole, which is shorter than its diff:
```python
import functools

import jax
import jax.numpy as jnp
from jax import lax
from jax.experimental import pallas as pl
from jax.experimental.pallas import tpu as pltpu
from jax.sharding import PartitionSpec as P

ITERS = 3
SIDE = 128
WIDTH = 64
LANES = 128
GRAM_ROWS = 48
DEGREE_ROWS = 16
F32 = jnp.float32
BF16 = jnp.bfloat16
HIGHEST = lax.Precision.HIGHEST


def iota(shape, dim):
    return lax.broadcasted_iota(jnp.int32, shape, dim)


def halves_to_rows(packed):
    return jnp.concatenate([packed[:, :WIDTH], packed[:, WIDTH:]], axis=0)


def rows_to_halves(rows):
    half = rows.shape[0] // 2
    return jnp.concatenate([rows[:half], rows[half:]], axis=1)


def lanes_to_packed(row, half):
    shape = (half, LANES)
    spread = jnp.broadcast_to(row, shape)
    delta = iota(shape, 1) - iota(shape, 0)
    first = jnp.sum(jnp.where(delta == 0, spread, 0.0), axis=1, keepdims=True)
    last = jnp.sum(jnp.where(delta == half, spread, 0.0), axis=1, keepdims=True)
    return jnp.where(iota(shape, 1) < WIDTH, first, last)


def split_two(value):
    high = value.astype(BF16).astype(F32)
    return high, value - high


def diagonal_blocks(square):
    return square[:WIDTH, :WIDTH] + square[WIDTH:, WIDTH:]


def inverse_factor(gram):
    shape = (WIDTH, WIDTH)
    on_diagonal = iota(shape, 0) == iota(shape, 1)
    diagonal = jnp.where(on_diagonal, gram, 0.0)
    down = lax.rsqrt(jnp.sum(diagonal, axis=1, keepdims=True))
    across = lax.rsqrt(jnp.sum(diagonal, axis=0, keepdims=True))
    whole = jnp.concatenate([gram * down * across, jnp.where(on_diagonal, 1.0, 0.0)], axis=1)
    n_blocks = WIDTH // 8
    blocks = [whole[8 * b : 8 * b + 8] for b in range(n_blocks)]
    below = iota((8, LANES), 0)
    for p in range(n_blocks):
        spread = {
            b: [
                jnp.broadcast_to(blocks[b][:, 8 * p + j : 8 * p + j + 1], (8, LANES))
                for j in range(8)
            ]
            for b in range(p, n_blocks)
        }
        for k in range(0, 8, 2):
            own = list(spread[p])
            p00, p01, p11 = own[k][k : k + 1], own[k + 1][k : k + 1], own[k + 1][k + 1 : k + 2]
            inverse = 1.0 / (p00 * p11 - p01 * p01)
            q00, q01, q11 = p11 * inverse, p01 * inverse, p00 * inverse
            row0, row1 = blocks[p][k : k + 1], blocks[p][k + 1 : k + 2]
            for b in range(p, n_blocks):
                if b == p and k == 6:
                    continue
                column0, column1 = spread[b][k], spread[b][k + 1]
                if b == p:
                    column0 = jnp.where(below > k + 1, column0, 0.0)
                    column1 = jnp.where(below > k + 1, column1, 0.0)
                times0 = q00 * column0 - q01 * column1
                times1 = q11 * column1 - q01 * column0
                for j in range(k + 2, 8):
                    spread[b][j] = spread[b][j] - (
                        times0 * own[j][k : k + 1] + times1 * own[j][k + 1 : k + 2]
                    )
                blocks[b] = blocks[b] - (times0 * row0 + times1 * row1)
    whole = jnp.concatenate(blocks, axis=0)
    left, right = whole[:, :WIDTH], whole[:, WIDTH:]
    pivots = jnp.sum(jnp.where(on_diagonal, left, 0.0), axis=1, keepdims=True)
    beside = iota(shape, 0) == iota(shape, 1) + 1
    coupling = jnp.sum(jnp.where(beside, left, 0.0), axis=1, keepdims=True)
    above = jnp.concatenate([pivots[WIDTH - 1 :], pivots[: WIDTH - 1]], axis=0)
    right_above = jnp.concatenate([right[WIDTH - 1 :], right[: WIDTH - 1]], axis=0)
    odd = iota((WIDTH, 1), 0) % 2 == 1
    ratio = jnp.where(odd, coupling / above, 0.0)
    return (right - ratio * right_above) * lax.rsqrt(pivots - ratio * coupling) * across


def both_halves(inverse):
    zero = jnp.zeros((WIDTH, WIDTH), F32)
    return jnp.concatenate(
        [
            jnp.concatenate([inverse, zero], axis=1),
            jnp.concatenate([zero, inverse], axis=1),
        ],
        axis=0,
    )


def times_transposed(left, right):
    return lax.dot_general(
        left, right, (((1,), (1,)), ((), ())), precision=HIGHEST, preferred_element_type=F32
    )


def factor_parts(both):
    high, low = split_two(both.T)
    return jnp.concatenate([high, high, low], axis=0).astype(BF16)


def apply_to_gram(gram, inverse):
    turned = jnp.dot(inverse, gram, precision=HIGHEST, preferred_element_type=F32)
    return times_transposed(turned, inverse)


def gram_to_message(gram, whole):
    shape = (WIDTH, WIDTH)
    on_diagonal = iota(shape, 0) == iota(shape, 1)
    high, low = split_two(gram)
    mixed = jnp.where(iota(shape, 0) >= iota(shape, 1), high, low.T)
    if not whole:
        mixed = jnp.where(on_diagonal, gram * (1.0 + 2.0**-7), mixed)
    message = rows_to_halves(mixed)
    if whole:
        diagonal = jnp.sum(jnp.where(on_diagonal, low, 0.0), axis=0, keepdims=True)
        diagonal = jnp.concatenate([diagonal, diagonal], axis=1)
        message = jnp.concatenate([message, jnp.broadcast_to(diagonal, (16, LANES))], axis=0)
    return message.astype(BF16)


def message_to_gram(message):
    shape = (WIDTH, WIDTH)
    square = halves_to_rows(message[:32])
    on_diagonal = iota(shape, 0) == iota(shape, 1)
    whole = square if message.shape[0] == 32 else square + message[32:33, :WIDTH]
    return jnp.where(on_diagonal, whole, square + square.T)


def degree_kernel(count, row_at, col_at, values, start, copies, row_degree, col_sum, row_sum):
    n_blocks = row_degree.shape[0]
    col_sum[...] = jnp.zeros_like(col_sum)
    row_sum[...] = jnp.zeros_like(row_sum)
    ones = jnp.ones((8, SIDE), BF16)
    for t in range(values.shape[0]):
        tile = values[t]
        alive = t < count[0]
        col_sum[jnp.where(alive, col_at[t], n_blocks)] += jnp.dot(
            ones, tile, preferred_element_type=F32
        )
        row_sum[jnp.where(alive, row_at[t], n_blocks)] += lax.dot_general(
            ones, tile, (((1,), (1,)), ((), ())), preferred_element_type=F32
        )
    for b in range(n_blocks):
        row_degree[b : b + 1] = row_sum[b, :1]
    panel = rows_to_halves(start[...].T)
    degree = jnp.concatenate([col_sum[b, :1] for b in range(n_blocks)], axis=0)
    for d in range(copies.shape[0]):
        copies[d, : panel.shape[0]] = panel
        copies[d, panel.shape[0] :] = degree


def layout_kernel(row_half, col_half, values, forward, backward):
    half = SIDE // 2
    slabs = [slice(at, at + row_half) for at in range(0, SIDE, row_half)]
    for t in range(values.shape[0]):
        tile = values[t]
        for at in range(0, half, row_half):
            forward[t, at : at + row_half, :SIDE] = tile[2 * at : 2 * at + row_half]
            forward[t, at : at + row_half, SIDE:] = tile[2 * at + row_half : 2 * at + 2 * row_half]
        order = slabs[0::2] + slabs[1::2]
        turned = jnp.concatenate([tile[rows] for rows in order], axis=0).T
        for at in range(0, half, col_half):
            backward[t, at : at + col_half, :SIDE] = turned[2 * at : 2 * at + col_half]
            backward[t, at : at + col_half, SIDE:] = turned[2 * at + col_half : 2 * at + 2 * col_half]


def product_kernel(kind, rows_from, n_to, rows_to, whole, *refs):
    count, source, target, gathered, tiles = refs[:5]
    if kind == "start":
        row_degree, out, weight, own_scale, spread, total = refs[5:]
    elif kind == "degree":
        out, weight, spread, total = refs[5:]
    elif whole:
        weight, factor, pending, out, spread, total = refs[5:]
    else:
        weight, factor, out, spread, total = refs[5:]
    half = SIDE // 2
    lane_low = iota((half, LANES), 1) < WIDTH
    n_blocks = total.shape[0] - 1
    per_block = half // rows_from

    if kind == "start":
        degree = 1.0 + jnp.sum(gathered[:, rows_from:, :], axis=0)

    grams = jnp.zeros((2 * LANES, LANES), F32)
    for b in range(n_blocks):
        rows = slice(b * half, (b + 1) * half)
        if kind == "start":
            packed_degree = lanes_to_packed(degree[b : b + 1], half)
            weight[rows] = packed_degree
            panel = (gathered[b, :rows_from] * lax.rsqrt(packed_degree)).astype(BF16).astype(F32)
        else:
            parts = [
                gathered[b * per_block + j, :rows_from].astype(F32) for j in range(per_block)
            ]
            panel = parts[0] if per_block == 1 else jnp.concatenate(parts, axis=0)
        if kind == "degree":
            packs = []
            for j in range(per_block):
                pieces = gathered[b * per_block + j, rows_from:].astype(F32)
                packs.append(lanes_to_packed(jnp.sum(pieces[:3], axis=0, keepdims=True), rows_from))
            packed_degree = packs[0] if per_block == 1 else jnp.concatenate(packs, axis=0)
            weight[rows] = packed_degree
        turned = pltpu.roll(panel, WIDTH, 1)
        spread[b, :half] = jnp.where(lane_low, panel, 0.0).astype(BF16)
        spread[b, half : 2 * half] = jnp.where(lane_low, turned, 0.0).astype(BF16)
        spread[b, 2 * half : 3 * half] = jnp.where(lane_low, 0.0, turned).astype(BF16)
        spread[b, 3 * half :] = jnp.where(lane_low, 0.0, panel).astype(BF16)
        if kind != "start":
            high, low = split_two(panel * weight[rows])
            both = jnp.concatenate([high, low], axis=1).astype(BF16)
            grams = grams + lax.dot_general(
                both, panel.astype(BF16), (((0,), (0,)), ((), ())), preferred_element_type=F32
            )
        total[b] = jnp.zeros((half, LANES), F32)
    total[n_blocks] = jnp.zeros((half, LANES), F32)

    for t in range(tiles.shape[0]):
        at = jnp.where(t < count[0], target[t], n_blocks)
        total[at] += jnp.dot(tiles[t], spread[source[t]], preferred_element_type=F32)

    if kind == "start":
        degrees = row_degree[...]
        parts = []
        for value in (degrees, pltpu.roll(degrees, WIDTH, 1)):
            high, rest = split_two(value)
            parts.append((high, *split_two(rest)))
        at = iota((DEGREE_ROWS, LANES), 0)
    else:
        gram = diagonal_blocks(grams[:LANES]) + diagonal_blocks(grams[LANES:])
        if whole:
            gram = apply_to_gram(gram, pending[:WIDTH, :WIDTH])
        message = gram_to_message(gram, whole)
    if kind == "start":
        own = lax.axis_index("group")
        own_scale[...] = lax.rsqrt(weight[pl.ds(own * rows_from, rows_from)])
    to_block = half // rows_to
    for b in range(n_blocks):
        product = total[b]
        if kind == "plain":
            high, low = split_two(product)
            mixed = jnp.concatenate([high, low, high], axis=1).astype(BF16)
            product = jnp.dot(mixed, factor[...], preferred_element_type=F32)
        product = product.astype(BF16)
        for j in range(to_block):
            d = b * to_block + j
            out[d, :rows_to] = product[j * rows_to : (j + 1) * rows_to]
            if kind == "start":
                high, middle, low = (part[b : b + 1] for part in parts[j])
                tail = jnp.where(at == 0, high, jnp.where(at == 1, middle, low))
                out[d, rows_to:] = jnp.where(at < 3, tail, 0.0).astype(BF16)
            else:
                out[d, rows_to:] = message


def sum_kernel(kind, n_from, rows, n_copies, *refs):
    if kind == "degree":
        received, copies, panel_out, scale_out = refs
    else:
        received, scale_ref, copies, panel_out, gram_out = refs
    summed = received[0].astype(F32)
    for s in range(1, n_from):
        summed = summed + received[s].astype(F32)
    panel = summed[:rows]
    if kind == "degree":
        degree = 1.0 + jnp.sum(summed[rows : rows + 3], axis=0, keepdims=True)
        scale = lax.rsqrt(lanes_to_packed(degree, rows))
        scale_out[...] = scale
    else:
        scale = scale_ref[...]
        gram_out[...] = message_to_gram(summed[rows:])
    panel = panel * scale
    panel_out[...] = panel
    if kind == "last":
        square = lax.dot_general(
            panel, panel, (((0,), (0,)), ((), ())), precision=HIGHEST, preferred_element_type=F32
        )
        message = rows_to_halves(diagonal_blocks(square))
    else:
        message = (panel * scale).astype(BF16)
    for d in range(n_copies):
        copies[d, : message.shape[0]] = message
    if kind == "degree":
        high, rest = split_two(degree)
        middle, low = split_two(rest)
        at = iota((DEGREE_ROWS, LANES), 0)
        tail = jnp.where(at == 0, high, jnp.where(at == 1, middle, jnp.where(at == 2, low, 0.0)))
        tail = tail.astype(BF16)
        for d in range(n_copies):
            copies[d, rows:] = tail


def factor_kernel(*refs):
    gram_ref, *pending, factor, parts = refs
    gram = gram_ref[...]
    if pending:
        gram = apply_to_gram(gram, pending[0][:WIDTH, :WIDTH])
    both = both_halves(inverse_factor(gram))
    factor[...] = both
    parts[...] = factor_parts(both)


def factor_last_kernel(gram, session, attendee, attendee_factor, factor, session_out, attendee_out):
    both = both_halves(inverse_factor(gram[...]))
    factor[...] = both
    session_out[...] = times_transposed(session[...], both)
    turned = times_transposed(attendee[...], attendee_factor[...])
    attendee_out[...] = halves_to_rows(times_transposed(turned, both))


def gram_last_kernel(n_from, n_copies, received, factor, copies):
    summed = received[0]
    for s in range(1, n_from):
        summed = summed + received[s]
    gram = apply_to_gram(halves_to_rows(summed), factor[:WIDTH, :WIDTH])
    message = gram_to_message(gram, True)
    for d in range(n_copies):
        copies[d] = message


def last_kernel(n_from, received, panel, out):
    summed = received[0].astype(F32)
    for s in range(1, n_from):
        summed = summed + received[s].astype(F32)
    both = both_halves(inverse_factor(message_to_gram(summed)))
    out[...] = halves_to_rows(times_transposed(panel[...], both)).T


VMEM = pl.BlockSpec(memory_space=pltpu.VMEM)
SMEM = pl.BlockSpec(memory_space=pltpu.SMEM)


def call(kernel, name, in_specs, out_shapes, scratch=(), flops=10**8, in_hbm=()):
    return pl.pallas_call(
        kernel,
        name=name,
        in_specs=in_specs,
        out_specs=[VMEM] * len(out_shapes),
        out_shape=[
            pltpu.HBM(s, d) if i in in_hbm else jax.ShapeDtypeStruct(s, d)
            for i, (s, d) in enumerate(out_shapes)
        ],
        scratch_shapes=list(scratch),
        cost_estimate=pl.CostEstimate(flops=flops, bytes_accessed=2**20, transcendentals=0),
        compiler_params=pltpu.CompilerParams(vmem_limit_bytes=32 * 1024 * 1024),
    )


def from_hbm(*arrays):
    return [pltpu.with_memory_space_constraint(array, pltpu.HBM) for array in arrays]


def exchange(array, axis):
    n, rows, lanes = array.shape
    return lax.all_to_all(
        array.reshape(n * rows, lanes), axis, split_axis=0, concat_axis=0, tiled=True
    ).reshape(n, rows, lanes)


def per_device(tile_vals, tile_rows, tile_cols, tile_count, start_panel):
    values = tile_vals[0, 0]
    slots = values.shape[0]
    n_group, n_loop = lax.axis_size("group"), lax.axis_size("loop")
    rows_dev, cols_dev = 2048, 2048
    row_blocks, col_blocks = rows_dev // SIDE, cols_dev // SIDE
    row_half, col_half = rows_dev // n_loop // 2, cols_dev // n_group // 2
    half = SIDE // 2
    count, row_at, col_at = tile_count[0], tile_rows[0, 0], tile_cols[0, 0]

    first, row_degree = call(
        degree_kernel,
        "degrees",
        [SMEM, SMEM, SMEM, VMEM, VMEM],
        [((n_group, col_half + col_blocks, LANES), F32), ((row_blocks, SIDE), F32)],
        [pltpu.VMEM((col_blocks + 1, 8, SIDE), F32), pltpu.VMEM((row_blocks + 1, 8, SIDE), F32)],
    )(count, row_at, col_at, values, start_panel[0].T)
    gathered = exchange(first, "group")
    forward, backward = call(
        functools.partial(layout_kernel, row_half, col_half),
        "layouts",
        [VMEM],
        [((slots, half, 2 * SIDE), BF16), ((slots, half, 2 * SIDE), BF16)],
    )(values)

    def scratch(blocks_from, blocks_to):
        return [
            pltpu.VMEM((blocks_from, 2 * SIDE, LANES), BF16),
            pltpu.VMEM((blocks_to + 1, half, LANES), F32),
        ]

    def factor_of(*args):
        return call(
            factor_kernel,
            "factor",
            [VMEM] * len(args),
            [((LANES, LANES), F32), ((3 * LANES, LANES), BF16)],
            in_hbm=(0,),
        )(*from_hbm(*args))

    def products(kind, whole, rows_from, n_to, rows_to, name, extra_rows, args, others=()):
        return call(
            functools.partial(product_kernel, kind, rows_from, n_to, rows_to, whole),
            name,
            [SMEM] * 3 + [VMEM] * (len(args) - 3),
            [((n_to, rows_to + extra_rows, LANES), BF16), *others],
            scratch(row_blocks, col_blocks),
        )(*args)

    gram_shape, panel_rows = ((WIDTH, WIDTH), F32), ((row_half, LANES), F32)
    panel_cols = ((col_half, LANES), F32)
    for iteration in range(ITERS):
        last = iteration == ITERS - 1
        args = (count, col_at, row_at, gathered, forward)
        to = (col_half, n_loop, row_half)
        if iteration == 0:
            outgoing, col_weight, col_scale = products(
                "start",
                False,
                *to,
                "forward_start",
                DEGREE_ROWS,
                (*args, row_degree),
                [((cols_dev // 2, LANES), F32), panel_cols],
            )
            received = exchange(outgoing, "loop")
            copies, attendee, row_scale = call(
                functools.partial(sum_kernel, "degree", n_loop, row_half, n_loop),
                "attendee_start",
                [VMEM],
                [((n_loop, row_half + DEGREE_ROWS, LANES), BF16), panel_rows, panel_rows],
            )(received)
        else:
            (outgoing,) = products(
                "plain", False, *to, "forward", 32, (*args, col_weight, col_parts)
            )
            received = exchange(outgoing, "loop")
            copies, attendee, gram = call(
                functools.partial(sum_kernel, "plain", n_loop, row_half, n_loop),
                "attendee",
                [VMEM, VMEM],
                [((n_loop, row_half, LANES), BF16), panel_rows, gram_shape],
                in_hbm=(0, 2),
            )(received, row_scale)
            row_factor, row_parts = factor_of(gram, col_factor)
        gathered = exchange(copies, "loop")
        args = (count, row_at, col_at, gathered, backward)
        to = (row_half, n_group, col_half)
        if iteration == 0:
            outgoing, row_weight = products(
                "degree", False, *to, "backward_start", 32, args, [((rows_dev // 2, LANES), F32)]
            )
        else:
            args = (*args, row_weight, row_parts)
            if last:
                args = (*args, *from_hbm(row_factor))
            (outgoing,) = products("plain", last, *to, "backward", 48 if last else 32, args)
        received = exchange(outgoing, "group")
        message = ((n_group, WIDTH // 2, LANES), F32) if last else ((n_group, col_half, LANES), BF16)
        copies, session, gram = call(
            functools.partial(sum_kernel, "last" if last else "plain", n_group, col_half, n_group),
            "session",
            [VMEM, VMEM],
            [message, panel_cols, gram_shape],
            in_hbm=(0, 2),
        )(received, col_scale)
        gathered = exchange(copies, "group")
        if iteration == 0:
            col_factor, col_parts = factor_of(gram)
        elif not last:
            col_factor, col_parts = factor_of(gram, row_factor)
    col_factor, session, attendee = call(
        factor_last_kernel,
        "factor_last",
        [VMEM] * 4,
        [((LANES, LANES), F32), panel_cols, ((2 * row_half, WIDTH), F32)],
    )(gram, session, attendee, row_factor)
    (copies,) = call(
        functools.partial(gram_last_kernel, n_group, n_loop),
        "gram_last",
        [VMEM, VMEM],
        [((n_loop, 48, LANES), BF16)],
    )(gathered, col_factor)
    (session,) = call(
        functools.partial(last_kernel, n_loop),
        "session_out",
        [VMEM, VMEM],
        [((WIDTH, 2 * col_half), F32)],
    )(exchange(copies, "loop"), session)
    return (session.T[None], attendee[None])


def solution(mesh):
    in_specs = (
        P("group", "loop", None, None, None),
        P("group", "loop", None),
        P("group", "loop", None),
        P("group", "loop"),
        P("loop", "group", None),
    )
    out_specs = (P("loop", "group", None), P("group", "loop", None))
    return jax.shard_map(
        per_device, mesh=mesh, in_specs=in_specs, out_specs=out_specs, check_vma=False
    )
```

time: 324 us -> 281 us (0.87)
  blocking collectives: 201 us -> 152 us
  waiting for transfers between devices: 16.5 us -> 36.8 us
  local copies, waits for them, and re-layouts: 24.5 us -> 5.33 us
  starting transfers between devices: 24 us -> 39.3 us
  Pallas kernels: 50.9 us -> 42.7 us
    all_to_all x11 -> x8, blocking collectives: 201 us -> 152 us  [exchange(): lax.all_to_all(array.reshape(n * rows, lanes), axis, split_axis=0, concat...]
    all_to_all x3 -> x6, waiting for transfers between devices: 16.5 us -> 36.8 us  [exchange(): lax.all_to_all(array.reshape(n * rows, lanes), axis, split_axis=0, concat...]
    all_to_all x3 -> x6, starting transfers between devices: 24 us -> 39.3 us  [exchange(): lax.all_to_all(array.reshape(n * rows, lanes), axis, split_axis=0, concat...]
    pallas_call x2, Pallas kernels: 12.1 us -> 1.61 us  [per_device(): call(functools.partial(sum_kernel, 'plain', n_loop, row_half, n_loop), 'a...]
    reshape x5 -> x0, local copies, waits for them, and re-layouts: 9.65 us -> none  [the longest x1 4.98 us: per_device(): turned.transpose(0, 1, 3, 2, 4)]
    transpose x1 -> x0, local copies, waits for them, and re-layouts: 6.16 us -> none  [per_device(): backward = turned.transpose(0, 1, 3, 2, 4).reshape(slots, half, 2 * SIDE)]
    pallas_call x10 -> x17, Pallas kernels: 32.2 us -> 37.2 us  [the longest x4 15.4 us: factor_of(): call(factor_kernel, 'factor', [VMEM] * len(args), [((LANES, LANES), F32),...]
  transfers between devices with their start and end apart: 3 -> 6, of which waited for: 2 -> 6; matrix products, arithmetic and copies ran while one was open for 6% -> 0% of each run, Pallas kernels for 0% -> 7%
where the time goes in v2:
time: 281 us; the launch traced here: 278 us
  blocking collectives  152 us (54%)
  Pallas kernels  42.7 us (15%)
  starting transfers between devices  39.3 us (14%)
  waiting for transfers between devices  36.8 us (13%)
  local copies, waits for them, and re-layouts  5.33 us (2%)
    all_to_all x8, blocking collectives, exchange(): lax.all_to_all(array.reshape(n * rows, lanes), axis, split_axis=0, concat...  152 us
    all_to_all x6, starting transfers between devices, exchange(): lax.all_to_all(array.reshape(n * rows, lanes), axis, split_axis=0, concat...  39.3 us
    all_to_all x6, waiting for transfers between devices, exchange(): lax.all_to_all(array.reshape(n * rows, lanes), axis, split_axis=0, concat...  36.8 us
    pallas_call x4, Pallas kernels, factor_of(): call(factor_kernel, 'factor', [VMEM] * len(args), [((LANES, LANES), F32),...  15.4 us
    pallas_call x6, Pallas kernels, products(): call(functools.partial(product_kernel, kind, rows_from, n_to, rows_to, wh...  12.1 us
  transfers between devices with their start and end apart: 6, of which 6 were waited for; matrix products, arithmetic and copies ran while one was open for 0% of the time, Pallas kernels for 7%

profile of v2, /device:TPU:1, one launch (start us, length us, event | category | flops | bytes accessed | tf_op | source)
XLA Modules:
  0.0 277.9 jit_solution(17044630837453955135)
XLA Ops:
  3.9 2.4 degrees.1
  6.3 10.9 %all-to-all-start = ((f32[16,80,128]{2,1,0:T(8,128)}), f32[16,80,128]{2,1,0:T(8,128)}, u32[]{:S(2)}, u32[]{:S(2)}) async-start(f32[16,80,128]{2,1,0:T(8,128)} %get-tuple-element.36), calls=%async_computation | async-start | bytes 1310720 | tf_op jit(solution)/shard_map/all_to_all | solution.py:378
  17.6 11.0 %all-to-all-done.refs_3_ = f32[16,80,128]{2,1,0:T(8,128)} async-done(((f32[16,80,128]{2,1,0:T(8,128)}), f32[16,80,128]{2,1,0:T(8,128)}, u32[]{:S(2)}, u32[]{:S(2)}) %all-to-all-start) | async-done | bytes 655392 | tf_op jit(solution)/shard_map/all_to_all | solution.py:378
  28.6 2.2 forward_start.1
  30.8 25.7 %all_to_all.84.refs_0_ = bf16[32,48,128]{2,1,0:T(8,128)(2,1)S(1)} all-to-all(bf16[32,48,128]{2,1,0:T(8,128)(2,1)S(1)} %get-tuple-element.39), channel_id=1, replica_groups=mesh['group'=16,'loop'=32] {'loop'}, dimensions={0} | all-to-all | bytes 786432 | tf_op jit(solution)/shard_map/all_to_all | solution.py:378
  57.2 20.2 %all_to_all.85.refs_3_ = bf16[32,48,128]{2,1,0:T(8,128)(2,1)S(1)} all-to-all(bf16[32,48,128]{2,1,0:T(8,128)(2,1)S(1)} %get-tuple-element.40), channel_id=1, replica_groups=mesh['group'=16,'loop'=32] {'loop'}, dimensions={0} | all-to-all | bytes 786432 | tf_op jit(solution)/shard_map/all_to_all | solution.py:378
  77.4 2.2 backward_start.1
  79.7 15.1 %all_to_all.86.refs_0_ = bf16[16,96,128]{2,1,0:T(8,128)(2,1)S(1)} all-to-all(bf16[16,96,128]{2,1,0:T(8,128)(2,1)S(1)} %get-tuple-element.42), channel_id=1, replica_groups=mesh['group'=16,'loop'=32] {'group'}, dimensions={0} | all-to-all | bytes 786432 | tf_op jit(solution)/shard_map/all_to_all | solution.py:378
  95.5 4.5 %all-to-all-start.4 = ((bf16[16,64,128]{2,1,0:T(8,128)(2,1)}), bf16[16,64,128]{2,1,0:T(8,128)(2,1)S(1)}, u32[]{:S(2)}, u32[]{:S(2)}) async-start(bf16[16,64,128]{2,1,0:T(8,128)(2,1)} %get-tuple-element.44), calls=%async_computation.4 | async-start | bytes 524288 | tf_op jit(solution)/shard_map/all_to_all | solution.py:378
  100.0 3.5 %factor.4 = (f32[128,128]{1,0:T(8,128)}, bf16[384,128]{1,0:T(8,128)(2,1)S(1)}) custom-call(f32[64,64]{1,0:T(8,128)} %get-tuple-element.46.refs_0_), custom_call_target="tpu_custom_call" | custom-call | flops 100000000 | bytes 1048576 | tf_op jit(solution)/shard_map/factor/pallas_call | solution.py:415
  103.5 3.7 %all-to-all-done.4.refs_3_ = bf16[16,64,128]{2,1,0:T(8,128)(2,1)S(1)} async-done(((bf16[16,64,128]{2,1,0:T(8,128)(2,1)}), bf16[16,64,128]{2,1,0:T(8,128)(2,1)S(1)}, u32[]{:S(2)}, u32[]{:S(2)}) %all-to-all-start.4) | async-done | bytes 262176 | tf_op jit(solution)/shard_map/all_to_all | solution.py:378
  107.9 1.8 forward.2
  109.7 21.2 %all_to_all.87.refs_0_ = bf16[32,64,128]{2,1,0:T(8,128)(2,1)S(1)} all-to-all(bf16[32,64,128]{2,1,0:T(8,128)(2,1)S(1)} %forward.2), channel_id=1, replica_groups=mesh['group'=16,'loop'=32] {'loop'}, dimensions={0} | all-to-all | bytes 1048576 | tf_op jit(solution)/shard_map/all_to_all | solution.py:378
  131.7 7.3 %all-to-all-start.6 = ((bf16[32,32,128]{2,1,0:T(8,128)(2,1)}), bf16[32,32,128]{2,1,0:T(8,128)(2,1)S(1)}, u32[]{:S(2)}, u32[]{:S(2)}) async-start(bf16[32,32,128]{2,1,0:T(8,128)(2,1)} %get-tuple-element.49), calls=%async_computation.6 | async-start | bytes 524288 | tf_op jit(solution)/shard_map/all_to_all | solution.py:378
  139.0 4.0 %factor.5 = (f32[128,128]{1,0:T(8,128)}, bf16[384,128]{1,0:T(8,128)(2,1)S(1)}) custom-call(f32[64,64]{1,0:T(8,128)} %get-tuple-element.51.refs_0_, f32[128,128]{1,0:T(8,128)} %get-tuple-element.52.refs_1_), custom_call_target="tpu_custom_call" | custom-call | flops 100000000 | bytes 1048576 | tf_op jit(solution)/shard_map/factor/pallas_call | solution.py:415
  143.0 7.6 %all-to-all-done.6.refs_3_ = bf16[32,32,128]{2,1,0:T(8,128)(2,1)S(1)} async-done(((bf16[32,32,128]{2,1,0:T(8,128)(2,1)}), bf16[32,32,128]{2,1,0:T(8,128)(2,1)S(1)}, u32[]{:S(2)}, u32[]{:S(2)}) %all-to-all-start.6) | async-done | bytes 262176 | tf_op jit(solution)/shard_map/all_to_all | solution.py:378
  153.1 14.7 %all_to_all.88.refs_0_ = bf16[16,96,128]{2,1,0:T(8,128)(2,1)S(1)} all-to-all(bf16[16,96,128]{2,1,0:T(8,128)(2,1)S(1)} %backward.2), channel_id=1, replica_groups=mesh['group'=16,'loop'=32] {'group'}, dimensions={0} | all-to-all | bytes 786432 | tf_op jit(solution)/shard_map/all_to_all | solution.py:378
  168.5 4.7 %all-to-all-start.8 = ((bf16[16,64,128]{2,1,0:T(8,128)(2,1)}), bf16[16,64,128]{2,1,0:T(8,128)(2,1)S(1)}, u32[]{:S(2)}, u32[]{:S(2)}) async-start(bf16[16,64,128]{2,1,0:T(8,128)(2,1)} %get-tuple-element.54), calls=%async_computation.8 | async-start | bytes 524288 | tf_op jit(solution)/shard_map/all_to_all | solution.py:378
  173.2 4.0 %factor.6 = (f32[128,128]{1,0:T(8,128)}, bf16[384,128]{1,0:T(8,128)(2,1)S(1)}) custom-call(f32[64,64]{1,0:T(8,128)} %get-tuple-element.55.refs_0_, f32[128,128]{1,0:T(8,128)} %get-tuple-element.56.refs_1_), custom_call_target="tpu_custom_call" | custom-call | flops 100000000 | bytes 1048576 | tf_op jit(solution)/shard_map/factor/pallas_call | solution.py:415
  177.2 3.3 %all-to-all-done.8.refs_3_ = bf16[16,64,128]{2,1,0:T(8,128)(2,1)S(1)} async-done(((bf16[16,64,128]{2,1,0:T(8,128)(2,1)}), bf16[16,64,128]{2,1,0:T(8,128)(2,1)S(1)}, u32[]{:S(2)}, u32[]{:S(2)}) %all-to-all-start.8) | async-done | bytes 262176 | tf_op jit(solution)/shard_map/all_to_all | solution.py:378
  181.1 1.8 forward.3
  182.9 21.1 %all_to_all.89.refs_0_ = bf16[32,64,128]{2,1,0:T(8,128)(2,1)S(1)} all-to-all(bf16[32,64,128]{2,1,0:T(8,128)(2,1)S(1)} %forward.3), channel_id=1, replica_groups=mesh['group'=16,'loop'=32] {'loop'}, dimensions={0} | all-to-all | bytes 1048576 | tf_op jit(solution)/shard_map/all_to_all | solution.py:378
  204.9 7.3 %all-to-all-start.10 = ((bf16[32,32,128]{2,1,0:T(8,128)(2,1)}), bf16[32,32,128]{2,1,0:T(8,128)(2,1)S(1)}, u32[]{:S(2)}, u32[]{:S(2)}) async-start(bf16[32,32,128]{2,1,0:T(8,128)(2,1)} %get-tuple-element.58), calls=%async_computation.10 | async-start | bytes 524288 | tf_op jit(solution)/shard_map/all_to_all | solution.py:378
  212.2 4.0 %factor.7 = (f32[128,128]{1,0:T(8,128)}, bf16[384,128]{1,0:T(8,128)(2,1)S(1)}) custom-call(f32[64,64]{1,0:T(8,128)} %get-tuple-element.59.refs_0_, f32[128,128]{1,0:T(8,128)} %get-tuple-element.60.refs_1_), custom_call_target="tpu_custom_call" | custom-call | flops 100000000 | bytes 1048576 | tf_op jit(solution)/shard_map/factor/pallas_call | solution.py:415
  216.1 7.6 %all-to-all-done.10.refs_3_ = bf16[32,32,128]{2,1,0:T(8,128)(2,1)S(1)} async-done(((bf16[32,32,128]{2,1,0:T(8,128)(2,1)}), bf16[32,32,128]{2,1,0:T(8,128)(2,1)S(1)}, u32[]{:S(2)}, u32[]{:S(2)}) %all-to-all-start.10) | async-done | bytes 262176 | tf_op jit(solution)/shard_map/all_to_all | solution.py:378
  224.4 2.3 backward.3
  226.7 15.4 %all_to_all.90.refs_0_ = bf16[16,112,128]{2,1,0:T(8,128)(2,1)S(1)} all-to-all(bf16[16,112,128]{2,1,0:T(8,128)(2,1)S(1)} %backward.3), channel_id=1, replica_groups=mesh['group'=16,'loop'=32] {'group'}, dimensions={0} | all-to-all | bytes 917504 | tf_op jit(solution)/shard_map/all_to_all | solution.py:378
  243.2 4.6 %all-to-all-start.12 = ((f32[16,32,128]{2,1,0:T(8,128)}), f32[16,32,128]{2,1,0:T(8,128)S(1)}, u32[]{:S(2)}, u32[]{:S(2)}) async-start(f32[16,32,128]{2,1,0:T(8,128)} %get-tuple-element.63), calls=%async_computation.12 | async-start | bytes 524288 | tf_op jit(solution)/shard_map/all_to_all | solution.py:378
  247.9 3.6 %factor_last.1 = (f32[128,128]{1,0:T(8,128)S(1)}, f32[64,128]{1,0:T(8,128)S(1)}, f32[64,64]{1,0:T(8,128)}) custom-call(f32[64,64]{1,0:T(8,128)S(1)} %copy-done.14, f32[64,128]{1,0:T(8,128)S(1)} %get-tuple-element.65.session, f32[32,128]{1,0:T(8,128)S(1)} %get-tuple-element.66.attendee, f32[128,128]{1,0:T(8,128)S(1)} %copy-done.2), custom_call_target="tpu_custom_call" | custom-call | flops 100000000 | bytes 1048576 | tf_op jit(solution)/shard_map/factor_last/pallas_call | solution.py:494
  251.4 3.7 %all-to-all-done.12.received = f32[16,32,128]{2,1,0:T(8,128)S(1)} async-done(((f32[16,32,128]{2,1,0:T(8,128)}), f32[16,32,128]{2,1,0:T(8,128)S(1)}, u32[]{:S(2)}, u32[]{:S(2)}) %all-to-all-start.12) | async-done | bytes 262176 | tf_op jit(solution)/shard_map/all_to_all | solution.py:378
  255.7 19.1 %all_to_all.91.received = bf16[32,48,128]{2,1,0:T(8,128)(2,1)S(1)} all-to-all(bf16[32,48,128]{2,1,0:T(8,128)(2,1)S(1)} %gram_last.1), channel_id=1, replica_groups=mesh['group'=16,'loop'=32] {'loop'}, dimensions={0} | all-to-all | bytes 786432 | tf_op jit(solution)/shard_map/all_to_all | solution.py:378
  274.8 3.2 %session_out.1 = f32[64,128]{1,0:T(8,128)} custom-call(bf16[32,48,128]{2,1,0:T(8,128)(2,1)S(1)} %all_to_all.91.received, f32[64,128]{1,0:T(8,128)S(1)} %get-tuple-element.68.panel), custom_call_target="tpu_custom_call" | custom-call | flops 100000000 | bytes 1048576 | tf_op jit(solution)/shard_map/session_out/pallas_call | solution.py:506
  (39 shorter events, 13.2 us)
Async XLA Ops:
  1.3 0.7 copy-start.4
  1.3 0.7 copy-start.9
  2.0 1.2 copy-start
  3.2 0.8 copy-start.3
  3.9 13.3 %copy-start.1 = (bf16[1,1,32,128,128]{4,3,2,1,0:T(8,128)(2,1)S(1)}, bf16[1,1,32,128,128]{4,3,2,1,0:T(8,128)(2,1)}, u32[]{:S(2)}) copy-start(bf16[1,1,32,128,128]{4,3,2,1,0:T(8,128)(2,1)} %param.5) | copy-start | bytes 3145732
  6.3 22.3 %all-to-all-start = ((f32[16,80,128]{2,1,0:T(8,128)}), f32[16,80,128]{2,1,0:T(8,128)}, u32[]{:S(2)}, u32[]{:S(2)}) async-start(f32[16,80,128]{2,1,0:T(8,128)} %get-tuple-element.36), calls=%async_computation | async-start | bytes 1310720 | tf_op jit(solution)/shard_map/all_to_all | solution.py:378
  95.5 11.7 %all-to-all-start.4 = ((bf16[16,64,128]{2,1,0:T(8,128)(2,1)}), bf16[16,64,128]{2,1,0:T(8,128)(2,1)S(1)}, u32[]{:S(2)}, u32[]{:S(2)}) async-start(bf16[16,64,128]{2,1,0:T(8,128)(2,1)} %get-tuple-element.44), calls=%async_computation.4 | async-start | bytes 524288 | tf_op jit(solution)/shard_map/all_to_all | solution.py:378
  107.2 0.7 copy-start.5
  107.2 0.7 copy-start.10
  131.7 18.9 %all-to-all-start.6 = ((bf16[32,32,128]{2,1,0:T(8,128)(2,1)}), bf16[32,32,128]{2,1,0:T(8,128)(2,1)S(1)}, u32[]{:S(2)}, u32[]{:S(2)}) async-start(bf16[32,32,128]{2,1,0:T(8,128)(2,1)} %get-tuple-element.49), calls=%async_computation.6 | async-start | bytes 524288 | tf_op jit(solution)/shard_map/all_to_all | solution.py:378
  150.6 0.7 copy-start.6
  150.6 0.7 copy-start.11
  168.5 11.9 %all-to-all-start.8 = ((bf16[16,64,128]{2,1,0:T(8,128)(2,1)}), bf16[16,64,128]{2,1,0:T(8,128)(2,1)S(1)}, u32[]{:S(2)}, u32[]{:S(2)}) async-start(bf16[16,64,128]{2,1,0:T(8,128)(2,1)} %get-tuple-element.54), calls=%async_computation.8 | async-start | bytes 524288 | tf_op jit(solution)/shard_map/all_to_all | solution.py:378
  180.4 0.7 copy-start.7
  180.4 0.7 copy-start.12
  204.9 18.9 %all-to-all-start.10 = ((bf16[32,32,128]{2,1,0:T(8,128)(2,1)}), bf16[32,32,128]{2,1,0:T(8,128)(2,1)S(1)}, u32[]{:S(2)}, u32[]{:S(2)}) async-start(bf16[32,32,128]{2,1,0:T(8,128)(2,1)} %get-tuple-element.58), calls=%async_computation.10 | async-start | bytes 524288 | tf_op jit(solution)/shard_map/all_to_all | solution.py:378
  223.7 0.7 copy-start.8
  223.7 0.7 copy-start.13
  243.2 4.6 %copy-start.2 = (f32[128,128]{1,0:T(8,128)S(1)}, f32[128,128]{1,0:T(8,128)}, u32[]{:S(2)}) copy-start(f32[128,128]{1,0:T(8,128)} %get-tuple-element.62.refs_7_.attendee_factor) | copy-start | bytes 196612
  243.2 4.6 %copy-start.14 = (f32[64,64]{1,0:T(8,128)S(1)}, f32[64,64]{1,0:T(8,128)}, u32[]{:S(2)}) copy-start(f32[64,64]{1,0:T(8,128)} %get-tuple-element.64.gram) | copy-start | bytes 49156
  243.2 11.8 %all-to-all-start.12 = ((f32[16,32,128]{2,1,0:T(8,128)}), f32[16,32,128]{2,1,0:T(8,128)S(1)}, u32[]{:S(2)}, u32[]{:S(2)}) async-start(f32[16,32,128]{2,1,0:T(8,128)} %get-tuple-element.63), calls=%async_computation.12 | async-start | bytes 524288 | tf_op jit(solution)/shard_map/all_to_all | solution.py:378

commit v3 on v2

--- a/solution.py
+++ b/solution.py
@@ -16,6 +16,9 @@
 F32 = jnp.float32
 BF16 = jnp.bfloat16
 HIGHEST = lax.Precision.HIGHEST
+
+LOOP_ORDER = [k % 8 * 4 + k // 8 for k in range(32)]
+LOOP_PLACE = [LOOP_ORDER.index(at) for at in range(32)]
 
 
 def iota(shape, dim):
@@ -143,9 +146,10 @@
 
 def message_to_gram(message):
     shape = (WIDTH, WIDTH)
-    square = halves_to_rows(message[:32])
+    half = message.shape[0] // 2
+    square = halves_to_rows(jnp.concatenate([message[:16], message[half : half + 16]], axis=0))
     on_diagonal = iota(shape, 0) == iota(shape, 1)
-    whole = square if message.shape[0] == 32 else square + message[32:33, :WIDTH]
+    whole = square if half == 16 else square + message[16:17, :WIDTH]
     return jnp.where(on_diagonal, whole, square + square.T)
 
 
@@ -187,16 +191,16 @@
             backward[t, at : at + col_half, SIDE:] = turned[2 * at + col_half : 2 * at + 2 * col_half]
 
 
-def product_kernel(kind, rows_from, n_to, rows_to, whole, *refs):
-    count, source, target, gathered, tiles = refs[:5]
+def product_kernel(kind, source, target, rows_from, n_to, rows_to, whole, from_pair, *refs):
+    index, gathered, tiles, *refs, spread, total = refs
     if kind == "start":
-        row_degree, out, weight, own_scale, spread, total = refs[5:]
+        row_degree, out, weight, own_scale = refs
     elif kind == "degree":
-        out, weight, spread, total = refs[5:]
+        out, weight = refs
     elif whole:
-        weight, factor, pending, out, spread, total = refs[5:]
+        weight, factor, pending, out = refs
     else:
-        weight, factor, out, spread, total = refs[5:]
+        weight, factor, out = refs
     half = SIDE // 2
     lane_low = iota((half, LANES), 1) < WIDTH
     n_blocks = total.shape[0] - 1
@@ -211,16 +215,19 @@
         if kind == "start":
             packed_degree = lanes_to_packed(degree[b : b + 1], half)
             weight[rows] = packed_degree
-            panel = (gathered[b, :rows_from] * lax.rsqrt(packed_degree)).astype(BF16).astype(F32)
+            place = b % 2 * (n_blocks // 2) + b // 2
+            panel = gathered[place, :rows_from] * lax.rsqrt(packed_degree)
+            panel = panel.astype(BF16).astype(F32)
         else:
-            parts = [
-                gathered[b * per_block + j, :rows_from].astype(F32) for j in range(per_block)
-            ]
+            places = [b * per_block + j for j in range(per_block)]
+            if per_block > 1:
+                places = [LOOP_PLACE[place] for place in places]
+            parts = [gathered[place, :rows_from].astype(F32) for place in places]
             panel = parts[0] if per_block == 1 else jnp.concatenate(parts, axis=0)
         if kind == "degree":
             packs = []
-            for j in range(per_block):
-                pieces = gathered[b * per_block + j, rows_from:].astype(F32)
+            for place in places:
+                pieces = gathered[place, rows_from:].astype(F32)
                 packs.append(lanes_to_packed(jnp.sum(pieces[:3], axis=0, keepdims=True), rows_from))
             packed_degree = packs[0] if per_block == 1 else jnp.concatenate(packs, axis=0)
             weight[rows] = packed_degree
@@ -239,8 +246,9 @@
     total[n_blocks] = jnp.zeros((half, LANES), F32)
 
     for t in range(tiles.shape[0]):
-        at = jnp.where(t < count[0], target[t], n_blocks)
-        total[at] += jnp.dot(tiles[t], spread[source[t]], preferred_element_type=F32)
+        total[index[target, t]] += jnp.dot(
+            tiles[t], spread[index[source, t]], preferred_element_type=F32
+        )
 
     if kind == "start":
         degrees = row_degree[...]
@@ -254,8 +262,13 @@
         if whole:
             gram = apply_to_gram(gram, pending[:WIDTH, :WIDTH])
         message = gram_to_message(gram, whole)
+        halves = [message[:16], message[16:32]]
+        if whole:
+            halves = [jnp.concatenate([part, message[32:]], axis=0) for part in halves]
+        if from_pair:
+            halves = [jnp.where(index[4, 1] == 0, *halves)] * 2
     if kind == "start":
-        own = lax.axis_index("group")
+        own = index[4, 0]
         own_scale[...] = lax.rsqrt(weight[pl.ds(own * rows_from, rows_from)])
     to_block = half // rows_to
     for b in range(n_blocks):
@@ -266,14 +279,14 @@
             product = jnp.dot(mixed, factor[...], preferred_element_type=F32)
         product = product.astype(BF16)
         for j in range(to_block):
-            d = b * to_block + j
+            d = LOOP_PLACE[b * to_block + j] if to_block > 1 else b
             out[d, :rows_to] = product[j * rows_to : (j + 1) * rows_to]
             if kind == "start":
                 high, middle, low = (part[b : b + 1] for part in parts[j])
                 tail = jnp.where(at == 0, high, jnp.where(at == 1, middle, low))
                 out[d, rows_to:] = jnp.where(at < 3, tail, 0.0).astype(BF16)
             else:
-                out[d, rows_to:] = message
+                out[d, rows_to:] = halves[b % 2]
 
 
 def sum_kernel(kind, n_from, rows, n_copies, *refs):
@@ -291,7 +304,7 @@
         scale_out[...] = scale
     else:
         scale = scale_ref[...]
-        gram_out[...] = message_to_gram(summed[rows:])
+        gram_out[...] = summed[rows:]
     panel = panel * scale
     panel_out[...] = panel
     if kind == "last":
@@ -315,7 +328,7 @@
 
 def factor_kernel(*refs):
     gram_ref, *pending, factor, parts = refs
-    gram = gram_ref[...]
+    gram = message_to_gram(gram_ref[...])
     if pending:
         gram = apply_to_gram(gram, pending[0][:WIDTH, :WIDTH])
     both = both_halves(inverse_factor(gram))
@@ -324,7 +337,7 @@
 
 
 def factor_last_kernel(gram, session, attendee, attendee_factor, factor, session_out, attendee_out):
-    both = both_halves(inverse_factor(gram[...]))
+    both = both_halves(inverse_factor(message_to_gram(gram[...])))
     factor[...] = both
     session_out[...] = times_transposed(session[...], both)
     turned = times_transposed(attendee[...], attendee_factor[...])
@@ -345,7 +358,8 @@
     summed = received[0].astype(F32)
     for s in range(1, n_from):
         summed = summed + received[s].astype(F32)
-    both = both_halves(inverse_factor(message_to_gram(summed)))
+    message = jnp.concatenate([summed[:16], summed[32:], summed[16:]], axis=0)
+    both = both_halves(inverse_factor(message_to_gram(message)))
     out[...] = halves_to_rows(times_transposed(panel[...], both)).T
 
 
@@ -373,10 +387,15 @@
     return [pltpu.with_memory_space_constraint(array, pltpu.HBM) for array in arrays]
 
 
-def exchange(array, axis):
+def exchange(array, axis, groups=None):
     n, rows, lanes = array.shape
     return lax.all_to_all(
-        array.reshape(n * rows, lanes), axis, split_axis=0, concat_axis=0, tiled=True
+        array.reshape(n * rows, lanes),
+        axis,
+        split_axis=0,
+        concat_axis=0,
+        axis_index_groups=groups or ([LOOP_ORDER] if axis == "loop" else None),
+        tiled=True,
     ).reshape(n, rows, lanes)
 
 
@@ -394,10 +413,12 @@
         degree_kernel,
         "degrees",
         [SMEM, SMEM, SMEM, VMEM, VMEM],
-        [((n_group, col_half + col_blocks, LANES), F32), ((row_blocks, SIDE), F32)],
+        [((n_group // 2, col_half + col_blocks, LANES), F32), ((row_blocks, SIDE), F32)],
         [pltpu.VMEM((col_blocks + 1, 8, SIDE), F32), pltpu.VMEM((row_blocks + 1, 8, SIDE), F32)],
-    )(count, row_at, col_at, values, start_panel[0].T)
-    gathered = exchange(first, "group")
+    )(count, row_at, col_at, *from_hbm(values, start_panel[0].T))
+    pairs = [[i, i + 1] for i in range(0, n_group, 2)]
+    gathered = exchange(first, "group", [list(range(core, n_group, 2)) for core in range(2)])
+    gathered = lax.all_gather(gathered, "group", axis_index_groups=pairs, axis=0, tiled=True)
     forward, backward = call(
         functools.partial(layout_kernel, row_half, col_half),
         "layouts",
@@ -405,11 +426,15 @@
         [((slots, half, 2 * SIDE), BF16), ((slots, half, 2 * SIDE), BF16)],
     )(values)
 
-    def scratch(blocks_from, blocks_to):
-        return [
-            pltpu.VMEM((blocks_from, 2 * SIDE, LANES), BF16),
-            pltpu.VMEM((blocks_to + 1, half, LANES), F32),
-        ]
+    alive = jnp.arange(slots) < count
+    group = lax.axis_index("group")
+    index = [row_at, col_at, jnp.where(alive, row_at, row_blocks)]
+    index += [jnp.where(alive, col_at, col_blocks), jnp.pad(jnp.stack([group, group % 2]), (0, slots - 2))]
+    index = jnp.pad(jnp.stack(index).astype(jnp.int32), ((0, 3), (0, LANES - slots)))
+    scratch = [
+        pltpu.VMEM((col_blocks, 2 * SIDE, LANES), BF16),
+        pltpu.VMEM((row_blocks + 1, half, LANES), F32),
+    ]
 
     def factor_of(*args):
         return call(
@@ -420,24 +445,32 @@
             in_hbm=(0,),
         )(*from_hbm(*args))
 
-    def products(kind, whole, rows_from, n_to, rows_to, name, extra_rows, args, others=()):
+    def products(kind, way, whole, rows_from, n_to, rows_to, name, extra_rows, args, others=()):
         return call(
-            functools.partial(product_kernel, kind, rows_from, n_to, rows_to, whole),
+            functools.partial(
+                product_kernel, kind, *way, rows_from, n_to, rows_to, whole, n_to == n_loop
+            ),
             name,
-            [SMEM] * 3 + [VMEM] * (len(args) - 3),
+            [SMEM] + [VMEM] * len(args),
             [((n_to, rows_to + extra_rows, LANES), BF16), *others],
-            scratch(row_blocks, col_blocks),
-        )(*args)
-
-    gram_shape, panel_rows = ((WIDTH, WIDTH), F32), ((row_half, LANES), F32)
+            scratch,
+        )(index, *args)
+
+    def swap_cores(half_message):
+        return lax.all_gather(
+            half_message, "group", axis_index_groups=pairs, axis=0, tiled=True
+        )
+
+    panel_rows = ((row_half, LANES), F32)
     panel_cols = ((col_half, LANES), F32)
     for iteration in range(ITERS):
         last = iteration == ITERS - 1
-        args = (count, col_at, row_at, gathered, forward)
+        args = (gathered, forward)
         to = (col_half, n_loop, row_half)
         if iteration == 0:
             outgoing, col_weight, col_scale = products(
                 "start",
+                (1, 2),
                 False,
                 *to,
                 "forward_start",
@@ -454,49 +487,50 @@
             )(received)
         else:
             (outgoing,) = products(
-                "plain", False, *to, "forward", 32, (*args, col_weight, col_parts)
+                "plain", (1, 2), False, *to, "forward", 16, (*args, col_weight, col_parts)
             )
             received = exchange(outgoing, "loop")
             copies, attendee, gram = call(
                 functools.partial(sum_kernel, "plain", n_loop, row_half, n_loop),
                 "attendee",
                 [VMEM, VMEM],
-                [((n_loop, row_half, LANES), BF16), panel_rows, gram_shape],
+                [((n_loop, row_half, LANES), BF16), panel_rows, ((16, LANES), F32)],
                 in_hbm=(0, 2),
             )(received, row_scale)
-            row_factor, row_parts = factor_of(gram, col_factor)
+            row_factor, row_parts = factor_of(swap_cores(gram), col_factor)
         gathered = exchange(copies, "loop")
-        args = (count, row_at, col_at, gathered, backward)
+        args = (gathered, backward)
         to = (row_half, n_group, col_half)
+        message_rows = 32 if last else 16
         if iteration == 0:
             outgoing, row_weight = products(
-                "degree", False, *to, "backward_start", 32, args, [((rows_dev // 2, LANES), F32)]
+                "degree", (0, 3), False, *to, "backward_start", 16, args, [((rows_dev // 2, LANES), F32)]
             )
         else:
             args = (*args, row_weight, row_parts)
             if last:
                 args = (*args, *from_hbm(row_factor))
-            (outgoing,) = products("plain", last, *to, "backward", 48 if last else 32, args)
+            (outgoing,) = products("plain", (0, 3), last, *to, "backward", message_rows, args)
         received = exchange(outgoing, "group")
         message = ((n_group, WIDTH // 2, LANES), F32) if last else ((n_group, col_half, LANES), BF16)
         copies, session, gram = call(
             functools.partial(sum_kernel, "last" if last else "plain", n_group, col_half, n_group),
             "session",
             [VMEM, VMEM],
-            [message, panel_cols, gram_shape],
+            [message, panel_cols, ((message_rows, LANES), F32)],
             in_hbm=(0, 2),
         )(received, col_scale)
         gathered = exchange(copies, "group")
         if iteration == 0:
-            col_factor, col_parts = factor_of(gram)
+            col_factor, col_parts = factor_of(swap_cores(gram))
         elif not last:
-            col_factor, col_parts = factor_of(gram, row_factor)
+            col_factor, col_parts = factor_of(swap_cores(gram), row_factor)
     col_factor, session, attendee = call(
         factor_last_kernel,
         "factor_last",
         [VMEM] * 4,
         [((LANES, LANES), F32), panel_cols, ((2 * row_half, WIDTH), F32)],
-    )(gram, session, attendee, row_factor)
+    )(*from_hbm(swap_cores(gram)), session, attendee, row_factor)
     (copies,) = call(
         functools.partial(gram_last_kernel, n_group, n_loop),
         "gram_last",

time: 281 us -> 272 us (0.968)
  waiting for transfers between devices: 36.8 us -> 19.6 us
  blocking collectives: 152 us -> 163 us
  starting transfers between devices: 39.3 us -> 35.8 us
  local copies, waits for them, and re-layouts: 5.33 us -> 2.06 us
    all_gather x0 -> x6, blocking collectives: none -> 19.4 us  [the longest x5 12 us: swap_cores(): lax.all_gather(half_message, 'group', axis_index_groups=pairs, axis=0, ti...]
    all_to_all x6, waiting for transfers between devices: 36.8 us -> 19.6 us  [exchange(): lax.all_to_all(array.reshape(n * rows, lanes), axis, split_axis=0, concat...]
    all_to_all x8, blocking collectives: 152 us -> 144 us  [exchange(): lax.all_to_all(array.reshape(n * rows, lanes), axis, split_axis=0, concat...]
    all_to_all x6, starting transfers between devices: 39.3 us -> 35.8 us  [exchange(): lax.all_to_all(array.reshape(n * rows, lanes), axis, split_axis=0, concat...]
    unnamed x30 -> x28, local copies, waits for them, and re-layouts: 5.33 us -> 2.02 us
  transfers between devices with their start and end apart: 6 -> 6, of which waited for: 6 -> 6; matrix products, arithmetic and copies ran while one was open for 0% -> 0% of each run, Pallas kernels for 7% -> 8%
where the time goes in v3:
time: 272 us; the launch traced here: 266 us
  blocking collectives  163 us (60%)
  Pallas kernels  44.1 us (16%)
  starting transfers between devices  35.8 us (13%)
  waiting for transfers between devices  19.6 us (7%)
    all_to_all x8, blocking collectives, exchange(): lax.all_to_all(array.reshape(n * rows, lanes), axis, split_axis=0, concat...  144 us
    all_to_all x6, starting transfers between devices, exchange(): lax.all_to_all(array.reshape(n * rows, lanes), axis, split_axis=0, concat...  35.8 us
    all_to_all x6, waiting for transfers between devices, exchange(): lax.all_to_all(array.reshape(n * rows, lanes), axis, split_axis=0, concat...  19.6 us
    pallas_call x4, Pallas kernels, factor_of(): call(factor_kernel, 'factor', [VMEM] * len(args), [((LANES, LANES), F32),...  15.8 us
    all_gather x5, blocking collectives, swap_cores(): lax.all_gather(half_message, 'group', axis_index_groups=pairs, axis=0, ti...  12 us
    pallas_call x6, Pallas kernels, products(): call(functools.partial(product_kernel, kind, *way, rows_from, n_to, rows_...  11.8 us
    all_gather x1, blocking collectives, per_device(): lax.all_gather(gathered, 'group', axis_index_groups=pairs, axis=0, tiled=...  7.47 us
  transfers between devices with their start and end apart: 6, of which 6 were waited for; matrix products, arithmetic and copies ran while one was open for 0% of the time, Pallas kernels for 8%

profile of v3, /device:TPU:1, one launch (start us, length us, event | category | flops | bytes accessed | tf_op | source)
XLA Modules:
  0.0 266.4 jit_solution(9507003857520097195)
XLA Ops:
  2.7 3.0 %degrees.1 = (f32[8,80,128]{2,1,0:T(8,128)}, f32[16,128]{1,0:T(8,128)S(1)}) custom-call(s32[1]{0:T(128)} %bitcast.21.count, s32[32]{0:T(128)S(1)} %bitcast.24, s32[32]{0:T(128)S(1)} %bitcast.26, bf16[32,128,128]{2,1,0:T(8,128)(2,1)} %bitcast.22, f32[64,128]{1,0:T(8,128)} %bitcast.29), custom_call_target="tpu_custom_call" | custom-call | flops 100000000 | bytes 1048576 | tf_op jit(solution)/shard_map/degrees/pallas_call | solution.py:412
  5.6 6.6 %all-to-all-start = ((f32[8,80,128]{2,1,0:T(8,128)}), f32[8,80,128]{2,1,0:T(8,128)}, u32[]{:S(2)}, u32[]{:S(2)}) async-start(f32[8,80,128]{2,1,0:T(8,128)} %get-tuple-element.36), calls=%async_computation | async-start | bytes 655360 | tf_op jit(solution)/shard_map/all_to_all | solution.py:392
  13.5 5.4 %all-to-all-done = f32[8,80,128]{2,1,0:T(8,128)} async-done(((f32[8,80,128]{2,1,0:T(8,128)}), f32[8,80,128]{2,1,0:T(8,128)}, u32[]{:S(2)}, u32[]{:S(2)}) %all-to-all-start) | async-done | bytes 327712 | tf_op jit(solution)/shard_map/all_to_all | solution.py:392
  18.9 7.5 %all_gather.18.refs_1_ = f32[16,80,128]{2,1,0:T(8,128)S(1)} all-gather(f32[8,80,128]{2,1,0:T(8,128)} %all-to-all-done), channel_id=1, replica_groups={{0,32},{64,96},{128,160},{192,224},{256,288},{320,352},{384,416},{448,4..., dimensions={0}, use_global_device_ids=true | all-gather | bytes 983040 | tf_op jit(solution)/shard_map/all_gather | solution.py:421
  28.0 26.3 %all_to_all.84.refs_0_ = bf16[32,48,128]{2,1,0:T(8,128)(2,1)S(1)} all-to-all(bf16[32,48,128]{2,1,0:T(8,128)(2,1)S(1)} %get-tuple-element.39), channel_id=1, replica_groups={{0,4,8,12,16,20,24,28,1,5,9,13,17,21,25,29,2,6,10,14,18,22,26,30,3,7,11..., dimensions={0} | all-to-all | bytes 786432 | tf_op jit(solution)/shard_map/all_to_all | solution.py:392
  55.1 19.6 %all_to_all.85.refs_1_ = bf16[32,48,128]{2,1,0:T(8,128)(2,1)S(1)} all-to-all(bf16[32,48,128]{2,1,0:T(8,128)(2,1)S(1)} %get-tuple-element.40), channel_id=1, replica_groups={{0,4,8,12,16,20,24,28,1,5,9,13,17,21,25,29,2,6,10,14,18,22,26,30,3,7,11..., dimensions={0} | all-to-all | bytes 786432 | tf_op jit(solution)/shard_map/all_to_all | solution.py:392
  74.7 2.3 backward_start.1
  77.0 15.2 %all_to_all.86.refs_0_ = bf16[16,80,128]{2,1,0:T(8,128)(2,1)S(1)} all-to-all(bf16[16,80,128]{2,1,0:T(8,128)(2,1)S(1)} %get-tuple-element.42), channel_id=1, replica_groups=mesh['group'=16,'loop'=32] {'group'}, dimensions={0} | all-to-all | bytes 655360 | tf_op jit(solution)/shard_map/all_to_all | solution.py:392
  93.0 4.6 %all-to-all-start.4 = ((bf16[16,64,128]{2,1,0:T(8,128)(2,1)}), bf16[16,64,128]{2,1,0:T(8,128)(2,1)S(1)}, u32[]{:S(2)}, u32[]{:S(2)}) async-start(bf16[16,64,128]{2,1,0:T(8,128)(2,1)} %get-tuple-element.44), calls=%async_computation.4 | async-start | bytes 524288 | tf_op jit(solution)/shard_map/all_to_all | solution.py:392
  97.6 1.9 all_gather.19.refs_0_
  99.6 3.5 %factor.4 = (f32[128,128]{1,0:T(8,128)}, bf16[384,128]{1,0:T(8,128)(2,1)S(1)}) custom-call(f32[32,128]{1,0:T(8,128)} %all_gather.19.refs_0_), custom_call_target="tpu_custom_call" | custom-call | flops 100000000 | bytes 1048576 | tf_op jit(solution)/shard_map/factor/pallas_call | solution.py:440
  106.7 17.7 %all_to_all.87.refs_0_ = bf16[32,48,128]{2,1,0:T(8,128)(2,1)S(1)} all-to-all(bf16[32,48,128]{2,1,0:T(8,128)(2,1)S(1)} %forward.2), channel_id=1, replica_groups={{0,4,8,12,16,20,24,28,1,5,9,13,17,21,25,29,2,6,10,14,18,22,26,30,3,7,11..., dimensions={0} | all-to-all | bytes 786432 | tf_op jit(solution)/shard_map/all_to_all | solution.py:392
  125.2 7.6 %all-to-all-start.6 = ((bf16[32,32,128]{2,1,0:T(8,128)(2,1)}), bf16[32,32,128]{2,1,0:T(8,128)(2,1)S(1)}, u32[]{:S(2)}, u32[]{:S(2)}) async-start(bf16[32,32,128]{2,1,0:T(8,128)(2,1)} %get-tuple-element.49), calls=%async_computation.6 | async-start | bytes 524288 | tf_op jit(solution)/shard_map/all_to_all | solution.py:392
  132.8 3.0 %all_gather.20.refs_0_ = f32[32,128]{1,0:T(8,128)} all-gather(f32[16,128]{1,0:T(8,128)S(1)} %copy-done.12), channel_id=1, replica_groups={{0,32},{64,96},{128,160},{192,224},{256,288},{320,352},{384,416},{448,4..., dimensions={0}, use_global_device_ids=true | all-gather | bytes 24576 | tf_op jit(solution)/shard_map/all_gather | solution.py:460
  135.8 4.1 %factor.5 = (f32[128,128]{1,0:T(8,128)}, bf16[384,128]{1,0:T(8,128)(2,1)S(1)}) custom-call(f32[32,128]{1,0:T(8,128)} %all_gather.20.refs_0_, f32[128,128]{1,0:T(8,128)} %get-tuple-element.52.refs_1_), custom_call_target="tpu_custom_call" | custom-call | flops 100000000 | bytes 1048576 | tf_op jit(solution)/shard_map/factor/pallas_call | solution.py:440
  139.9 5.2 %all-to-all-done.6.refs_1_ = bf16[32,32,128]{2,1,0:T(8,128)(2,1)S(1)} async-done(((bf16[32,32,128]{2,1,0:T(8,128)(2,1)}), bf16[32,32,128]{2,1,0:T(8,128)(2,1)S(1)}, u32[]{:S(2)}, u32[]{:S(2)}) %all-to-all-start.6) | async-done | bytes 262176 | tf_op jit(solution)/shard_map/all_to_all | solution.py:392
  146.9 14.9 %all_to_all.88.refs_0_ = bf16[16,80,128]{2,1,0:T(8,128)(2,1)S(1)} all-to-all(bf16[16,80,128]{2,1,0:T(8,128)(2,1)S(1)} %backward.2), channel_id=1, replica_groups=mesh['group'=16,'loop'=32] {'group'}, dimensions={0} | all-to-all | bytes 655360 | tf_op jit(solution)/shard_map/all_to_all | solution.py:392
  162.6 4.8 %all-to-all-start.8 = ((bf16[16,64,128]{2,1,0:T(8,128)(2,1)}), bf16[16,64,128]{2,1,0:T(8,128)(2,1)S(1)}, u32[]{:S(2)}, u32[]{:S(2)}) async-start(bf16[16,64,128]{2,1,0:T(8,128)(2,1)} %get-tuple-element.54), calls=%async_computation.8 | async-start | bytes 524288 | tf_op jit(solution)/shard_map/all_to_all | solution.py:392
  167.4 1.9 all_gather.21.refs_0_
  169.3 4.1 %factor.6 = (f32[128,128]{1,0:T(8,128)}, bf16[384,128]{1,0:T(8,128)(2,1)S(1)}) custom-call(f32[32,128]{1,0:T(8,128)} %all_gather.21.refs_0_, f32[128,128]{1,0:T(8,128)} %get-tuple-element.56.refs_1_), custom_call_target="tpu_custom_call" | custom-call | flops 100000000 | bytes 1048576 | tf_op jit(solution)/shard_map/factor/pallas_call | solution.py:440
  176.5 17.0 %all_to_all.89.refs_0_ = bf16[32,48,128]{2,1,0:T(8,128)(2,1)S(1)} all-to-all(bf16[32,48,128]{2,1,0:T(8,128)(2,1)S(1)} %forward.3), channel_id=1, replica_groups={{0,4,8,12,16,20,24,28,1,5,9,13,17,21,25,29,2,6,10,14,18,22,26,30,3,7,11..., dimensions={0} | all-to-all | bytes 786432 | tf_op jit(solution)/shard_map/all_to_all | solution.py:392
  194.3 7.6 %all-to-all-start.10 = ((bf16[32,32,128]{2,1,0:T(8,128)(2,1)}), bf16[32,32,128]{2,1,0:T(8,128)(2,1)S(1)}, u32[]{:S(2)}, u32[]{:S(2)}) async-start(bf16[32,32,128]{2,1,0:T(8,128)(2,1)} %get-tuple-element.58), calls=%async_computation.10 | async-start | bytes 524288 | tf_op jit(solution)/shard_map/all_to_all | solution.py:392
  201.8 3.0 %all_gather.22.refs_0_ = f32[32,128]{1,0:T(8,128)} all-gather(f32[16,128]{1,0:T(8,128)S(1)} %copy-done.10), channel_id=1, replica_groups={{0,32},{64,96},{128,160},{192,224},{256,288},{320,352},{384,416},{448,4..., dimensions={0}, use_global_device_ids=true | all-gather | bytes 24576 | tf_op jit(solution)/shard_map/all_gather | solution.py:460
  204.9 4.1 %factor.7 = (f32[128,128]{1,0:T(8,128)}, bf16[384,128]{1,0:T(8,128)(2,1)S(1)}) custom-call(f32[32,128]{1,0:T(8,128)} %all_gather.22.refs_0_, f32[128,128]{1,0:T(8,128)} %get-tuple-element.60.refs_1_), custom_call_target="tpu_custom_call" | custom-call | flops 100000000 | bytes 1048576 | tf_op jit(solution)/shard_map/factor/pallas_call | solution.py:440
  209.0 5.2 %all-to-all-done.10.refs_1_ = bf16[32,32,128]{2,1,0:T(8,128)(2,1)S(1)} async-done(((bf16[32,32,128]{2,1,0:T(8,128)(2,1)}), bf16[32,32,128]{2,1,0:T(8,128)(2,1)S(1)}, u32[]{:S(2)}, u32[]{:S(2)}) %all-to-all-start.10) | async-done | bytes 262176 | tf_op jit(solution)/shard_map/all_to_all | solution.py:392
  214.1 2.3 backward.3
  216.4 16.2 %all_to_all.90.refs_0_ = bf16[16,96,128]{2,1,0:T(8,128)(2,1)S(1)} all-to-all(bf16[16,96,128]{2,1,0:T(8,128)(2,1)S(1)} %backward.3), channel_id=1, replica_groups=mesh['group'=16,'loop'=32] {'group'}, dimensions={0} | all-to-all | bytes 786432 | tf_op jit(solution)/shard_map/all_to_all | solution.py:392
  233.8 4.6 %all-to-all-start.12 = ((f32[16,32,128]{2,1,0:T(8,128)}), f32[16,32,128]{2,1,0:T(8,128)S(1)}, u32[]{:S(2)}, u32[]{:S(2)}) async-start(f32[16,32,128]{2,1,0:T(8,128)} %get-tuple-element.63), calls=%async_computation.12 | async-start | bytes 524288 | tf_op jit(solution)/shard_map/all_to_all | solution.py:392
  238.4 2.0 all_gather.23.gram
  240.4 4.3 %factor_last.1 = (f32[128,128]{1,0:T(8,128)S(1)}, f32[64,128]{1,0:T(8,128)S(1)}, f32[64,64]{1,0:T(8,128)}) custom-call(f32[64,128]{1,0:T(8,128)} %all_gather.23.gram, f32[64,128]{1,0:T(8,128)S(1)} %get-tuple-element.65.session, f32[32,128]{1,0:T(8,128)S(1)} %get-tuple-element.66.attendee, f32[128,128]{1,0:T(8,128)S(1)} %copy-done.1), custom_call_target="tpu_custom_call" | custom-call | flops 100000000 | bytes 1048576 | tf_op jit(solution)/shard_map/factor_last/pallas_call | solution.py:528
  246.3 17.0 %all_to_all.91.received = bf16[32,48,128]{2,1,0:T(8,128)(2,1)S(1)} all-to-all(bf16[32,48,128]{2,1,0:T(8,128)(2,1)S(1)} %gram_last.1), channel_id=1, replica_groups={{0,4,8,12,16,20,24,28,1,5,9,13,17,21,25,29,2,6,10,14,18,22,26,30,3,7,11..., dimensions={0} | all-to-all | bytes 786432 | tf_op jit(solution)/shard_map/all_to_all | solution.py:392
  263.2 3.2 %session_out.1 = f32[64,128]{1,0:T(8,128)} custom-call(bf16[32,48,128]{2,1,0:T(8,128)(2,1)S(1)} %all_to_all.91.received, f32[64,128]{1,0:T(8,128)S(1)} %get-tuple-element.68.panel), custom_call_target="tpu_custom_call" | custom-call | flops 100000000 | bytes 1048576 | tf_op jit(solution)/shard_map/session_out/pallas_call | solution.py:540
  (48 shorter events, 19.3 us)
Async XLA Ops:
  0.6 12.5 %copy-start = (bf16[1,1,32,128,128]{4,3,2,1,0:T(8,128)(2,1)S(1)}, bf16[1,1,32,128,128]{4,3,2,1,0:T(8,128)(2,1)}, u32[]{:S(2)}) copy-start(bf16[1,1,32,128,128]{4,3,2,1,0:T(8,128)(2,1)} %param.5) | copy-start | bytes 3145732
  1.4 0.7 copy-start.5
  2.0 0.7 copy-start.7
  5.6 13.2 %all-to-all-start = ((f32[8,80,128]{2,1,0:T(8,128)}), f32[8,80,128]{2,1,0:T(8,128)}, u32[]{:S(2)}, u32[]{:S(2)}) async-start(f32[8,80,128]{2,1,0:T(8,128)} %get-tuple-element.36), calls=%async_computation | async-start | bytes 655360 | tf_op jit(solution)/shard_map/all_to_all | solution.py:392
  12.4 0.7 copy-start.6
  12.4 0.7 copy-start.8
  28.0 64.2 %copy-start.2 = (f32[64,128]{1,0:T(8,128)}, f32[64,128]{1,0:T(8,128)S(1)}, u32[]{:S(2)}) copy-start(f32[64,128]{1,0:T(8,128)S(1)} %get-tuple-element.43.refs_1_) | copy-start | bytes 98308
  93.0 4.6 %copy-start.11 = (f32[16,128]{1,0:T(8,128)S(1)}, f32[16,128]{1,0:T(8,128)}, u32[]{:S(2)}) copy-start(f32[16,128]{1,0:T(8,128)} %get-tuple-element.46) | copy-start | bytes 24580
  93.0 11.8 %all-to-all-start.4 = ((bf16[16,64,128]{2,1,0:T(8,128)(2,1)}), bf16[16,64,128]{2,1,0:T(8,128)(2,1)S(1)}, u32[]{:S(2)}, u32[]{:S(2)}) async-start(bf16[16,64,128]{2,1,0:T(8,128)(2,1)} %get-tuple-element.44), calls=%async_computation.4 | async-start | bytes 524288 | tf_op jit(solution)/shard_map/all_to_all | solution.py:392
  125.2 7.6 %copy-start.12 = (f32[16,128]{1,0:T(8,128)S(1)}, f32[16,128]{1,0:T(8,128)}, u32[]{:S(2)}) copy-start(f32[16,128]{1,0:T(8,128)} %get-tuple-element.51) | copy-start | bytes 24580
  125.2 19.9 %all-to-all-start.6 = ((bf16[32,32,128]{2,1,0:T(8,128)(2,1)}), bf16[32,32,128]{2,1,0:T(8,128)(2,1)S(1)}, u32[]{:S(2)}, u32[]{:S(2)}) async-start(bf16[32,32,128]{2,1,0:T(8,128)(2,1)} %get-tuple-element.49), calls=%async_computation.6 | async-start | bytes 524288 | tf_op jit(solution)/shard_map/all_to_all | solution.py:392
  146.9 14.9 %copy-start.3 = (f32[64,128]{1,0:T(8,128)S(1)}, f32[64,128]{1,0:T(8,128)}, u32[]{:S(2)}) copy-start(f32[64,128]{1,0:T(8,128)} %copy-done.2) | copy-start | bytes 98308
  162.6 4.8 %copy-start.13 = (f32[16,128]{1,0:T(8,128)S(1)}, f32[16,128]{1,0:T(8,128)}, u32[]{:S(2)}) copy-start(f32[16,128]{1,0:T(8,128)} %get-tuple-element.55) | copy-start | bytes 24580
  162.6 12.0 %all-to-all-start.8 = ((bf16[16,64,128]{2,1,0:T(8,128)(2,1)}), bf16[16,64,128]{2,1,0:T(8,128)(2,1)S(1)}, u32[]{:S(2)}, u32[]{:S(2)}) async-start(bf16[16,64,128]{2,1,0:T(8,128)(2,1)} %get-tuple-element.54), calls=%async_computation.8 | async-start | bytes 524288 | tf_op jit(solution)/shard_map/all_to_all | solution.py:392
  194.3 7.6 %copy-start.10 = (f32[16,128]{1,0:T(8,128)S(1)}, f32[16,128]{1,0:T(8,128)}, u32[]{:S(2)}) copy-start(f32[16,128]{1,0:T(8,128)} %get-tuple-element.59) | copy-start | bytes 24580
  194.3 19.9 %all-to-all-start.10 = ((bf16[32,32,128]{2,1,0:T(8,128)(2,1)}), bf16[32,32,128]{2,1,0:T(8,128)(2,1)S(1)}, u32[]{:S(2)}, u32[]{:S(2)}) async-start(bf16[32,32,128]{2,1,0:T(8,128)(2,1)} %get-tuple-element.58), calls=%async_computation.10 | async-start | bytes 524288 | tf_op jit(solution)/shard_map/all_to_all | solution.py:392
  216.4 16.2 %copy-start.4 = (f32[64,128]{1,0:T(8,128)S(1)}, f32[64,128]{1,0:T(8,128)}, u32[]{:S(2)}) copy-start(f32[64,128]{1,0:T(8,128)} %copy-done.2) | copy-start | bytes 98308
  233.8 4.6 %copy-start.9 = (f32[32,128]{1,0:T(8,128)S(1)}, f32[32,128]{1,0:T(8,128)}, u32[]{:S(2)}) copy-start(f32[32,128]{1,0:T(8,128)} %get-tuple-element.64) | copy-start | bytes 49156
  233.8 6.6 %copy-start.1 = (f32[128,128]{1,0:T(8,128)S(1)}, f32[128,128]{1,0:T(8,128)}, u32[]{:S(2)}) copy-start(f32[128,128]{1,0:T(8,128)} %get-tuple-element.62.refs_5_.attendee_factor) | copy-start | bytes 196612
  233.8 11.8 %all-to-all-start.12 = ((f32[16,32,128]{2,1,0:T(8,128)}), f32[16,32,128]{2,1,0:T(8,128)S(1)}, u32[]{:S(2)}, u32[]{:S(2)}) async-start(f32[16,32,128]{2,1,0:T(8,128)} %get-tuple-element.63), calls=%async_computation.12 | async-start | bytes 524288 | tf_op jit(solution)/shard_map/all_to_all | solution.py:392

commit v4 on v3

--- a/solution.py
+++ b/solution.py
@@ -124,7 +124,28 @@
     return jnp.concatenate([high, high, low], axis=0).astype(BF16)
 
 
-def apply_to_gram(gram, inverse):
+def apply_parts(panel, parts):
+    high, low = split_two(panel)
+    mixed = jnp.concatenate([high, low, high], axis=1).astype(BF16)
+    return jnp.dot(mixed, parts, preferred_element_type=F32)
+
+
+def inverse_from_parts(parts):
+    return (parts[:WIDTH, :WIDTH].astype(F32) + parts[2 * LANES :][:WIDTH, :WIDTH].astype(F32)).T
+
+
+def dot_parts(left, right):
+    (left_high, left_low), (right_high, right_low) = split_two(left), split_two(right)
+    return jnp.dot(
+        jnp.concatenate([left_high, left_low, left_high], axis=1).astype(BF16),
+        jnp.concatenate([right_high, right_high, right_low], axis=0).astype(BF16),
+        preferred_element_type=F32,
+    )
+
+
+def apply_to_gram(gram, inverse, exact=True):
+    if not exact:
+        return dot_parts(dot_parts(inverse, gram), inverse.T)
     turned = jnp.dot(inverse, gram, precision=HIGHEST, preferred_element_type=F32)
     return times_transposed(turned, inverse)
 
@@ -153,34 +174,31 @@
     return jnp.where(on_diagonal, whole, square + square.T)
 
 
-def degree_kernel(count, row_at, col_at, values, start, copies, row_degree, col_sum, row_sum):
-    n_blocks = row_degree.shape[0]
-    col_sum[...] = jnp.zeros_like(col_sum)
-    row_sum[...] = jnp.zeros_like(row_sum)
+def sum_per_block(target, sums, n_blocks):
+    shape = (n_blocks, sums.shape[0])
+    chosen = jnp.where(iota(shape, 0) == target, 1.0, 0.0)
+    return jnp.dot(chosen, sums, precision=HIGHEST, preferred_element_type=F32)
+
+
+def degree_kernel(index, values, start, copies):
+    slots, half = values.shape[0], start.shape[1] // 2
+    sums = [jnp.sum(values[t].astype(F32), axis=0, keepdims=True) for t in range(slots)]
+    sums = jnp.concatenate(sums, axis=0)
+    degree = sum_per_block(index[3:4, :slots], sums, copies.shape[1] - half)
+    message = jnp.concatenate([rows_to_halves(start[...].T), degree], axis=0)
+    for d in range(copies.shape[0]):
+        copies[d] = message
+
+
+def layout_kernel(row_half, col_half, index, values, forward, backward, row_degree, row_sum):
     ones = jnp.ones((8, SIDE), BF16)
-    for t in range(values.shape[0]):
-        tile = values[t]
-        alive = t < count[0]
-        col_sum[jnp.where(alive, col_at[t], n_blocks)] += jnp.dot(
-            ones, tile, preferred_element_type=F32
-        )
-        row_sum[jnp.where(alive, row_at[t], n_blocks)] += lax.dot_general(
-            ones, tile, (((1,), (1,)), ((), ())), preferred_element_type=F32
-        )
-    for b in range(n_blocks):
-        row_degree[b : b + 1] = row_sum[b, :1]
-    panel = rows_to_halves(start[...].T)
-    degree = jnp.concatenate([col_sum[b, :1] for b in range(n_blocks)], axis=0)
-    for d in range(copies.shape[0]):
-        copies[d, : panel.shape[0]] = panel
-        copies[d, panel.shape[0] :] = degree
-
-
-def layout_kernel(row_half, col_half, values, forward, backward):
     half = SIDE // 2
     slabs = [slice(at, at + row_half) for at in range(0, SIDE, row_half)]
     for t in range(values.shape[0]):
         tile = values[t]
+        row_sum[t : t + 1] = lax.dot_general(
+            ones, tile, (((1,), (1,)), ((), ())), preferred_element_type=F32
+        )[:1]
         for at in range(0, half, row_half):
             forward[t, at : at + row_half, :SIDE] = tile[2 * at : 2 * at + row_half]
             forward[t, at : at + row_half, SIDE:] = tile[2 * at + row_half : 2 * at + 2 * row_half]
@@ -189,6 +207,8 @@
         for at in range(0, half, col_half):
             backward[t, at : at + col_half, :SIDE] = turned[2 * at : 2 * at + col_half]
             backward[t, at : at + col_half, SIDE:] = turned[2 * at + col_half : 2 * at + 2 * col_half]
+    slots = values.shape[0]
+    row_degree[...] = sum_per_block(index[2:3, :slots], row_sum[...], row_degree.shape[0])
 
 
 def product_kernel(kind, source, target, rows_from, n_to, rows_to, whole, from_pair, *refs):
@@ -197,8 +217,6 @@
         row_degree, out, weight, own_scale = refs
     elif kind == "degree":
         out, weight = refs
-    elif whole:
-        weight, factor, pending, out = refs
     else:
         weight, factor, out = refs
     half = SIDE // 2
@@ -259,8 +277,8 @@
         at = iota((DEGREE_ROWS, LANES), 0)
     else:
         gram = diagonal_blocks(grams[:LANES]) + diagonal_blocks(grams[LANES:])
-        if whole:
-            gram = apply_to_gram(gram, pending[:WIDTH, :WIDTH])
+        if kind == "plain":
+            gram = apply_to_gram(gram, inverse_from_parts(factor[...]), exact=whole)
         message = gram_to_message(gram, whole)
         halves = [message[:16], message[16:32]]
         if whole:
@@ -274,9 +292,7 @@
     for b in range(n_blocks):
         product = total[b]
         if kind == "plain":
-            high, low = split_two(product)
-            mixed = jnp.concatenate([high, low, high], axis=1).astype(BF16)
-            product = jnp.dot(mixed, factor[...], preferred_element_type=F32)
+            product = apply_parts(product, factor[...])
         product = product.astype(BF16)
         for j in range(to_block):
             d = LOOP_PLACE[b * to_block + j] if to_block > 1 else b
@@ -326,21 +342,16 @@
             copies[d, rows:] = tail
 
 
-def factor_kernel(*refs):
-    gram_ref, *pending, factor, parts = refs
-    gram = message_to_gram(gram_ref[...])
-    if pending:
-        gram = apply_to_gram(gram, pending[0][:WIDTH, :WIDTH])
-    both = both_halves(inverse_factor(gram))
-    factor[...] = both
-    parts[...] = factor_parts(both)
-
-
-def factor_last_kernel(gram, session, attendee, attendee_factor, factor, session_out, attendee_out):
-    both = both_halves(inverse_factor(message_to_gram(gram[...])))
-    factor[...] = both
+def factor_kernel(gram, parts):
+    parts[...] = factor_parts(both_halves(inverse_factor(message_to_gram(gram[...]))))
+
+
+def factor_last_kernel(gram, session, attendee, attendee_parts, factor, session_out, attendee_out):
+    inverse = inverse_factor(message_to_gram(gram[...]))
+    factor[...] = inverse
+    both = both_halves(inverse)
     session_out[...] = times_transposed(session[...], both)
-    turned = times_transposed(attendee[...], attendee_factor[...])
+    turned = apply_parts(attendee[...], attendee_parts[...])
     attendee_out[...] = halves_to_rows(times_transposed(turned, both))
 
 
@@ -348,7 +359,7 @@
     summed = received[0]
     for s in range(1, n_from):
         summed = summed + received[s]
-    gram = apply_to_gram(halves_to_rows(summed), factor[:WIDTH, :WIDTH])
+    gram = apply_to_gram(halves_to_rows(summed), factor[...])
     message = gram_to_message(gram, True)
     for d in range(n_copies):
         copies[d] = message
@@ -409,41 +420,40 @@
     half = SIDE // 2
     count, row_at, col_at = tile_count[0], tile_rows[0, 0], tile_cols[0, 0]
 
-    first, row_degree = call(
-        degree_kernel,
-        "degrees",
-        [SMEM, SMEM, SMEM, VMEM, VMEM],
-        [((n_group // 2, col_half + col_blocks, LANES), F32), ((row_blocks, SIDE), F32)],
-        [pltpu.VMEM((col_blocks + 1, 8, SIDE), F32), pltpu.VMEM((row_blocks + 1, 8, SIDE), F32)],
-    )(count, row_at, col_at, *from_hbm(values, start_panel[0].T))
-    pairs = [[i, i + 1] for i in range(0, n_group, 2)]
-    gathered = exchange(first, "group", [list(range(core, n_group, 2)) for core in range(2)])
-    gathered = lax.all_gather(gathered, "group", axis_index_groups=pairs, axis=0, tiled=True)
-    forward, backward = call(
-        functools.partial(layout_kernel, row_half, col_half),
-        "layouts",
-        [VMEM],
-        [((slots, half, 2 * SIDE), BF16), ((slots, half, 2 * SIDE), BF16)],
-    )(values)
-
     alive = jnp.arange(slots) < count
     group = lax.axis_index("group")
     index = [row_at, col_at, jnp.where(alive, row_at, row_blocks)]
     index += [jnp.where(alive, col_at, col_blocks), jnp.pad(jnp.stack([group, group % 2]), (0, slots - 2))]
     index = jnp.pad(jnp.stack(index).astype(jnp.int32), ((0, 3), (0, LANES - slots)))
+    (first,) = call(
+        degree_kernel,
+        "start_message",
+        [VMEM] * 3,
+        [((n_group // 2, col_half + col_blocks, LANES), F32)],
+        in_hbm=(0,),
+    )(index, *from_hbm(values, start_panel[0].T))
+    pairs = [[i, i + 1] for i in range(0, n_group, 2)]
+    gathered = exchange(first, "group", [list(range(core, n_group, 2)) for core in range(2)])
+    gathered = lax.all_gather(gathered, "group", axis_index_groups=pairs, axis=0, tiled=True)
+    forward, backward, row_degree = call(
+        functools.partial(layout_kernel, row_half, col_half),
+        "layouts",
+        [VMEM] * 2,
+        [
+            ((slots, half, 2 * SIDE), BF16),
+            ((slots, half, 2 * SIDE), BF16),
+            ((row_blocks, SIDE), F32),
+        ],
+        [pltpu.VMEM((slots, SIDE), F32)],
+    )(index, values)
+
     scratch = [
         pltpu.VMEM((col_blocks, 2 * SIDE, LANES), BF16),
         pltpu.VMEM((row_blocks + 1, half, LANES), F32),
     ]
 
-    def factor_of(*args):
-        return call(
-            factor_kernel,
-            "factor",
-            [VMEM] * len(args),
-            [((LANES, LANES), F32), ((3 * LANES, LANES), BF16)],
-            in_hbm=(0,),
-        )(*from_hbm(*args))
+    def factor_of(gram):
+        return call(factor_kernel, "factor", [VMEM], [((3 * LANES, LANES), BF16)])(gram)[0]
 
     def products(kind, way, whole, rows_from, n_to, rows_to, name, extra_rows, args, others=()):
         return call(
@@ -497,7 +507,7 @@
                 [((n_loop, row_half, LANES), BF16), panel_rows, ((16, LANES), F32)],
                 in_hbm=(0, 2),
             )(received, row_scale)
-            row_factor, row_parts = factor_of(swap_cores(gram), col_factor)
+            row_parts = factor_of(swap_cores(gram))
         gathered = exchange(copies, "loop")
         args = (gathered, backward)
         to = (row_half, n_group, col_half)
@@ -508,8 +518,6 @@
             )
         else:
             args = (*args, row_weight, row_parts)
-            if last:
-                args = (*args, *from_hbm(row_factor))
             (outgoing,) = products("plain", (0, 3), last, *to, "backward", message_rows, args)
         received = exchange(outgoing, "group")
         message = ((n_group, WIDTH // 2, LANES), F32) if last else ((n_group, col_half, LANES), BF16)
@@ -521,16 +529,14 @@
             in_hbm=(0, 2),
         )(received, col_scale)
         gathered = exchange(copies, "group")
-        if iteration == 0:
-            col_factor, col_parts = factor_of(swap_cores(gram))
-        elif not last:
-            col_factor, col_parts = factor_of(swap_cores(gram), row_factor)
+        if not last:
+            col_parts = factor_of(swap_cores(gram))
     col_factor, session, attendee = call(
         factor_last_kernel,
         "factor_last",
         [VMEM] * 4,
-        [((LANES, LANES), F32), panel_cols, ((2 * row_half, WIDTH), F32)],
-    )(*from_hbm(swap_cores(gram)), session, attendee, row_factor)
+        [((WIDTH, WIDTH), F32), panel_cols, ((2 * row_half, WIDTH), F32)],
+    )(swap_cores(gram), session, attendee, row_parts)
     (copies,) = call(
         functools.partial(gram_last_kernel, n_group, n_loop),
         "gram_last",

time: 272 us -> 269 us (0.989)
  waiting for transfers between devices: 19.6 us -> 28.3 us
  Pallas kernels: 44.1 us -> 36.5 us
    all_to_all x6, waiting for transfers between devices: 19.6 us -> 28.3 us  [exchange(): lax.all_to_all(array.reshape(n * rows, lanes), axis, split_axis=0, concat...]
    pallas_call x6, Pallas kernels: 23.1 us -> 14.7 us  [the longest x4 8.98 us: factor_of(): call(factor_kernel, 'factor', [VMEM], [((3 * LANES, LANES), BF16)])(gram)[0]]
  transfers between devices with their start and end apart: 6 -> 6, of which waited for: 6 -> 6; matrix products, arithmetic and copies ran while one was open for 0% -> 0% of each run, Pallas kernels for 8% -> 5%
where the time goes in v4:
time: 269 us; the launch traced here: 265 us
  blocking collectives  162 us (60%)
  Pallas kernels  36.5 us (14%)
  starting transfers between devices  35.8 us (13%)
  waiting for transfers between devices  28.3 us (11%)
    all_to_all x8, blocking collectives, exchange(): lax.all_to_all(array.reshape(n * rows, lanes), axis, split_axis=0, concat...  143 us
    all_to_all x6, starting transfers between devices, exchange(): lax.all_to_all(array.reshape(n * rows, lanes), axis, split_axis=0, concat...  35.8 us
    all_to_all x6, waiting for transfers between devices, exchange(): lax.all_to_all(array.reshape(n * rows, lanes), axis, split_axis=0, concat...  28.3 us
    pallas_call x6, Pallas kernels, products(): call(functools.partial(product_kernel, kind, *way, rows_from, n_to, rows_...  12.3 us
    all_gather x5, blocking collectives, swap_cores(): lax.all_gather(half_message, 'group', axis_index_groups=pairs, axis=0, ti...  11.3 us
    pallas_call x4, Pallas kernels, factor_of(): call(factor_kernel, 'factor', [VMEM], [((3 * LANES, LANES), BF16)])(gram)[0]  8.98 us
    all_gather x1, blocking collectives, per_device(): lax.all_gather(gathered, 'group', axis_index_groups=pairs, axis=0, tiled=...  7.47 us
  transfers between devices with their start and end apart: 6, of which 6 were waited for; matrix products, arithmetic and copies ran while one was open for 0% of the time, Pallas kernels for 5%

profile of v4, /device:TPU:1, one launch (start us, length us, event | category | flops | bytes accessed | tf_op | source)
XLA Modules:
  0.0 264.7 jit_solution(17811324393869116495)
XLA Ops:
  2.1 2.3 start_message.1
  4.4 6.7 %all-to-all-start = ((f32[8,80,128]{2,1,0:T(8,128)}), f32[8,80,128]{2,1,0:T(8,128)}, u32[]{:S(2)}, u32[]{:S(2)}) async-start(f32[8,80,128]{2,1,0:T(8,128)} %start_message.1), calls=%async_computation | async-start | bytes 655360 | tf_op jit(solution)/shard_map/all_to_all | solution.py:403
  11.9 5.8 %all-to-all-done = f32[8,80,128]{2,1,0:T(8,128)} async-done(((f32[8,80,128]{2,1,0:T(8,128)}), f32[8,80,128]{2,1,0:T(8,128)}, u32[]{:S(2)}, u32[]{:S(2)}) %all-to-all-start) | async-done | bytes 327712 | tf_op jit(solution)/shard_map/all_to_all | solution.py:403
  17.7 7.5 %all_gather.18.refs_1_ = f32[16,80,128]{2,1,0:T(8,128)S(1)} all-gather(f32[8,80,128]{2,1,0:T(8,128)} %all-to-all-done), channel_id=1, replica_groups={{0,32},{64,96},{128,160},{192,224},{256,288},{320,352},{384,416},{448,4..., dimensions={0}, use_global_device_ids=true | all-gather | bytes 983040 | tf_op jit(solution)/shard_map/all_gather | solution.py:437
  26.8 26.2 %all_to_all.84.refs_0_ = bf16[32,48,128]{2,1,0:T(8,128)(2,1)S(1)} all-to-all(bf16[32,48,128]{2,1,0:T(8,128)(2,1)S(1)} %get-tuple-element.29), channel_id=1, replica_groups={{0,4,8,12,16,20,24,28,1,5,9,13,17,21,25,29,2,6,10,14,18,22,26,30,3,7,11..., dimensions={0} | all-to-all | bytes 786432 | tf_op jit(solution)/shard_map/all_to_all | solution.py:403
  53.8 19.7 %all_to_all.85.refs_1_ = bf16[32,48,128]{2,1,0:T(8,128)(2,1)S(1)} all-to-all(bf16[32,48,128]{2,1,0:T(8,128)(2,1)S(1)} %get-tuple-element.30), channel_id=1, replica_groups={{0,4,8,12,16,20,24,28,1,5,9,13,17,21,25,29,2,6,10,14,18,22,26,30,3,7,11..., dimensions={0} | all-to-all | bytes 786432 | tf_op jit(solution)/shard_map/all_to_all | solution.py:403
  73.5 2.3 backward_start.1
  75.8 15.2 %all_to_all.86.refs_0_ = bf16[16,80,128]{2,1,0:T(8,128)(2,1)S(1)} all-to-all(bf16[16,80,128]{2,1,0:T(8,128)(2,1)S(1)} %get-tuple-element.32), channel_id=1, replica_groups=mesh['group'=16,'loop'=32] {'group'}, dimensions={0} | all-to-all | bytes 655360 | tf_op jit(solution)/shard_map/all_to_all | solution.py:403
  91.7 4.6 %all-to-all-start.4 = ((bf16[16,64,128]{2,1,0:T(8,128)(2,1)}), bf16[16,64,128]{2,1,0:T(8,128)(2,1)S(1)}, u32[]{:S(2)}, u32[]{:S(2)}) async-start(bf16[16,64,128]{2,1,0:T(8,128)(2,1)} %get-tuple-element.34), calls=%async_computation.4 | async-start | bytes 524288 | tf_op jit(solution)/shard_map/all_to_all | solution.py:403
  98.2 2.2 factor.4.refs_4_
  100.4 3.2 %all-to-all-done.4.refs_1_ = bf16[16,64,128]{2,1,0:T(8,128)(2,1)S(1)} async-done(((bf16[16,64,128]{2,1,0:T(8,128)(2,1)}), bf16[16,64,128]{2,1,0:T(8,128)(2,1)S(1)}, u32[]{:S(2)}, u32[]{:S(2)}) %all-to-all-start.4) | async-done | bytes 262176 | tf_op jit(solution)/shard_map/all_to_all | solution.py:403
  103.6 2.1 forward.2
  105.7 17.7 %all_to_all.87.refs_0_ = bf16[32,48,128]{2,1,0:T(8,128)(2,1)S(1)} all-to-all(bf16[32,48,128]{2,1,0:T(8,128)(2,1)S(1)} %forward.2), channel_id=1, replica_groups={{0,4,8,12,16,20,24,28,1,5,9,13,17,21,25,29,2,6,10,14,18,22,26,30,3,7,11..., dimensions={0} | all-to-all | bytes 786432 | tf_op jit(solution)/shard_map/all_to_all | solution.py:403
  124.2 7.6 %all-to-all-start.6 = ((bf16[32,32,128]{2,1,0:T(8,128)(2,1)}), bf16[32,32,128]{2,1,0:T(8,128)(2,1)S(1)}, u32[]{:S(2)}, u32[]{:S(2)}) async-start(bf16[32,32,128]{2,1,0:T(8,128)(2,1)} %get-tuple-element.38), calls=%async_computation.6 | async-start | bytes 524288 | tf_op jit(solution)/shard_map/all_to_all | solution.py:403
  131.7 2.9 %all_gather.20.gram = f32[32,128]{1,0:T(8,128)S(1)} all-gather(f32[16,128]{1,0:T(8,128)S(1)} %copy-done.7), channel_id=1, replica_groups={{0,32},{64,96},{128,160},{192,224},{256,288},{320,352},{384,416},{448,4..., dimensions={0}, use_global_device_ids=true | all-gather | bytes 24576 | tf_op jit(solution)/shard_map/all_gather | solution.py:470
  134.6 2.2 factor.5.refs_4_
  136.9 7.2 %all-to-all-done.6.refs_1_ = bf16[32,32,128]{2,1,0:T(8,128)(2,1)S(1)} async-done(((bf16[32,32,128]{2,1,0:T(8,128)(2,1)}), bf16[32,32,128]{2,1,0:T(8,128)(2,1)S(1)}, u32[]{:S(2)}, u32[]{:S(2)}) %all-to-all-start.6) | async-done | bytes 262176 | tf_op jit(solution)/shard_map/all_to_all | solution.py:403
  144.0 2.1 backward.2
  146.2 14.7 %all_to_all.88.refs_0_ = bf16[16,80,128]{2,1,0:T(8,128)(2,1)S(1)} all-to-all(bf16[16,80,128]{2,1,0:T(8,128)(2,1)S(1)} %backward.2), channel_id=1, replica_groups=mesh['group'=16,'loop'=32] {'group'}, dimensions={0} | all-to-all | bytes 655360 | tf_op jit(solution)/shard_map/all_to_all | solution.py:403
  161.7 4.8 %all-to-all-start.8 = ((bf16[16,64,128]{2,1,0:T(8,128)(2,1)}), bf16[16,64,128]{2,1,0:T(8,128)(2,1)S(1)}, u32[]{:S(2)}, u32[]{:S(2)}) async-start(bf16[16,64,128]{2,1,0:T(8,128)(2,1)} %get-tuple-element.41), calls=%async_computation.8 | async-start | bytes 524288 | tf_op jit(solution)/shard_map/all_to_all | solution.py:403
  168.3 2.2 factor.6.refs_4_
  170.5 3.2 %all-to-all-done.8.refs_1_ = bf16[16,64,128]{2,1,0:T(8,128)(2,1)S(1)} async-done(((bf16[16,64,128]{2,1,0:T(8,128)(2,1)}), bf16[16,64,128]{2,1,0:T(8,128)(2,1)S(1)}, u32[]{:S(2)}, u32[]{:S(2)}) %all-to-all-start.8) | async-done | bytes 262176 | tf_op jit(solution)/shard_map/all_to_all | solution.py:403
  175.8 17.0 %all_to_all.89.refs_0_ = bf16[32,48,128]{2,1,0:T(8,128)(2,1)S(1)} all-to-all(bf16[32,48,128]{2,1,0:T(8,128)(2,1)S(1)} %forward.3), channel_id=1, replica_groups={{0,4,8,12,16,20,24,28,1,5,9,13,17,21,25,29,2,6,10,14,18,22,26,30,3,7,11..., dimensions={0} | all-to-all | bytes 786432 | tf_op jit(solution)/shard_map/all_to_all | solution.py:403
  193.6 7.6 %all-to-all-start.10 = ((bf16[32,32,128]{2,1,0:T(8,128)(2,1)}), bf16[32,32,128]{2,1,0:T(8,128)(2,1)S(1)}, u32[]{:S(2)}, u32[]{:S(2)}) async-start(bf16[32,32,128]{2,1,0:T(8,128)(2,1)} %get-tuple-element.43), calls=%async_computation.10 | async-start | bytes 524288 | tf_op jit(solution)/shard_map/all_to_all | solution.py:403
  201.1 2.9 %all_gather.22.gram = f32[32,128]{1,0:T(8,128)S(1)} all-gather(f32[16,128]{1,0:T(8,128)S(1)} %copy-done.5), channel_id=1, replica_groups={{0,32},{64,96},{128,160},{192,224},{256,288},{320,352},{384,416},{448,4..., dimensions={0}, use_global_device_ids=true | all-gather | bytes 24576 | tf_op jit(solution)/shard_map/all_gather | solution.py:470
  204.0 2.2 factor.7.refs_4_.attendee_parts
  206.3 7.1 %all-to-all-done.10.refs_1_ = bf16[32,32,128]{2,1,0:T(8,128)(2,1)S(1)} async-done(((bf16[32,32,128]{2,1,0:T(8,128)(2,1)}), bf16[32,32,128]{2,1,0:T(8,128)(2,1)S(1)}, u32[]{:S(2)}, u32[]{:S(2)}) %all-to-all-start.10) | async-done | bytes 262176 | tf_op jit(solution)/shard_map/all_to_all | solution.py:403
  215.5 15.4 %all_to_all.90.refs_0_ = bf16[16,96,128]{2,1,0:T(8,128)(2,1)S(1)} all-to-all(bf16[16,96,128]{2,1,0:T(8,128)(2,1)S(1)} %backward.3), channel_id=1, replica_groups=mesh['group'=16,'loop'=32] {'group'}, dimensions={0} | all-to-all | bytes 786432 | tf_op jit(solution)/shard_map/all_to_all | solution.py:403
  232.1 4.6 %all-to-all-start.12 = ((f32[16,32,128]{2,1,0:T(8,128)}), f32[16,32,128]{2,1,0:T(8,128)S(1)}, u32[]{:S(2)}, u32[]{:S(2)}) async-start(f32[16,32,128]{2,1,0:T(8,128)} %get-tuple-element.45), calls=%async_computation.12 | async-start | bytes 524288 | tf_op jit(solution)/shard_map/all_to_all | solution.py:403
  238.6 3.4 %factor_last.1 = (f32[64,64]{1,0:T(8,128)S(1)}, f32[64,128]{1,0:T(8,128)S(1)}, f32[64,64]{1,0:T(8,128)}) custom-call(f32[64,128]{1,0:T(8,128)S(1)} %all_gather.23.gram, f32[64,128]{1,0:T(8,128)S(1)} %get-tuple-element.47.session, f32[32,128]{1,0:T(8,128)S(1)} %get-tuple-element.48.attendee, bf16[384,128]{1,0:T(8,128)(2,1)S(1)} %factor.7.refs_4_.attendee_parts), custom_call_target="tpu_custom_call" | custom-call | flops 100000000 | bytes 1048576 | tf_op jit(solution)/shard_map/factor_last/pallas_call | solution.py:534
  244.6 17.0 %all_to_all.91.received = bf16[32,48,128]{2,1,0:T(8,128)(2,1)S(1)} all-to-all(bf16[32,48,128]{2,1,0:T(8,128)(2,1)S(1)} %gram_last.1), channel_id=1, replica_groups={{0,4,8,12,16,20,24,28,1,5,9,13,17,21,25,29,2,6,10,14,18,22,26,30,3,7,11..., dimensions={0} | all-to-all | bytes 786432 | tf_op jit(solution)/shard_map/all_to_all | solution.py:403
  261.5 3.2 %session_out.1 = f32[64,128]{1,0:T(8,128)} custom-call(bf16[32,48,128]{2,1,0:T(8,128)(2,1)S(1)} %all_to_all.91.received, f32[64,128]{1,0:T(8,128)S(1)} %get-tuple-element.50.panel), custom_call_target="tpu_custom_call" | custom-call | flops 100000000 | bytes 1048576 | tf_op jit(solution)/shard_map/session_out/pallas_call | solution.py:546
  (42 shorter events, 20.4 us)
Async XLA Ops:
  1.4 0.7 copy-start.9
  1.4 0.7 copy-start.10
  2.0 9.0 %copy-start = (bf16[1,1,32,128,128]{4,3,2,1,0:T(8,128)(2,1)S(1)}, bf16[1,1,32,128,128]{4,3,2,1,0:T(8,128)(2,1)}, u32[]{:S(2)}) copy-start(bf16[1,1,32,128,128]{4,3,2,1,0:T(8,128)(2,1)} %param.5) | copy-start | bytes 3145732
  4.4 13.2 %all-to-all-start = ((f32[8,80,128]{2,1,0:T(8,128)}), f32[8,80,128]{2,1,0:T(8,128)}, u32[]{:S(2)}, u32[]{:S(2)}) async-start(f32[8,80,128]{2,1,0:T(8,128)} %start_message.1), calls=%async_computation | async-start | bytes 655360 | tf_op jit(solution)/shard_map/all_to_all | solution.py:403
  26.8 64.2 %copy-start.1 = (f32[64,128]{1,0:T(8,128)}, f32[64,128]{1,0:T(8,128)S(1)}, u32[]{:S(2)}) copy-start(f32[64,128]{1,0:T(8,128)S(1)} %get-tuple-element.33.refs_1_) | copy-start | bytes 98308
  91.7 4.6 %copy-start.6 = (f32[16,128]{1,0:T(8,128)S(1)}, f32[16,128]{1,0:T(8,128)}, u32[]{:S(2)}) copy-start(f32[16,128]{1,0:T(8,128)} %get-tuple-element.36) | copy-start | bytes 24580
  91.7 11.8 %all-to-all-start.4 = ((bf16[16,64,128]{2,1,0:T(8,128)(2,1)}), bf16[16,64,128]{2,1,0:T(8,128)(2,1)S(1)}, u32[]{:S(2)}, u32[]{:S(2)}) async-start(bf16[16,64,128]{2,1,0:T(8,128)(2,1)} %get-tuple-element.34), calls=%async_computation.4 | async-start | bytes 524288 | tf_op jit(solution)/shard_map/all_to_all | solution.py:403
  124.2 7.6 %copy-start.7 = (f32[16,128]{1,0:T(8,128)S(1)}, f32[16,128]{1,0:T(8,128)}, u32[]{:S(2)}) copy-start(f32[16,128]{1,0:T(8,128)} %get-tuple-element.40) | copy-start | bytes 24580
  124.2 19.9 %all-to-all-start.6 = ((bf16[32,32,128]{2,1,0:T(8,128)(2,1)}), bf16[32,32,128]{2,1,0:T(8,128)(2,1)S(1)}, u32[]{:S(2)}, u32[]{:S(2)}) async-start(bf16[32,32,128]{2,1,0:T(8,128)(2,1)} %get-tuple-element.38), calls=%async_computation.6 | async-start | bytes 524288 | tf_op jit(solution)/shard_map/all_to_all | solution.py:403
  146.2 14.8 %copy-start.2 = (f32[64,128]{1,0:T(8,128)S(1)}, f32[64,128]{1,0:T(8,128)}, u32[]{:S(2)}) copy-start(f32[64,128]{1,0:T(8,128)} %copy-done.1) | copy-start | bytes 98308
  161.7 4.8 %copy-start.8 = (f32[16,128]{1,0:T(8,128)S(1)}, f32[16,128]{1,0:T(8,128)}, u32[]{:S(2)}) copy-start(f32[16,128]{1,0:T(8,128)} %get-tuple-element.42) | copy-start | bytes 24580
  161.7 12.0 %all-to-all-start.8 = ((bf16[16,64,128]{2,1,0:T(8,128)(2,1)}), bf16[16,64,128]{2,1,0:T(8,128)(2,1)S(1)}, u32[]{:S(2)}, u32[]{:S(2)}) async-start(bf16[16,64,128]{2,1,0:T(8,128)(2,1)} %get-tuple-element.41), calls=%async_computation.8 | async-start | bytes 524288 | tf_op jit(solution)/shard_map/all_to_all | solution.py:403
  193.6 7.6 %copy-start.5 = (f32[16,128]{1,0:T(8,128)S(1)}, f32[16,128]{1,0:T(8,128)}, u32[]{:S(2)}) copy-start(f32[16,128]{1,0:T(8,128)} %get-tuple-element.44) | copy-start | bytes 24580
  193.6 19.9 %all-to-all-start.10 = ((bf16[32,32,128]{2,1,0:T(8,128)(2,1)}), bf16[32,32,128]{2,1,0:T(8,128)(2,1)S(1)}, u32[]{:S(2)}, u32[]{:S(2)}) async-start(bf16[32,32,128]{2,1,0:T(8,128)(2,1)} %get-tuple-element.43), calls=%async_computation.10 | async-start | bytes 524288 | tf_op jit(solution)/shard_map/all_to_all | solution.py:403
  215.5 15.5 %copy-start.3 = (f32[64,128]{1,0:T(8,128)S(1)}, f32[64,128]{1,0:T(8,128)}, u32[]{:S(2)}) copy-start(f32[64,128]{1,0:T(8,128)} %copy-done.1) | copy-start | bytes 98308
  232.1 4.6 %copy-start.4 = (f32[32,128]{1,0:T(8,128)S(1)}, f32[32,128]{1,0:T(8,128)}, u32[]{:S(2)}) copy-start(f32[32,128]{1,0:T(8,128)} %get-tuple-element.46) | copy-start | bytes 49156
  232.1 11.8 %all-to-all-start.12 = ((f32[16,32,128]{2,1,0:T(8,128)}), f32[16,32,128]{2,1,0:T(8,128)S(1)}, u32[]{:S(2)}, u32[]{:S(2)}) async-start(f32[16,32,128]{2,1,0:T(8,128)} %get-tuple-element.45), calls=%async_computation.12 | async-start | bytes 524288 | tf_op jit(solution)/shard_map/all_to_all | solution.py:403

commit v5 on v4

--- a/solution.py
+++ b/solution.py
@@ -11,7 +11,6 @@
 SIDE = 128
 WIDTH = 64
 LANES = 128
-GRAM_ROWS = 48
 DEGREE_ROWS = 16
 F32 = jnp.float32
 BF16 = jnp.bfloat16
@@ -157,21 +156,14 @@
     mixed = jnp.where(iota(shape, 0) >= iota(shape, 1), high, low.T)
     if not whole:
         mixed = jnp.where(on_diagonal, gram * (1.0 + 2.0**-7), mixed)
-    message = rows_to_halves(mixed)
-    if whole:
-        diagonal = jnp.sum(jnp.where(on_diagonal, low, 0.0), axis=0, keepdims=True)
-        diagonal = jnp.concatenate([diagonal, diagonal], axis=1)
-        message = jnp.concatenate([message, jnp.broadcast_to(diagonal, (16, LANES))], axis=0)
-    return message.astype(BF16)
+    return rows_to_halves(mixed).astype(BF16)
 
 
 def message_to_gram(message):
     shape = (WIDTH, WIDTH)
-    half = message.shape[0] // 2
-    square = halves_to_rows(jnp.concatenate([message[:16], message[half : half + 16]], axis=0))
+    square = halves_to_rows(message)
     on_diagonal = iota(shape, 0) == iota(shape, 1)
-    whole = square if half == 16 else square + message[16:17, :WIDTH]
-    return jnp.where(on_diagonal, whole, square + square.T)
+    return jnp.where(on_diagonal, square, square + square.T)
 
 
 def sum_per_block(target, sums, n_blocks):
@@ -281,8 +273,6 @@
             gram = apply_to_gram(gram, inverse_from_parts(factor[...]), exact=whole)
         message = gram_to_message(gram, whole)
         halves = [message[:16], message[16:32]]
-        if whole:
-            halves = [jnp.concatenate([part, message[32:]], axis=0) for part in halves]
         if from_pair:
             halves = [jnp.where(index[4, 1] == 0, *halves)] * 2
     if kind == "start":
@@ -369,8 +359,7 @@
     summed = received[0].astype(F32)
     for s in range(1, n_from):
         summed = summed + received[s].astype(F32)
-    message = jnp.concatenate([summed[:16], summed[32:], summed[16:]], axis=0)
-    both = both_halves(inverse_factor(message_to_gram(message)))
+    both = both_halves(inverse_factor(message_to_gram(summed)))
     out[...] = halves_to_rows(times_transposed(panel[...], both)).T
 
 
@@ -511,21 +500,20 @@
         gathered = exchange(copies, "loop")
         args = (gathered, backward)
         to = (row_half, n_group, col_half)
-        message_rows = 32 if last else 16
         if iteration == 0:
             outgoing, row_weight = products(
                 "degree", (0, 3), False, *to, "backward_start", 16, args, [((rows_dev // 2, LANES), F32)]
             )
         else:
             args = (*args, row_weight, row_parts)
-            (outgoing,) = products("plain", (0, 3), last, *to, "backward", message_rows, args)
+            (outgoing,) = products("plain", (0, 3), last, *to, "backward", 16, args)
         received = exchange(outgoing, "group")
         message = ((n_group, WIDTH // 2, LANES), F32) if last else ((n_group, col_half, LANES), BF16)
         copies, session, gram = call(
             functools.partial(sum_kernel, "last" if last else "plain", n_group, col_half, n_group),
             "session",
             [VMEM, VMEM],
-            [message, panel_cols, ((message_rows, LANES), F32)],
+            [message, panel_cols, ((16, LANES), F32)],
             in_hbm=(0, 2),
         )(received, col_scale)
         gathered = exchange(copies, "group")
@@ -541,7 +529,7 @@
         functools.partial(gram_last_kernel, n_group, n_loop),
         "gram_last",
         [VMEM, VMEM],
-        [((n_loop, 48, LANES), BF16)],
+        [((n_loop, 32, LANES), BF16)],
     )(gathered, col_factor)
     (session,) = call(
         functools.partial(last_kernel, n_loop),

time: 269 us -> 266 us (0.989)
  no operation moved by 1% of the time
where the time goes in v5:
time: 266 us; the launch traced here: 263 us
  blocking collectives  160 us (60%)
  Pallas kernels  36.5 us (14%)
  starting transfers between devices  35.8 us (13%)
  waiting for transfers between devices  28.4 us (11%)
    all_to_all x8, blocking collectives, exchange(): lax.all_to_all(array.reshape(n * rows, lanes), axis, split_axis=0, concat...  141 us
    all_to_all x6, starting transfers between devices, exchange(): lax.all_to_all(array.reshape(n * rows, lanes), axis, split_axis=0, concat...  35.8 us
    all_to_all x6, waiting for transfers between devices, exchange(): lax.all_to_all(array.reshape(n * rows, lanes), axis, split_axis=0, concat...  28.4 us
    pallas_call x6, Pallas kernels, products(): call(functools.partial(product_kernel, kind, *way, rows_from, n_to, rows_...  12.3 us
    all_gather x5, blocking collectives, swap_cores(): lax.all_gather(half_message, 'group', axis_index_groups=pairs, axis=0, ti...  11.3 us
    pallas_call x4, Pallas kernels, factor_of(): call(factor_kernel, 'factor', [VMEM], [((3 * LANES, LANES), BF16)])(gram)[0]  8.98 us
    all_gather x1, blocking collectives, per_device(): lax.all_gather(gathered, 'group', axis_index_groups=pairs, axis=0, tiled=...  7.47 us
  transfers between devices with their start and end apart: 6, of which 6 were waited for; matrix products, arithmetic and copies ran while one was open for 0% of the time, Pallas kernels for 5%

profile of v5, /device:TPU:1, one launch (start us, length us, event | category | flops | bytes accessed | tf_op | source)
XLA Modules:
  0.0 262.8 jit_solution(16351338110181906030)
XLA Ops:
  2.1 2.3 start_message.1
  4.4 6.7 %all-to-all-start = ((f32[8,80,128]{2,1,0:T(8,128)}), f32[8,80,128]{2,1,0:T(8,128)}, u32[]{:S(2)}, u32[]{:S(2)}) async-start(f32[8,80,128]{2,1,0:T(8,128)} %start_message.1), calls=%async_computation | async-start | bytes 655360 | tf_op jit(solution)/shard_map/all_to_all | solution.py:392
  11.9 5.8 %all-to-all-done = f32[8,80,128]{2,1,0:T(8,128)} async-done(((f32[8,80,128]{2,1,0:T(8,128)}), f32[8,80,128]{2,1,0:T(8,128)}, u32[]{:S(2)}, u32[]{:S(2)}) %all-to-all-start) | async-done | bytes 327712 | tf_op jit(solution)/shard_map/all_to_all | solution.py:392
  17.7 7.5 %all_gather.18.refs_1_ = f32[16,80,128]{2,1,0:T(8,128)S(1)} all-gather(f32[8,80,128]{2,1,0:T(8,128)} %all-to-all-done), channel_id=1, replica_groups={{0,32},{64,96},{128,160},{192,224},{256,288},{320,352},{384,416},{448,4..., dimensions={0}, use_global_device_ids=true | all-gather | bytes 983040 | tf_op jit(solution)/shard_map/all_gather | solution.py:426
  26.8 26.3 %all_to_all.84.refs_0_ = bf16[32,48,128]{2,1,0:T(8,128)(2,1)S(1)} all-to-all(bf16[32,48,128]{2,1,0:T(8,128)(2,1)S(1)} %get-tuple-element.29), channel_id=1, replica_groups={{0,4,8,12,16,20,24,28,1,5,9,13,17,21,25,29,2,6,10,14,18,22,26,30,3,7,11..., dimensions={0} | all-to-all | bytes 786432 | tf_op jit(solution)/shard_map/all_to_all | solution.py:392
  53.8 19.6 %all_to_all.85.refs_1_ = bf16[32,48,128]{2,1,0:T(8,128)(2,1)S(1)} all-to-all(bf16[32,48,128]{2,1,0:T(8,128)(2,1)S(1)} %get-tuple-element.30), channel_id=1, replica_groups={{0,4,8,12,16,20,24,28,1,5,9,13,17,21,25,29,2,6,10,14,18,22,26,30,3,7,11..., dimensions={0} | all-to-all | bytes 786432 | tf_op jit(solution)/shard_map/all_to_all | solution.py:392
  73.5 2.3 backward_start.1
  75.8 15.2 %all_to_all.86.refs_0_ = bf16[16,80,128]{2,1,0:T(8,128)(2,1)S(1)} all-to-all(bf16[16,80,128]{2,1,0:T(8,128)(2,1)S(1)} %get-tuple-element.32), channel_id=1, replica_groups=mesh['group'=16,'loop'=32] {'group'}, dimensions={0} | all-to-all | bytes 655360 | tf_op jit(solution)/shard_map/all_to_all | solution.py:392
  91.7 4.6 %all-to-all-start.4 = ((bf16[16,64,128]{2,1,0:T(8,128)(2,1)}), bf16[16,64,128]{2,1,0:T(8,128)(2,1)S(1)}, u32[]{:S(2)}, u32[]{:S(2)}) async-start(bf16[16,64,128]{2,1,0:T(8,128)(2,1)} %get-tuple-element.34), calls=%async_computation.4 | async-start | bytes 524288 | tf_op jit(solution)/shard_map/all_to_all | solution.py:392
  98.2 2.2 factor.4.refs_4_
  100.4 3.2 %all-to-all-done.4.refs_1_ = bf16[16,64,128]{2,1,0:T(8,128)(2,1)S(1)} async-done(((bf16[16,64,128]{2,1,0:T(8,128)(2,1)}), bf16[16,64,128]{2,1,0:T(8,128)(2,1)S(1)}, u32[]{:S(2)}, u32[]{:S(2)}) %all-to-all-start.4) | async-done | bytes 262176 | tf_op jit(solution)/shard_map/all_to_all | solution.py:392
  103.6 2.1 forward.2
  105.7 17.7 %all_to_all.87.refs_0_ = bf16[32,48,128]{2,1,0:T(8,128)(2,1)S(1)} all-to-all(bf16[32,48,128]{2,1,0:T(8,128)(2,1)S(1)} %forward.2), channel_id=1, replica_groups={{0,4,8,12,16,20,24,28,1,5,9,13,17,21,25,29,2,6,10,14,18,22,26,30,3,7,11..., dimensions={0} | all-to-all | bytes 786432 | tf_op jit(solution)/shard_map/all_to_all | solution.py:392
  124.1 7.6 %all-to-all-start.6 = ((bf16[32,32,128]{2,1,0:T(8,128)(2,1)}), bf16[32,32,128]{2,1,0:T(8,128)(2,1)S(1)}, u32[]{:S(2)}, u32[]{:S(2)}) async-start(bf16[32,32,128]{2,1,0:T(8,128)(2,1)} %get-tuple-element.38), calls=%async_computation.6 | async-start | bytes 524288 | tf_op jit(solution)/shard_map/all_to_all | solution.py:392
  131.7 2.9 %all_gather.20.gram = f32[32,128]{1,0:T(8,128)S(1)} all-gather(f32[16,128]{1,0:T(8,128)S(1)} %copy-done.7), channel_id=1, replica_groups={{0,32},{64,96},{128,160},{192,224},{256,288},{320,352},{384,416},{448,4..., dimensions={0}, use_global_device_ids=true | all-gather | bytes 24576 | tf_op jit(solution)/shard_map/all_gather | solution.py:459
  134.6 2.2 factor.5.refs_4_
  136.9 7.2 %all-to-all-done.6.refs_1_ = bf16[32,32,128]{2,1,0:T(8,128)(2,1)S(1)} async-done(((bf16[32,32,128]{2,1,0:T(8,128)(2,1)}), bf16[32,32,128]{2,1,0:T(8,128)(2,1)S(1)}, u32[]{:S(2)}, u32[]{:S(2)}) %all-to-all-start.6) | async-done | bytes 262176 | tf_op jit(solution)/shard_map/all_to_all | solution.py:392
  144.0 2.1 backward.2
  146.2 14.7 %all_to_all.88.refs_0_ = bf16[16,80,128]{2,1,0:T(8,128)(2,1)S(1)} all-to-all(bf16[16,80,128]{2,1,0:T(8,128)(2,1)S(1)} %backward.2), channel_id=1, replica_groups=mesh['group'=16,'loop'=32] {'group'}, dimensions={0} | all-to-all | bytes 655360 | tf_op jit(solution)/shard_map/all_to_all | solution.py:392
  161.6 4.8 %all-to-all-start.8 = ((bf16[16,64,128]{2,1,0:T(8,128)(2,1)}), bf16[16,64,128]{2,1,0:T(8,128)(2,1)S(1)}, u32[]{:S(2)}, u32[]{:S(2)}) async-start(bf16[16,64,128]{2,1,0:T(8,128)(2,1)} %get-tuple-element.41), calls=%async_computation.8 | async-start | bytes 524288 | tf_op jit(solution)/shard_map/all_to_all | solution.py:392
  168.3 2.2 factor.6.refs_4_
  170.5 3.2 %all-to-all-done.8.refs_1_ = bf16[16,64,128]{2,1,0:T(8,128)(2,1)S(1)} async-done(((bf16[16,64,128]{2,1,0:T(8,128)(2,1)}), bf16[16,64,128]{2,1,0:T(8,128)(2,1)S(1)}, u32[]{:S(2)}, u32[]{:S(2)}) %all-to-all-start.8) | async-done | bytes 262176 | tf_op jit(solution)/shard_map/all_to_all | solution.py:392
  175.8 17.0 %all_to_all.89.refs_0_ = bf16[32,48,128]{2,1,0:T(8,128)(2,1)S(1)} all-to-all(bf16[32,48,128]{2,1,0:T(8,128)(2,1)S(1)} %forward.3), channel_id=1, replica_groups={{0,4,8,12,16,20,24,28,1,5,9,13,17,21,25,29,2,6,10,14,18,22,26,30,3,7,11..., dimensions={0} | all-to-all | bytes 786432 | tf_op jit(solution)/shard_map/all_to_all | solution.py:392
  193.5 7.6 %all-to-all-start.10 = ((bf16[32,32,128]{2,1,0:T(8,128)(2,1)}), bf16[32,32,128]{2,1,0:T(8,128)(2,1)S(1)}, u32[]{:S(2)}, u32[]{:S(2)}) async-start(bf16[32,32,128]{2,1,0:T(8,128)(2,1)} %get-tuple-element.43), calls=%async_computation.10 | async-start | bytes 524288 | tf_op jit(solution)/shard_map/all_to_all | solution.py:392
  201.1 2.9 %all_gather.22.gram = f32[32,128]{1,0:T(8,128)S(1)} all-gather(f32[16,128]{1,0:T(8,128)S(1)} %copy-done.4), channel_id=1, replica_groups={{0,32},{64,96},{128,160},{192,224},{256,288},{320,352},{384,416},{448,4..., dimensions={0}, use_global_device_ids=true | all-gather | bytes 24576 | tf_op jit(solution)/shard_map/all_gather | solution.py:459
  204.0 2.2 factor.7.refs_4_.attendee_parts
  206.3 7.1 %all-to-all-done.10.refs_1_ = bf16[32,32,128]{2,1,0:T(8,128)(2,1)S(1)} async-done(((bf16[32,32,128]{2,1,0:T(8,128)(2,1)}), bf16[32,32,128]{2,1,0:T(8,128)(2,1)S(1)}, u32[]{:S(2)}, u32[]{:S(2)}) %all-to-all-start.10) | async-done | bytes 262176 | tf_op jit(solution)/shard_map/all_to_all | solution.py:392
  215.5 14.7 %all_to_all.90.refs_0_ = bf16[16,80,128]{2,1,0:T(8,128)(2,1)S(1)} all-to-all(bf16[16,80,128]{2,1,0:T(8,128)(2,1)S(1)} %backward.3), channel_id=1, replica_groups=mesh['group'=16,'loop'=32] {'group'}, dimensions={0} | all-to-all | bytes 655360 | tf_op jit(solution)/shard_map/all_to_all | solution.py:392
  231.4 4.6 %all-to-all-start.12 = ((f32[16,32,128]{2,1,0:T(8,128)}), f32[16,32,128]{2,1,0:T(8,128)S(1)}, u32[]{:S(2)}, u32[]{:S(2)}) async-start(f32[16,32,128]{2,1,0:T(8,128)} %get-tuple-element.45), calls=%async_computation.12 | async-start | bytes 524288 | tf_op jit(solution)/shard_map/all_to_all | solution.py:392
  237.8 3.4 %factor_last.1 = (f32[64,64]{1,0:T(8,128)S(1)}, f32[64,128]{1,0:T(8,128)S(1)}, f32[64,64]{1,0:T(8,128)}) custom-call(f32[32,128]{1,0:T(8,128)S(1)} %all_gather.23.gram, f32[64,128]{1,0:T(8,128)S(1)} %get-tuple-element.47.session, f32[32,128]{1,0:T(8,128)S(1)} %get-tuple-element.48.attendee, bf16[384,128]{1,0:T(8,128)(2,1)S(1)} %factor.7.refs_4_.attendee_parts), custom_call_target="tpu_custom_call" | custom-call | flops 100000000 | bytes 1048576 | tf_op jit(solution)/shard_map/factor_last/pallas_call | solution.py:522
  243.8 15.8 %all_to_all.91.received = bf16[32,32,128]{2,1,0:T(8,128)(2,1)S(1)} all-to-all(bf16[32,32,128]{2,1,0:T(8,128)(2,1)S(1)} %gram_last.1), channel_id=1, replica_groups={{0,4,8,12,16,20,24,28,1,5,9,13,17,21,25,29,2,6,10,14,18,22,26,30,3,7,11..., dimensions={0} | all-to-all | bytes 524288 | tf_op jit(solution)/shard_map/all_to_all | solution.py:392
  259.6 3.2 %session_out.1 = f32[64,128]{1,0:T(8,128)} custom-call(bf16[32,32,128]{2,1,0:T(8,128)(2,1)S(1)} %all_to_all.91.received, f32[64,128]{1,0:T(8,128)S(1)} %get-tuple-element.50.panel), custom_call_target="tpu_custom_call" | custom-call | flops 100000000 | bytes 1048576 | tf_op jit(solution)/shard_map/session_out/pallas_call | solution.py:534
  (42 shorter events, 20.4 us)
Async XLA Ops:
  1.4 0.7 copy-start.9
  1.4 0.7 copy-start.10
  2.0 9.0 %copy-start = (bf16[1,1,32,128,128]{4,3,2,1,0:T(8,128)(2,1)S(1)}, bf16[1,1,32,128,128]{4,3,2,1,0:T(8,128)(2,1)}, u32[]{:S(2)}) copy-start(bf16[1,1,32,128,128]{4,3,2,1,0:T(8,128)(2,1)} %param.5) | copy-start | bytes 3145732
  4.4 13.2 %all-to-all-start = ((f32[8,80,128]{2,1,0:T(8,128)}), f32[8,80,128]{2,1,0:T(8,128)}, u32[]{:S(2)}, u32[]{:S(2)}) async-start(f32[8,80,128]{2,1,0:T(8,128)} %start_message.1), calls=%async_computation | async-start | bytes 655360 | tf_op jit(solution)/shard_map/all_to_all | solution.py:392
  26.8 64.2 %copy-start.1 = (f32[64,128]{1,0:T(8,128)}, f32[64,128]{1,0:T(8,128)S(1)}, u32[]{:S(2)}) copy-start(f32[64,128]{1,0:T(8,128)S(1)} %get-tuple-element.33.refs_1_) | copy-start | bytes 98308
  91.7 4.6 %copy-start.6 = (f32[16,128]{1,0:T(8,128)S(1)}, f32[16,128]{1,0:T(8,128)}, u32[]{:S(2)}) copy-start(f32[16,128]{1,0:T(8,128)} %get-tuple-element.36) | copy-start | bytes 24580
  91.7 11.8 %all-to-all-start.4 = ((bf16[16,64,128]{2,1,0:T(8,128)(2,1)}), bf16[16,64,128]{2,1,0:T(8,128)(2,1)S(1)}, u32[]{:S(2)}, u32[]{:S(2)}) async-start(bf16[16,64,128]{2,1,0:T(8,128)(2,1)} %get-tuple-element.34), calls=%async_computation.4 | async-start | bytes 524288 | tf_op jit(solution)/shard_map/all_to_all | solution.py:392
  124.1 7.6 %copy-start.7 = (f32[16,128]{1,0:T(8,128)S(1)}, f32[16,128]{1,0:T(8,128)}, u32[]{:S(2)}) copy-start(f32[16,128]{1,0:T(8,128)} %get-tuple-element.40) | copy-start | bytes 24580
  124.1 19.9 %all-to-all-start.6 = ((bf16[32,32,128]{2,1,0:T(8,128)(2,1)}), bf16[32,32,128]{2,1,0:T(8,128)(2,1)S(1)}, u32[]{:S(2)}, u32[]{:S(2)}) async-start(bf16[32,32,128]{2,1,0:T(8,128)(2,1)} %get-tuple-element.38), calls=%async_computation.6 | async-start | bytes 524288 | tf_op jit(solution)/shard_map/all_to_all | solution.py:392
  146.1 14.7 %copy-start.2 = (f32[64,128]{1,0:T(8,128)S(1)}, f32[64,128]{1,0:T(8,128)}, u32[]{:S(2)}) copy-start(f32[64,128]{1,0:T(8,128)} %copy-done.1) | copy-start | bytes 98308
  161.6 4.8 %copy-start.8 = (f32[16,128]{1,0:T(8,128)S(1)}, f32[16,128]{1,0:T(8,128)}, u32[]{:S(2)}) copy-start(f32[16,128]{1,0:T(8,128)} %get-tuple-element.42) | copy-start | bytes 24580
  161.6 12.0 %all-to-all-start.8 = ((bf16[16,64,128]{2,1,0:T(8,128)(2,1)}), bf16[16,64,128]{2,1,0:T(8,128)(2,1)S(1)}, u32[]{:S(2)}, u32[]{:S(2)}) async-start(bf16[16,64,128]{2,1,0:T(8,128)(2,1)} %get-tuple-element.41), calls=%async_computation.8 | async-start | bytes 524288 | tf_op jit(solution)/shard_map/all_to_all | solution.py:392
  193.5 7.6 %copy-start.4 = (f32[16,128]{1,0:T(8,128)S(1)}, f32[16,128]{1,0:T(8,128)}, u32[]{:S(2)}) copy-start(f32[16,128]{1,0:T(8,128)} %get-tuple-element.44) | copy-start | bytes 24580
  193.5 19.9 %all-to-all-start.10 = ((bf16[32,32,128]{2,1,0:T(8,128)(2,1)}), bf16[32,32,128]{2,1,0:T(8,128)(2,1)S(1)}, u32[]{:S(2)}, u32[]{:S(2)}) async-start(bf16[32,32,128]{2,1,0:T(8,128)(2,1)} %get-tuple-element.43), calls=%async_computation.10 | async-start | bytes 524288 | tf_op jit(solution)/shard_map/all_to_all | solution.py:392
  215.5 14.8 %copy-start.3 = (f32[64,128]{1,0:T(8,128)S(1)}, f32[64,128]{1,0:T(8,128)}, u32[]{:S(2)}) copy-start(f32[64,128]{1,0:T(8,128)} %copy-done.1) | copy-start | bytes 98308
  231.4 4.6 %copy-start.5 = (f32[16,128]{1,0:T(8,128)S(1)}, f32[16,128]{1,0:T(8,128)}, u32[]{:S(2)}) copy-start(f32[16,128]{1,0:T(8,128)} %get-tuple-element.46) | copy-start | bytes 24580
  231.4 11.8 %all-to-all-start.12 = ((f32[16,32,128]{2,1,0:T(8,128)}), f32[16,32,128]{2,1,0:T(8,128)S(1)}, u32[]{:S(2)}, u32[]{:S(2)}) async-start(f32[16,32,128]{2,1,0:T(8,128)} %get-tuple-element.45), calls=%async_computation.12 | async-start | bytes 524288 | tf_op jit(solution)/shard_map/all_to_all | solution.py:392

commit v6 on v5

--- a/solution.py
+++ b/solution.py
@@ -317,7 +317,7 @@
         square = lax.dot_general(
             panel, panel, (((0,), (0,)), ((), ())), precision=HIGHEST, preferred_element_type=F32
         )
-        message = rows_to_halves(diagonal_blocks(square))
+        message = gram_to_message(diagonal_blocks(square), True)
     else:
         message = (panel * scale).astype(BF16)
     for d in range(n_copies):
@@ -346,10 +346,10 @@
 
 
 def gram_last_kernel(n_from, n_copies, received, factor, copies):
-    summed = received[0]
+    summed = received[0].astype(F32)
     for s in range(1, n_from):
-        summed = summed + received[s]
-    gram = apply_to_gram(halves_to_rows(summed), factor[...])
+        summed = summed + received[s].astype(F32)
+    gram = apply_to_gram(message_to_gram(summed), factor[...])
     message = gram_to_message(gram, True)
     for d in range(n_copies):
         copies[d] = message
@@ -508,7 +508,7 @@
             args = (*args, row_weight, row_parts)
             (outgoing,) = products("plain", (0, 3), last, *to, "backward", 16, args)
         received = exchange(outgoing, "group")
-        message = ((n_group, WIDTH // 2, LANES), F32) if last else ((n_group, col_half, LANES), BF16)
+        message = ((n_group, WIDTH // 2, LANES), BF16) if last else ((n_group, col_half, LANES), BF16)
         copies, session, gram = call(
             functools.partial(sum_kernel, "last" if last else "plain", n_group, col_half, n_group),
             "session",

time: 266 us -> 265 us (level)
  no operation moved by 1% of the time
where the time goes in v6:
time: 265 us; the launch traced here: 262 us
  blocking collectives  160 us (60%)
  Pallas kernels  36.6 us (14%)
  starting transfers between devices  35.8 us (14%)
  waiting for transfers between devices  27.3 us (10%)
    all_to_all x8, blocking collectives, exchange(): lax.all_to_all(array.reshape(n * rows, lanes), axis, split_axis=0, concat...  141 us
    all_to_all x6, starting transfers between devices, exchange(): lax.all_to_all(array.reshape(n * rows, lanes), axis, split_axis=0, concat...  35.8 us
    all_to_all x6, waiting for transfers between devices, exchange(): lax.all_to_all(array.reshape(n * rows, lanes), axis, split_axis=0, concat...  27.3 us
    pallas_call x6, Pallas kernels, products(): call(functools.partial(product_kernel, kind, *way, rows_from, n_to, rows_...  12.3 us
    all_gather x5, blocking collectives, swap_cores(): lax.all_gather(half_message, 'group', axis_index_groups=pairs, axis=0, ti...  11.3 us
    pallas_call x4, Pallas kernels, factor_of(): call(factor_kernel, 'factor', [VMEM], [((3 * LANES, LANES), BF16)])(gram)[0]  8.98 us
    all_gather x1, blocking collectives, per_device(): lax.all_gather(gathered, 'group', axis_index_groups=pairs, axis=0, tiled=...  7.47 us
  transfers between devices with their start and end apart: 6, of which 6 were waited for; matrix products, arithmetic and copies ran while one was open for 0% of the time, Pallas kernels for 5%

profile of v6, /device:TPU:1, one launch (start us, length us, event | category | flops | bytes accessed | tf_op | source)
XLA Modules:
  0.0 261.9 jit_solution(5128637176404430048)
XLA Ops:
  2.1 2.3 start_message.1
  4.4 6.7 %all-to-all-start = ((f32[8,80,128]{2,1,0:T(8,128)}), f32[8,80,128]{2,1,0:T(8,128)}, u32[]{:S(2)}, u32[]{:S(2)}) async-start(f32[8,80,128]{2,1,0:T(8,128)} %start_message.1), calls=%async_computation | async-start | bytes 655360 | tf_op jit(solution)/shard_map/all_to_all | solution.py:392
  11.9 5.8 %all-to-all-done = f32[8,80,128]{2,1,0:T(8,128)} async-done(((f32[8,80,128]{2,1,0:T(8,128)}), f32[8,80,128]{2,1,0:T(8,128)}, u32[]{:S(2)}, u32[]{:S(2)}) %all-to-all-start) | async-done | bytes 327712 | tf_op jit(solution)/shard_map/all_to_all | solution.py:392
  17.7 7.5 %all_gather.18.refs_1_ = f32[16,80,128]{2,1,0:T(8,128)S(1)} all-gather(f32[8,80,128]{2,1,0:T(8,128)} %all-to-all-done), channel_id=1, replica_groups={{0,32},{64,96},{128,160},{192,224},{256,288},{320,352},{384,416},{448,4..., dimensions={0}, use_global_device_ids=true | all-gather | bytes 983040 | tf_op jit(solution)/shard_map/all_gather | solution.py:426
  26.8 26.2 %all_to_all.84.refs_0_ = bf16[32,48,128]{2,1,0:T(8,128)(2,1)S(1)} all-to-all(bf16[32,48,128]{2,1,0:T(8,128)(2,1)S(1)} %get-tuple-element.29), channel_id=1, replica_groups={{0,4,8,12,16,20,24,28,1,5,9,13,17,21,25,29,2,6,10,14,18,22,26,30,3,7,11..., dimensions={0} | all-to-all | bytes 786432 | tf_op jit(solution)/shard_map/all_to_all | solution.py:392
  53.8 19.7 %all_to_all.85.refs_1_ = bf16[32,48,128]{2,1,0:T(8,128)(2,1)S(1)} all-to-all(bf16[32,48,128]{2,1,0:T(8,128)(2,1)S(1)} %get-tuple-element.30), channel_id=1, replica_groups={{0,4,8,12,16,20,24,28,1,5,9,13,17,21,25,29,2,6,10,14,18,22,26,30,3,7,11..., dimensions={0} | all-to-all | bytes 786432 | tf_op jit(solution)/shard_map/all_to_all | solution.py:392
  73.5 2.3 backward_start.1
  75.8 15.2 %all_to_all.86.refs_0_ = bf16[16,80,128]{2,1,0:T(8,128)(2,1)S(1)} all-to-all(bf16[16,80,128]{2,1,0:T(8,128)(2,1)S(1)} %get-tuple-element.32), channel_id=1, replica_groups=mesh['group'=16,'loop'=32] {'group'}, dimensions={0} | all-to-all | bytes 655360 | tf_op jit(solution)/shard_map/all_to_all | solution.py:392
  91.7 4.6 %all-to-all-start.4 = ((bf16[16,64,128]{2,1,0:T(8,128)(2,1)}), bf16[16,64,128]{2,1,0:T(8,128)(2,1)S(1)}, u32[]{:S(2)}, u32[]{:S(2)}) async-start(bf16[16,64,128]{2,1,0:T(8,128)(2,1)} %get-tuple-element.34), calls=%async_computation.4 | async-start | bytes 524288 | tf_op jit(solution)/shard_map/all_to_all | solution.py:392
  98.2 2.2 factor.4.refs_4_
  100.4 3.2 %all-to-all-done.4.refs_1_ = bf16[16,64,128]{2,1,0:T(8,128)(2,1)S(1)} async-done(((bf16[16,64,128]{2,1,0:T(8,128)(2,1)}), bf16[16,64,128]{2,1,0:T(8,128)(2,1)S(1)}, u32[]{:S(2)}, u32[]{:S(2)}) %all-to-all-start.4) | async-done | bytes 262176 | tf_op jit(solution)/shard_map/all_to_all | solution.py:392
  105.7 17.7 %all_to_all.87.refs_0_ = bf16[32,48,128]{2,1,0:T(8,128)(2,1)S(1)} all-to-all(bf16[32,48,128]{2,1,0:T(8,128)(2,1)S(1)} %forward.2), channel_id=1, replica_groups={{0,4,8,12,16,20,24,28,1,5,9,13,17,21,25,29,2,6,10,14,18,22,26,30,3,7,11..., dimensions={0} | all-to-all | bytes 786432 | tf_op jit(solution)/shard_map/all_to_all | solution.py:392
  124.2 7.6 %all-to-all-start.6 = ((bf16[32,32,128]{2,1,0:T(8,128)(2,1)}), bf16[32,32,128]{2,1,0:T(8,128)(2,1)S(1)}, u32[]{:S(2)}, u32[]{:S(2)}) async-start(bf16[32,32,128]{2,1,0:T(8,128)(2,1)} %get-tuple-element.38), calls=%async_computation.6 | async-start | bytes 524288 | tf_op jit(solution)/shard_map/all_to_all | solution.py:392
  131.8 2.9 %all_gather.20.gram = f32[32,128]{1,0:T(8,128)S(1)} all-gather(f32[16,128]{1,0:T(8,128)S(1)} %copy-done.7), channel_id=1, replica_groups={{0,32},{64,96},{128,160},{192,224},{256,288},{320,352},{384,416},{448,4..., dimensions={0}, use_global_device_ids=true | all-gather | bytes 24576 | tf_op jit(solution)/shard_map/all_gather | solution.py:459
  134.7 2.2 factor.5.refs_4_
  136.9 7.1 %all-to-all-done.6.refs_1_ = bf16[32,32,128]{2,1,0:T(8,128)(2,1)S(1)} async-done(((bf16[32,32,128]{2,1,0:T(8,128)(2,1)}), bf16[32,32,128]{2,1,0:T(8,128)(2,1)S(1)}, u32[]{:S(2)}, u32[]{:S(2)}) %all-to-all-start.6) | async-done | bytes 262176 | tf_op jit(solution)/shard_map/all_to_all | solution.py:392
  144.1 2.1 backward.2
  146.2 14.8 %all_to_all.88.refs_0_ = bf16[16,80,128]{2,1,0:T(8,128)(2,1)S(1)} all-to-all(bf16[16,80,128]{2,1,0:T(8,128)(2,1)S(1)} %backward.2), channel_id=1, replica_groups=mesh['group'=16,'loop'=32] {'group'}, dimensions={0} | all-to-all | bytes 655360 | tf_op jit(solution)/shard_map/all_to_all | solution.py:392
  161.7 4.8 %all-to-all-start.8 = ((bf16[16,64,128]{2,1,0:T(8,128)(2,1)}), bf16[16,64,128]{2,1,0:T(8,128)(2,1)S(1)}, u32[]{:S(2)}, u32[]{:S(2)}) async-start(bf16[16,64,128]{2,1,0:T(8,128)(2,1)} %get-tuple-element.41), calls=%async_computation.8 | async-start | bytes 524288 | tf_op jit(solution)/shard_map/all_to_all | solution.py:392
  168.3 2.2 factor.6.refs_4_
  170.6 3.2 %all-to-all-done.8.refs_1_ = bf16[16,64,128]{2,1,0:T(8,128)(2,1)S(1)} async-done(((bf16[16,64,128]{2,1,0:T(8,128)(2,1)}), bf16[16,64,128]{2,1,0:T(8,128)(2,1)S(1)}, u32[]{:S(2)}, u32[]{:S(2)}) %all-to-all-start.8) | async-done | bytes 262176 | tf_op jit(solution)/shard_map/all_to_all | solution.py:392
  173.7 2.1 forward.3
  175.8 17.0 %all_to_all.89.refs_0_ = bf16[32,48,128]{2,1,0:T(8,128)(2,1)S(1)} all-to-all(bf16[32,48,128]{2,1,0:T(8,128)(2,1)S(1)} %forward.3), channel_id=1, replica_groups={{0,4,8,12,16,20,24,28,1,5,9,13,17,21,25,29,2,6,10,14,18,22,26,30,3,7,11..., dimensions={0} | all-to-all | bytes 786432 | tf_op jit(solution)/shard_map/all_to_all | solution.py:392
  193.6 7.6 %all-to-all-start.10 = ((bf16[32,32,128]{2,1,0:T(8,128)(2,1)}), bf16[32,32,128]{2,1,0:T(8,128)(2,1)S(1)}, u32[]{:S(2)}, u32[]{:S(2)}) async-start(bf16[32,32,128]{2,1,0:T(8,128)(2,1)} %get-tuple-element.43), calls=%async_computation.10 | async-start | bytes 524288 | tf_op jit(solution)/shard_map/all_to_all | solution.py:392
  201.2 2.9 %all_gather.22.gram = f32[32,128]{1,0:T(8,128)S(1)} all-gather(f32[16,128]{1,0:T(8,128)S(1)} %copy-done.4), channel_id=1, replica_groups={{0,32},{64,96},{128,160},{192,224},{256,288},{320,352},{384,416},{448,4..., dimensions={0}, use_global_device_ids=true | all-gather | bytes 24576 | tf_op jit(solution)/shard_map/all_gather | solution.py:459
  204.1 2.2 factor.7.refs_4_.attendee_parts
  206.3 7.1 %all-to-all-done.10.refs_1_ = bf16[32,32,128]{2,1,0:T(8,128)(2,1)S(1)} async-done(((bf16[32,32,128]{2,1,0:T(8,128)(2,1)}), bf16[32,32,128]{2,1,0:T(8,128)(2,1)S(1)}, u32[]{:S(2)}, u32[]{:S(2)}) %all-to-all-start.10) | async-done | bytes 262176 | tf_op jit(solution)/shard_map/all_to_all | solution.py:392
  215.6 14.7 %all_to_all.90.refs_0_ = bf16[16,80,128]{2,1,0:T(8,128)(2,1)S(1)} all-to-all(bf16[16,80,128]{2,1,0:T(8,128)(2,1)S(1)} %backward.3), channel_id=1, replica_groups=mesh['group'=16,'loop'=32] {'group'}, dimensions={0} | all-to-all | bytes 655360 | tf_op jit(solution)/shard_map/all_to_all | solution.py:392
  231.5 4.6 %all-to-all-start.12 = ((bf16[16,32,128]{2,1,0:T(8,128)(2,1)}), bf16[16,32,128]{2,1,0:T(8,128)(2,1)S(1)}, u32[]{:S(2)}, u32[]{:S(2)}) async-start(bf16[16,32,128]{2,1,0:T(8,128)(2,1)} %get-tuple-element.45), calls=%async_computation.12 | async-start | bytes 262144 | tf_op jit(solution)/shard_map/all_to_all | solution.py:392
  237.9 3.4 %factor_last.1 = (f32[64,64]{1,0:T(8,128)S(1)}, f32[64,128]{1,0:T(8,128)S(1)}, f32[64,64]{1,0:T(8,128)}) custom-call(f32[32,128]{1,0:T(8,128)S(1)} %all_gather.23.gram, f32[64,128]{1,0:T(8,128)S(1)} %get-tuple-element.47.session, f32[32,128]{1,0:T(8,128)S(1)} %get-tuple-element.48.attendee, bf16[384,128]{1,0:T(8,128)(2,1)S(1)} %factor.7.refs_4_.attendee_parts), custom_call_target="tpu_custom_call" | custom-call | flops 100000000 | bytes 1048576 | tf_op jit(solution)/shard_map/factor_last/pallas_call | solution.py:522
  243.0 15.8 %all_to_all.91.received = bf16[32,32,128]{2,1,0:T(8,128)(2,1)S(1)} all-to-all(bf16[32,32,128]{2,1,0:T(8,128)(2,1)S(1)} %gram_last.1), channel_id=1, replica_groups={{0,4,8,12,16,20,24,28,1,5,9,13,17,21,25,29,2,6,10,14,18,22,26,30,3,7,11..., dimensions={0} | all-to-all | bytes 524288 | tf_op jit(solution)/shard_map/all_to_all | solution.py:392
  258.7 3.2 %session_out.1 = f32[64,128]{1,0:T(8,128)} custom-call(bf16[32,32,128]{2,1,0:T(8,128)(2,1)S(1)} %all_to_all.91.received, f32[64,128]{1,0:T(8,128)S(1)} %get-tuple-element.50.panel), custom_call_target="tpu_custom_call" | custom-call | flops 100000000 | bytes 1048576 | tf_op jit(solution)/shard_map/session_out/pallas_call | solution.py:534
  (42 shorter events, 19.5 us)
Async XLA Ops:
  1.4 0.7 copy-start.9
  1.4 0.7 copy-start.10
  2.0 9.0 %copy-start = (bf16[1,1,32,128,128]{4,3,2,1,0:T(8,128)(2,1)S(1)}, bf16[1,1,32,128,128]{4,3,2,1,0:T(8,128)(2,1)}, u32[]{:S(2)}) copy-start(bf16[1,1,32,128,128]{4,3,2,1,0:T(8,128)(2,1)} %param.5) | copy-start | bytes 3145732
  4.4 13.2 %all-to-all-start = ((f32[8,80,128]{2,1,0:T(8,128)}), f32[8,80,128]{2,1,0:T(8,128)}, u32[]{:S(2)}, u32[]{:S(2)}) async-start(f32[8,80,128]{2,1,0:T(8,128)} %start_message.1), calls=%async_computation | async-start | bytes 655360 | tf_op jit(solution)/shard_map/all_to_all | solution.py:392
  26.8 64.2 %copy-start.1 = (f32[64,128]{1,0:T(8,128)}, f32[64,128]{1,0:T(8,128)S(1)}, u32[]{:S(2)}) copy-start(f32[64,128]{1,0:T(8,128)S(1)} %get-tuple-element.33.refs_1_) | copy-start | bytes 98308
  91.7 4.6 %copy-start.6 = (f32[16,128]{1,0:T(8,128)S(1)}, f32[16,128]{1,0:T(8,128)}, u32[]{:S(2)}) copy-start(f32[16,128]{1,0:T(8,128)} %get-tuple-element.36) | copy-start | bytes 24580
  91.7 11.8 %all-to-all-start.4 = ((bf16[16,64,128]{2,1,0:T(8,128)(2,1)}), bf16[16,64,128]{2,1,0:T(8,128)(2,1)S(1)}, u32[]{:S(2)}, u32[]{:S(2)}) async-start(bf16[16,64,128]{2,1,0:T(8,128)(2,1)} %get-tuple-element.34), calls=%async_computation.4 | async-start | bytes 524288 | tf_op jit(solution)/shard_map/all_to_all | solution.py:392
  124.2 7.6 %copy-start.7 = (f32[16,128]{1,0:T(8,128)S(1)}, f32[16,128]{1,0:T(8,128)}, u32[]{:S(2)}) copy-start(f32[16,128]{1,0:T(8,128)} %get-tuple-element.40) | copy-start | bytes 24580
  124.2 19.9 %all-to-all-start.6 = ((bf16[32,32,128]{2,1,0:T(8,128)(2,1)}), bf16[32,32,128]{2,1,0:T(8,128)(2,1)S(1)}, u32[]{:S(2)}, u32[]{:S(2)}) async-start(bf16[32,32,128]{2,1,0:T(8,128)(2,1)} %get-tuple-element.38), calls=%async_computation.6 | async-start | bytes 524288 | tf_op jit(solution)/shard_map/all_to_all | solution.py:392
  146.2 14.8 %copy-start.2 = (f32[64,128]{1,0:T(8,128)S(1)}, f32[64,128]{1,0:T(8,128)}, u32[]{:S(2)}) copy-start(f32[64,128]{1,0:T(8,128)} %copy-done.1) | copy-start | bytes 98308
  161.7 4.8 %copy-start.8 = (f32[16,128]{1,0:T(8,128)S(1)}, f32[16,128]{1,0:T(8,128)}, u32[]{:S(2)}) copy-start(f32[16,128]{1,0:T(8,128)} %get-tuple-element.42) | copy-start | bytes 24580
  161.7 12.0 %all-to-all-start.8 = ((bf16[16,64,128]{2,1,0:T(8,128)(2,1)}), bf16[16,64,128]{2,1,0:T(8,128)(2,1)S(1)}, u32[]{:S(2)}, u32[]{:S(2)}) async-start(bf16[16,64,128]{2,1,0:T(8,128)(2,1)} %get-tuple-element.41), calls=%async_computation.8 | async-start | bytes 524288 | tf_op jit(solution)/shard_map/all_to_all | solution.py:392
  193.6 7.6 %copy-start.4 = (f32[16,128]{1,0:T(8,128)S(1)}, f32[16,128]{1,0:T(8,128)}, u32[]{:S(2)}) copy-start(f32[16,128]{1,0:T(8,128)} %get-tuple-element.44) | copy-start | bytes 24580
  193.6 19.9 %all-to-all-start.10 = ((bf16[32,32,128]{2,1,0:T(8,128)(2,1)}), bf16[32,32,128]{2,1,0:T(8,128)(2,1)S(1)}, u32[]{:S(2)}, u32[]{:S(2)}) async-start(bf16[32,32,128]{2,1,0:T(8,128)(2,1)} %get-tuple-element.43), calls=%async_computation.10 | async-start | bytes 524288 | tf_op jit(solution)/shard_map/all_to_all | solution.py:392
  215.5 14.8 %copy-start.3 = (f32[64,128]{1,0:T(8,128)S(1)}, f32[64,128]{1,0:T(8,128)}, u32[]{:S(2)}) copy-start(f32[64,128]{1,0:T(8,128)} %copy-done.1) | copy-start | bytes 98308
  231.5 4.6 %copy-start.5 = (f32[16,128]{1,0:T(8,128)S(1)}, f32[16,128]{1,0:T(8,128)}, u32[]{:S(2)}) copy-start(f32[16,128]{1,0:T(8,128)} %get-tuple-element.46) | copy-start | bytes 24580
  231.5 10.8 %all-to-all-start.12 = ((bf16[16,32,128]{2,1,0:T(8,128)(2,1)}), bf16[16,32,128]{2,1,0:T(8,128)(2,1)S(1)}, u32[]{:S(2)}, u32[]{:S(2)}) async-start(bf16[16,32,128]{2,1,0:T(8,128)(2,1)} %get-tuple-element.45), calls=%async_computation.12 | async-start | bytes 262144 | tf_op jit(solution)/shard_map/all_to_all | solution.py:392
